TPU v7x, 32 devices: a whole 2x2x4 slice. The times are simulated.
32 devices in a mesh: band: 2 (over x), lev: 16 (over z, y, core).
Axes of the slice: x: 2, y: 2, z: 4, core: 2. Of those that a mesh axis runs over, the one named last changes fastest.
Arguments:
- tracer: float32 [64, 16, 16, 512], P(None, 'lev', 'band'), parts along dimension 2, may hold values from -6 to 6
- east_flow: float32 [16, 16, 512], P('lev', 'band'), parts along dimension 1, may hold values from -0.3 to 0.3
- north_flow: float32 [16, 16, 512], P('lev', 'band'), parts along dimension 1, may hold values from -0.3 to 0.3
- up_flow: float32 [16, 16, 512], P('lev', 'band'), parts along dimension 1, may hold values from -0.3 to 0.3
- diffusivity: float32 [16, 16, 512], P('lev', 'band'), parts along dimension 1, may hold values from 30 to 300
- thickness: float32 [16], replicated, may hold values from 1.5 to 4
- kmt: int32 [16, 512], P('band'), parts along dimension 0, may hold values from 0 to 16, as said below
- group: int32 [64], replicated, may hold values from 0 to 7, as said below
- group_rate: float32 [8, 16], replicated, may hold values from 0.02 to 0.4
Outputs:
- updated: float32 [64, 16, 16, 512], P(None, 'lev', 'band'), parts along dimension 2
There are 2 independent parts, one for each index of `band`. A program takes and returns all parts, laid end to end along the dimension named above; an argument that names none is the same for every part. Nothing has to cross between parts.
Inputs may be any that keep to these rules, and one draw needn't show every extreme that they name: `kmt`: 0 marks land; some column has all 16 levels wet and some is land. Every group holds some tracers.
All inputs are finite; a program needn't handle non-finite values.
Results may differ from a plain program's by a relative error of at most 0.0003.
Values sent between devices are 32-bit elements; how exact they have to be, the bound alone decides.
No kernel may reach another device: no remote copies, remote signals or barrier semaphores. Data moves between devices by JAX's collectives and lax.ppermute only.
A program may use at most 256 MiB of HBM per device.

v0:
```python
import jax
import jax.numpy as jnp
from jax import lax
from jax.sharding import PartitionSpec as P


def with_halo(cells, sides, width):
    for axis, dim in sides:
        count = lax.axis_size(axis)
        ends = count - 1
        head = lax.slice_in_dim(cells, 0, width, axis=dim)
        tail = lax.slice_in_dim(cells, cells.shape[dim] - width, cells.shape[dim], axis=dim)
        cells = jnp.concatenate(
            [
                lax.ppermute(tail, axis, [(i, (i + 1) % count) for i in range(ends)]),
                cells,
                lax.ppermute(head, axis, [((i + 1) % count, i) for i in range(ends)]),
            ],
            axis=dim,
        )
    return cells


def forward(carry, inputs):
    cprime, dprime = carry
    lower, diag, upper, rhs = inputs
    denom = diag - lower * cprime
    cnew = upper / denom
    dnew = (rhs - lower * dprime) / denom
    return ((cnew, dnew), (cnew, dnew))


def backward(x_next, inputs):
    cprime, dprime = inputs
    value = dprime - cprime * x_next
    return (value, value)


def rate_table(group, group_rate):
    ngrp = group_rate.shape[0]
    onehot = (group[:, None] == jnp.arange(ngrp, dtype=jnp.int32)[None]).astype(jnp.float32)
    return jnp.dot(onehot, group_rate, precision=lax.Precision.HIGHEST)


def block_step(
    tracer, east_flow, north_flow, up_flow, diffusivity, thickness, kmt, group, group_rate
):
    f32 = jnp.float32
    ntr, ldev, ny, nx = tracer.shape
    nz = thickness.shape[0]
    width = nx // lax.axis_size("lev")
    flows = jnp.stack([east_flow, north_flow, up_flow, diffusivity], 0)
    conc, flow_cols = (
        lax.all_to_all(tracer, "lev", split_axis=3, concat_axis=1, tiled=True),
        lax.all_to_all(flows, "lev", split_axis=3, concat_axis=1, tiled=True),
    )
    joined = jnp.concatenate([conc, flow_cols[:1]], 0)
    padded = with_halo(joined, (("lev", 3),), 1)
    conc_pad = padded[:ntr]
    east_all = padded[ntr]
    start = lax.axis_index("lev") * width
    kmt_ext = jnp.pad(kmt, ((0, 0), (1, 1)))
    kmt_pad = lax.dynamic_slice_in_dim(kmt_ext, start, width + 2, 1)
    level = jnp.arange(nz, dtype=jnp.int32)
    wet_pad = (level[:, None, None] < kmt_pad[None]).astype(f32)
    wet = wet_pad[:, :, 1:-1]
    east = east_all[:, :, :-1] * wet_pad[:, :, :-1] * wet_pad[:, :, 1:]
    face_e = (
        jnp.maximum(east, 0.0) * conc_pad[..., :-1] + jnp.minimum(east, 0.0) * conc_pad[..., 1:]
    )
    div_e = face_e[..., 1:] - face_e[..., :-1]
    north = flow_cols[1][:, :-1, :] * wet[:, :-1, :] * wet[:, 1:, :]
    face_n = jnp.maximum(north, 0.0) * conc[:, :, :-1] + jnp.minimum(north, 0.0) * conc[:, :, 1:]
    zrow = jnp.zeros((ntr, nz, 1, width), f32)
    div_n = jnp.concatenate([face_n, zrow], 2) - jnp.concatenate([zrow, face_n], 2)
    wet_up = wet * jnp.concatenate([jnp.zeros((1, ny, width), f32), wet[:-1]], 0)
    dz_prev = jnp.concatenate([thickness[:1], thickness[:-1]])
    dz3 = thickness[:, None, None]
    rate = rate_table(group, group_rate)
    zlev = jnp.zeros((ntr, 1, ny, width), f32)
    c_above = jnp.concatenate([zlev, conc[:, :-1]], 1)
    upward = flow_cols[2] * wet_up
    dz_min = jnp.minimum(dz_prev, thickness)[:, None, None]
    flux = dz_min * (jnp.maximum(upward, 0.0) * conc + jnp.minimum(upward, 0.0) * c_above)
    flux_below = jnp.concatenate([flux[:, 1:], zlev], 1)
    star = wet * (conc - div_e - div_n + (flux_below - flux) / dz3 - rate[:, :, None, None] * conc)
    coeff = flow_cols[3] * wet_up / (0.5 * (dz_prev + thickness))[:, None, None]
    ncol = ny * width
    coeff = coeff.reshape(nz, ncol)
    coeff_next = jnp.concatenate([coeff[1:], jnp.zeros((1, ncol), f32)], 0)
    lower = -coeff / thickness[:, None]
    upper = -coeff_next / thickness[:, None]
    diag = 1.0 - lower - upper
    rhs = jnp.moveaxis(star.reshape(ntr, nz, ncol), 1, 0)
    begin = (jnp.zeros((ntr, ncol), f32), jnp.zeros((ntr, ncol), f32))
    _, (cps, dps) = lax.scan(forward, begin, (lower, diag, upper, rhs))
    _, solved = lax.scan(backward, jnp.zeros((ntr, ncol), f32), (cps, dps), reverse=True)
    solved = jnp.moveaxis(solved, 0, 1).reshape(ntr, nz, ny, width)
    return lax.all_to_all(solved, "lev", split_axis=1, concat_axis=3, tiled=True)


def shards(tracer, east_flow, north_flow, up_flow, diffusivity, thickness, kmt, group, group_rate):
    return block_step(
        tracer, east_flow, north_flow, up_flow, diffusivity, thickness, kmt, group, group_rate
    )


def solution(mesh):
    placed = (
        P(None, "lev", "band", None),
        P("lev", "band", None),
        P("lev", "band", None),
        P("lev", "band", None),
        P("lev", "band", None),
        P(),
        P("band", None),
        P(),
        P(),
    )
    return jax.shard_map(
        shards, mesh=mesh, in_specs=placed, out_specs=P(None, "lev", "band", None), check_vma=False
    )
```

profile of v0, /device:TPU:0, one launch (start us, length us, event | category | flops | bytes accessed | tf_op | source)
XLA Modules:
  0.0 123.7 jit_solution(7248785982951354768)
XLA Ops:
  0.0 0.8 pad_maximum_fusion.9
  0.8 0.7 copy.80
  1.5 0.6 broadcast.83
  2.0 4.2 %reduce = f32[512,4,8]{2,1,0:T(4,128)S(1)} reduce(f32[512,4,1,8]{3,2,1,0:T(1,128)S(1)} %bitcast.100, f32[]{:T(128)} %broadcast.83), dimensions={2}, to_apply=%bitcast.63.reduce_sub_computation | reduce | bytes 131076
  6.3 1.8 %reshape.32 = f32[16,1,1024]{2,1,0:T(1,128)} reshape(f32[512,4,8]{2,1,0:T(4,128)S(1)} %reduce) | data formatting | bytes 131072
  8.1 7.4 %all-to-all-start = ((f32[16,1,1024]{2,1,0:T(1,128)}), f32[16,1,1024]{2,1,0:T(1,128)S(1)}, u32[]{:S(2)}, u32[]{:S(2)}) async-start(f32[16,1,1024]{2,1,0:T(1,128)} %reshape.32), calls=%async_computation | async-start | bytes 131072 | tf_op jit(solution)/shard_map/all_to_all | solution.py:55
  15.5 1.1 copy.85
  16.6 0.0 copy-start.6
  16.6 0.0 copy-start.7
  16.6 0.0 copy-start.8
  16.6 2.3 %reshape.34 = f32[16,1,16384]{2,1,0:T(1,128)} reshape(f32[512,1,8,64]{3,2,1,0:T(8,128)S(1)} %bitcast.96) | data formatting | bytes 2097152
  18.9 3.4 %all-to-all-done = f32[16,1,1024]{2,1,0:T(1,128)S(1)} async-done(((f32[16,1,1024]{2,1,0:T(1,128)}), f32[16,1,1024]{2,1,0:T(1,128)S(1)}, u32[]{:S(2)}, u32[]{:S(2)}) %all-to-all-start) | async-done | bytes 65568 | tf_op jit(solution)/shard_map/all_to_all | solution.py:55
  22.3 3.8 %all-to-all-start.1 = ((f32[16,1,16384]{2,1,0:T(1,128)}), f32[16,1,16384]{2,1,0:T(1,128)S(1)}, u32[]{:S(2)}, u32[]{:S(2)}) async-start(f32[16,1,16384]{2,1,0:T(1,128)} %reshape.34), calls=%async_computation.1 | async-start | bytes 2097152 | tf_op jit(solution)/shard_map/all_to_all | solution.py:54
  26.2 0.1 pad_dynamic-slice_fusion
  26.3 0.1 slice.125
  26.4 0.1 fusion.19
  26.5 0.0 copy-done
  26.5 0.2 fusion.17
  26.7 0.8 reduce.1
  27.6 1.7 %reshape.33 = f32[512,4,1,8]{3,2,1,0:T(1,128)S(1)} reshape(f32[16,1024]{1,0:T(8,128)S(1)} %reduce.1) | data formatting | bytes 131072
  29.2 0.4 copy.97
  29.6 2.2 %copy.88 = f32[1,16,8,32]{0,3,1,2:T(8,128)} copy(f32[1,16,8,32]{3,1,2,0:T(8,128)S(1)} %slice_bitcast_fusion.2) | data formatting | bytes 32768 | tf_op jit(solution)/shard_map/slice | solution.py:57
  31.8 0.1 broadcast_maximum_fusion
  31.9 0.1 slice.101
  32.0 0.1 neg.11
  32.1 0.1 subtract_subtract_fusion
  32.2 0.1 broadcast_maximum_fusion.2
  32.3 16.6 %all-to-all-done.1 = f32[16,1,16384]{2,1,0:T(1,128)S(1)} async-done(((f32[16,1,16384]{2,1,0:T(1,128)}), f32[16,1,16384]{2,1,0:T(1,128)S(1)}, u32[]{:S(2)}, u32[]{:S(2)}) %all-to-all-start.1) | async-done | bytes 1048608 | tf_op jit(solution)/shard_map/all_to_all | solution.py:54
  48.9 3.2 %reduce.2 = f32[16,16384]{1,0:T(8,128)S(1)} reduce(f32[16,1,16384]{2,1,0:T(1,128)S(1)} %all-to-all-done.1, f32[]{:T(128)} %broadcast.83), dimensions={1}, to_apply=%all_to_all.40.reduce_sub_computation | reduce | bytes 2097156 | tf_op jit(solution)/shard_map/all_to_all | solution.py:54
  52.1 2.2 %reshape.35 = f32[512,1,8,64]{3,2,1,0:T(8,128)} reshape(f32[16,16384]{1,0:T(8,128)S(1)} %reduce.2) | data formatting | bytes 2097152
  54.3 2.0 %copy.86 = f32[64,1,8,512]{0,3,2,1:T(8,128)S(1)} copy(f32[64,1,8,512]{0,2,1,3:T(8,128)} %bitcast.97) | data formatting | bytes 2097152 | tf_op jit(solution)/shard_map/all_to_all | solution.py:54
  56.3 0.2 slice.140
  56.5 1.4 %copy-done.1 = f32[1,16,8,32]{0,3,1,2:T(8,128)S(1)} copy-done((f32[1,16,8,32]{0,3,1,2:T(8,128)S(1)}, f32[1,16,8,32]{0,3,1,2:T(8,128)}, u32[]{:S(2)}) %copy-start.1) | copy-done | bytes 16408
  57.9 0.3 pad_maximum_fusion.8
  58.2 2.5 %collective-permute-start = (f32[65,16,8,1]{0,3,1,2:T(1,128)S(1)}, f32[65,16,8,1]{0,3,1,2:T(1,128)S(1)}, u32[]{:S(2)}, u32[]{:S(2)}) collective-permute-start(f32[65,16,8,1]{0,3,1,2:T(1,128)S(1)} %get-tuple-element.304), channel_id=1, source_target_pairs={{0,1},{1,2},{2,3},{3,4},{4,5},{5,6},{6,7},{7,8},{8,9},{9,10},{10,1... | collective-permute-start | bytes 99848 | tf_op jit(solution)/shard_map/ppermute | solution.py:15
  60.7 1.5 %collective-permute-start.1 = (f32[65,16,8,1]{0,3,1,2:T(1,128)S(1)}, f32[65,16,8,1]{0,3,1,2:T(1,128)S(1)}, u32[]{:S(2)}, u32[]{:S(2)}) collective-permute-start(f32[65,16,8,1]{0,3,1,2:T(1,128)S(1)} %get-tuple-element.305), channel_id=1, source_target_pairs={{1,0},{2,1},{3,2},{4,3},{5,4},{6,5},{7,6},{8,7},{9,8},{10,9},{11,1... | collective-permute-start | bytes 99848 | tf_op jit(solution)/shard_map/ppermute | solution.py:17
  62.3 1.3 %add_multiply_fusion = f32[64,16,8,32]{0,3,1,2:T(8,128)S(1)} fusion(f32[64,15,8,32]{0,3,1,2:T(8,128)S(1)} %slice.140, f32[64,16,8,32]{0,3,1,2:T(8,128)S(1)} %bitcast.90, f32[16,8,32]{2,0,1:T(8,128)S(1)} %get-tuple-element.307, f32[16,8,32]{2,0,1:T(8,128)S(1)} %get-tuple-element.306, f32[16]{0:T(128)S(1)} %get-tuple-element.315), kind=kLoop, calls=%fused_computation.30 | loop fusion | flops 1048576 | bytes 3113024 | tf_op jit(solution)/shard_map/mul | solution.py:84
  63.6 2.2 %fusion.12 = f32[64,16,7,32]{0,3,1,2:T(8,128)} fusion(f32[64,16,8,32]{0,3,1,2:T(8,128)S(1)} %bitcast.91, f32[16,7,32]{2,0,1:T(8,128)S(1)} %get-tuple-element.309, f32[16,7,32]{2,0,1:T(8,128)S(1)} %get-tuple-element.308), kind=kLoop, calls=%fused_computation.32 | loop fusion | flops 688128 | bytes 2781184 | tf_op jit(solution)/shard_map/add | solution.py:73
  65.7 0.0 copy-done.2
  65.7 0.0 collective-permute-done
  65.8 0.0 collective-permute-done.1
  65.8 2.6 %pad_maximum_fusion.4 = f32[1,16,8,34]{0,3,1,2:T(8,128)} fusion(f32[65,16,8,1]{0,3,1,2:T(1,128)S(1)} %collective-permute-done.1, f32[65,16,8,1]{0,3,1,2:T(1,128)S(1)} %collective-permute-done, f32[1,16,8,32]{0,3,1,2:T(8,128)S(1)} %copy-done.1, f32[64,16,8,32]{0,3,1,2:T(8,128)S(1)} %bitcast.92), kind=kLoop, calls=%fused_computation.21 | loop fusion | flops 13056 | bytes 1148928 | tf_op jit(solution)/shard_map/concatenate | solution.py:13
  68.4 2.7 %copy.100 = f32[1,16,8,34]{3,1,2,0:T(8,128)S(1)} copy(f32[1,16,8,34]{0,3,1,2:T(8,128)} %pad_maximum_fusion.4) | data formatting | bytes 34816 | tf_op jit(solution)/shard_map/squeeze | solution.py:60
  71.1 0.1 broadcast_maximum_fusion.1
  71.2 0.0 slice-start
  71.3 0.0 copy-start.4
  71.3 5.1 %fusion.5 = f32[64,16,8,33]{0,3,1,2:T(8,128)S(1)} fusion(f32[65,16,8,1]{0,3,1,2:T(1,128)S(1)} %collective-permute-done.1, f32[1,16,8,32]{0,3,1,2:T(8,128)} %copy.88, f32[64,16,8,32]{0,3,1,2:T(8,128)S(1)} %bitcast.93, f32[65,16,8,1]{0,3,1,2:T(1,128)S(1)} %collective-permute-done, f32[16,8,33]{2,0,1:T(8,128)S(1)} %get-tuple-element.313, ...), kind=kLoop, calls=%fused_computation.16 | loop fusion | flops 1892352 | bytes 2246656 | tf_op jit(solution)/shard_map/add | solution.py:69
  76.4 0.0 copy-done.3
  76.4 1.7 %fusion.11 = f32[64,16,8,32]{0,3,1,2:T(8,128)S(1)} fusion(f32[64,16,8,32]{0,3,1,2:T(8,128)S(1)} %bitcast.94, f32[64,16,8,33]{0,3,1,2:T(8,128)S(1)} %fusion.5, f32[64,16,8,32]{0,3,1,2:T(8,128)S(1)} %copy-done.3, f32[64,15,8,32]{0,3,1,2:T(8,128)S(1)} %slice-done, f32[64,16,7,32]{0,3,1,2:T(8,128)S(1)} %copy-done.4, f32[64,16]{0,1:T(8,128)S(1)} %fusion.17, ...), kind=kLoop, calls=%fused_computation.29 | loop fusion | flops 2621440 | bytes 7163968 | tf_op jit(solution)/shard_map/mul | solution.py:86
  78.1 0.2 copy.92
  78.4 0.6 copy.93
  78.9 0.1 broadcast.47.clone
  79.0 0.1 broadcast.47.clone.1
  79.2 1.8 %while.34 = (s32[]{:T(128)}, f32[64,256]{1,0:T(8,128)S(1)}, f32[64,256]{1,0:T(8,128)S(1)}, f32[16,64,256]{2,1,0:T(8,128)S(1)}, f32[16,64,256]{2,1,0:T(8,128)S(1)...) while((s32[]{:T(128)}, f32[64,256]{1,0:T(8,128)S(1)}, ...), condition=%wide.region_1.2_spmd.clone, body=%wide.region_0.1_spmd.clone.sunk | while | flops 131075 | bytes 468099 | solution.py:96
  80.9 0.1 broadcast.47
  81.0 0.7 while.35
  81.7 0.6 copy.94
  82.3 1.3 %reshape.36 = f32[16,1,16384]{2,1,0:T(1,128)S(1)} reshape(f32[16,8,32,64]{3,2,1,0:T(8,128)S(1)} %bitcast.95) | data formatting | bytes 2097152
  83.7 33.7 %all_to_all.51 = f32[16,1,16384]{2,1,0:T(1,128)S(1)} all-to-all(f32[16,1,16384]{2,1,0:T(1,128)S(1)} %reshape.36), channel_id=1, replica_groups=mesh['band'=2,'lev'=16] {'lev'}, dimensions={0} | all-to-all | bytes 2097152 | tf_op jit(solution)/shard_map/all_to_all | solution.py:99
  117.4 3.2 %reduce.3 = f32[16,16384]{1,0:T(8,128)S(1)} reduce(f32[16,1,16384]{2,1,0:T(1,128)S(1)} %all_to_all.51, f32[]{:T(128)} %broadcast.83), dimensions={1}, to_apply=%all_to_all.44.reduce_sub_computation | reduce | bytes 2097156 | tf_op jit(solution)/shard_map/all_to_all | solution.py:99
  120.6 0.8 reshape.37
  121.5 0.2 bitcast_bitcast_fusion
  121.7 0.2 copy.95
  121.9 1.8 %copy.96 = f32[64,1,8,512]{3,2,1,0:T(8,128)} copy(f32[64,1,8,512]{0,3,2,1:T(8,128)S(1)} %bitcast.99) | data formatting | bytes 2097152 | tf_op jit(solution)/shard_map/all_to_all | solution.py:99
  (84 shorter events, 1.6 us)
Async XLA Ops:
  0.0 26.5 %copy-start = (f32[8,16]{1,0:T(8,128)S(1)}, f32[8,16]{1,0:T(8,128)}, u32[]{:S(2)}) copy-start(f32[8,16]{1,0:T(8,128)} %param.21) | copy-start | bytes 1540
  0.8 14.7 %copy-start.5 = (f32[64,1,8,512]{3,2,1,0:T(8,128)S(1)}, f32[64,1,8,512]{3,2,1,0:T(8,128)}, u32[]{:S(2)}) copy-start(f32[64,1,8,512]{3,2,1,0:T(8,128)} %param.13) | copy-start | bytes 3145732
  8.1 14.3 %all-to-all-start = ((f32[16,1,1024]{2,1,0:T(1,128)}), f32[16,1,1024]{2,1,0:T(1,128)S(1)}, u32[]{:S(2)}, u32[]{:S(2)}) async-start(f32[16,1,1024]{2,1,0:T(1,128)} %reshape.32), calls=%async_computation | async-start | bytes 131072 | tf_op jit(solution)/shard_map/all_to_all | solution.py:55
  16.6 9.6 %copy-start.6 = (s32[8,512]{1,0:T(8,128)S(1)}, s32[8,512]{1,0:T(8,128)}, u32[]{:S(2)}) copy-start(s32[8,512]{1,0:T(8,128)} %param.19) | copy-start | bytes 49156
  16.6 9.8 %copy-start.7 = (f32[16]{0:T(128)S(1)}, f32[16]{0:T(128)}, u32[]{:S(2)}) copy-start(f32[16]{0:T(128)} %param.18) | copy-start | bytes 196
  16.6 9.9 %copy-start.8 = (s32[64]{0:T(128)S(1)}, s32[64]{0:T(128)}, u32[]{:S(2)}) copy-start(s32[64]{0:T(128)} %param.20) | copy-start | bytes 772
  22.3 26.6 %all-to-all-start.1 = ((f32[16,1,16384]{2,1,0:T(1,128)}), f32[16,1,16384]{2,1,0:T(1,128)S(1)}, u32[]{:S(2)}, u32[]{:S(2)}) async-start(f32[16,1,16384]{2,1,0:T(1,128)} %reshape.34), calls=%async_computation.1 | async-start | bytes 2097152 | tf_op jit(solution)/shard_map/all_to_all | solution.py:54
  56.3 1.6 %copy-start.1 = (f32[1,16,8,32]{0,3,1,2:T(8,128)S(1)}, f32[1,16,8,32]{0,3,1,2:T(8,128)}, u32[]{:S(2)}) copy-start(f32[1,16,8,32]{0,3,1,2:T(8,128)} %copy.88) | copy-start | bytes 49156
  58.2 7.5 %collective-permute-start = (f32[65,16,8,1]{0,3,1,2:T(1,128)S(1)}, f32[65,16,8,1]{0,3,1,2:T(1,128)S(1)}, u32[]{:S(2)}, u32[]{:S(2)}) collective-permute-start(f32[65,16,8,1]{0,3,1,2:T(1,128)S(1)} %get-tuple-element.304), channel_id=1, source_target_pairs={{0,1},{1,2},{2,3},{3,4},{4,5},{5,6},{6,7},{7,8},{8,9},{9,10},{10,1... | collective-permute-start | bytes 99848 | tf_op jit(solution)/shard_map/ppermute | solution.py:15
  60.7 5.0 %collective-permute-start.1 = (f32[65,16,8,1]{0,3,1,2:T(1,128)S(1)}, f32[65,16,8,1]{0,3,1,2:T(1,128)S(1)}, u32[]{:S(2)}, u32[]{:S(2)}) collective-permute-start(f32[65,16,8,1]{0,3,1,2:T(1,128)S(1)} %get-tuple-element.305), channel_id=1, source_target_pairs={{1,0},{2,1},{3,2},{4,3},{5,4},{6,5},{7,6},{8,7},{9,8},{10,9},{11,1... | collective-permute-start | bytes 99848 | tf_op jit(solution)/shard_map/ppermute | solution.py:17
  63.6 2.2 %copy-start.2 = (f32[64,16,8,32]{0,3,1,2:T(8,128)}, f32[64,16,8,32]{0,3,1,2:T(8,128)S(1)}, u32[]{:S(2)}) copy-start(f32[64,16,8,32]{0,3,1,2:T(8,128)S(1)} %add_multiply_fusion) | copy-start | bytes 3145732
  71.2 5.1 %copy-start.3 = (f32[64,16,8,32]{0,3,1,2:T(8,128)S(1)}, f32[64,16,8,32]{0,3,1,2:T(8,128)}, u32[]{:S(2)}) copy-start(f32[64,16,8,32]{0,3,1,2:T(8,128)} %copy-done.2) | copy-start | bytes 3145732
  71.2 5.1 %slice-start = ((f32[64,16,8,32]{0,3,1,2:T(8,128)}), f32[64,15,8,32]{0,3,1,2:T(8,128)S(1)}, s32[]{:S(2)}) async-start(f32[64,16,8,32]{0,3,1,2:T(8,128)} %copy-done.2), calls=%async_computation.3 | async-start | bytes 3932160 | tf_op jit(solution)/shard_map/slice | solution.py:85
  71.3 5.1 %copy-start.4 = (f32[64,16,7,32]{0,3,1,2:T(8,128)S(1)}, f32[64,16,7,32]{0,3,1,2:T(8,128)}, u32[]{:S(2)}) copy-start(f32[64,16,7,32]{0,3,1,2:T(8,128)} %fusion.12) | copy-start | bytes 2752516
where the time goes:
time: 125 us; the launch traced here: 124 us
  blocking collectives  33.7 us (27%)
  other arithmetic  27.2 us (22%)
  local copies, waits for them, and re-layouts  25.9 us (21%)
  waiting for transfers between devices  20 us (16%)
  starting transfers between devices  15.2 us (12%)
    all_to_all x1, blocking collectives, block_step(): lax.all_to_all(solved, 'lev', split_axis=1, concat_axis=3, tiled=True)  33.7 us
    all_to_all x1, waiting for transfers between devices, block_step(): lax.all_to_all(tracer, 'lev', split_axis=3, concat_axis=1, tiled=True)  16.6 us
    unnamed x27, local copies, waits for them, and re-layouts  13.7 us
    all_to_all x1, starting transfers between devices, block_step(): lax.all_to_all(flows, 'lev', split_axis=3, concat_axis=1, tiled=True)  7.39 us
    add x1, other arithmetic, block_step(): jnp.maximum(east, 0.0) * conc_pad[..., :-1]  5.09 us
    unnamed x4, other arithmetic  4.25 us
    all_to_all x1, starting transfers between devices, block_step(): lax.all_to_all(tracer, 'lev', split_axis=3, concat_axis=1, tiled=True)  3.84 us
    all_to_all x1, waiting for transfers between devices, block_step(): lax.all_to_all(flows, 'lev', split_axis=3, concat_axis=1, tiled=True)  3.43 us
  transfers between devices with their start and end apart: 4, of which 2 were waited for; matrix products, arithmetic and copies ran while one was open for 10% of the time, Pallas kernels for 0%

commit v1 on v0

v1 whole, which is shorter than its diff:
```python
import functools

import jax
import jax.numpy as jnp
from jax import lax
from jax.experimental import pallas as pl
from jax.experimental.pallas import tpu as pltpu
from jax.sharding import PartitionSpec as P

LANES = 128
ROWS = 8
EAST, NORTH, UP, DIFF, EDGE, EXTRA = 0, 1, 2, 3, 4, 5
f32 = jnp.float32
VMEM_LIMIT = 32 * 1024 * 1024


def lanes_iota():
    return lax.broadcasted_iota(jnp.int32, (ROWS, LANES), 1)


def rows_iota():
    return lax.broadcasted_iota(jnp.int32, (ROWS, LANES), 0)


def pack_kernel(nb, tc, tpc, meta, tracer, east, north, up, diff, kmt, out):
    level = meta[0]
    lane = lanes_iota()
    wet = [
        (level < kmt[:, b * LANES : (b + 1) * LANES]).astype(f32) for b in range(nb)
    ]
    flow = [None]
    for b in range(1, nb):
        ends = east[0, :, b * LANES - LANES : b * LANES][:, LANES - 1 :]
        ends = ends * wet[b - 1][:, LANES - 1 :] * wet[b][:, :1]
        flow.append(jnp.broadcast_to(ends, (ROWS, LANES)))
    for c in range(tc):
        faces = [jnp.zeros((ROWS, LANES), f32) for _ in range(nb)]
        for t in range(tpc):
            tiles = [tracer[c * tpc + t, 0, :, b * LANES : (b + 1) * LANES] for b in range(nb)]
            for b in range(nb):
                out[b * tc + c, t] = tiles[b]
            for b in range(1, nb):
                west = pltpu.roll(tiles[b - 1], (2 * t + 1) % LANES, 1)
                here = pltpu.roll(tiles[b], 2 * t, 1) if t else tiles[b]
                face = jnp.maximum(flow[b], 0.0) * west + jnp.minimum(flow[b], 0.0) * here
                faces[b] = jnp.where(lane == 2 * t, face, faces[b])
        for b in range(nb):
            edge = faces[b]
            if b + 1 < nb:
                edge = edge - pltpu.roll(faces[b + 1], LANES - 1, 1)
            out[b * tc + c, tpc + EDGE] = edge
    for b in range(nb):
        cols = slice(b * LANES, (b + 1) * LANES)
        for c in range(tc):
            out[b * tc + c, tpc + EAST] = east[0, :, cols]
            out[b * tc + c, tpc + NORTH] = north[0, :, cols]
            out[b * tc + c, tpc + UP] = up[0, :, cols]
            out[b * tc + c, tpc + DIFF] = diff[0, :, cols]


def solve_kernel(
    half, tpc, meta, thickness, group, rates, got, kmt_all, across,
    f_out, cin_out, alpha_out, message,
):
    upper, block, chunk = meta[0], meta[1], meta[2]
    sign = 1.0 - 2.0 * upper.astype(f32)
    kmt = kmt_all[:, pl.ds(pl.multiple_of(block * LANES, LANES), LANES)]
    lane, row = lanes_iota(), rows_iota()
    ends = jnp.logical_or(lane == 0, lane == LANES - 1)
    first = jnp.where(upper == 1, 2 * half - 1, 0)
    step = 1 - 2 * upper

    def level_of(o):
        return first + step * o

    def slot_of(o):
        return jnp.where(upper == 1, half - 1 - o, o)

    zero = jnp.zeros((ROWS, LANES), f32)
    cin = tout = outer = add_mid = zero
    for o in range(half):
        k = level_of(o)
        slot = slot_of(o)
        dz, dz_next = thickness[k], thickness[level_of(o + 1)]
        wet = (k < kmt).astype(f32)
        wet_next = (level_of(o + 1) < kmt).astype(f32)
        if o + 1 < half:
            face = jnp.where(upper == 1, slot, slot_of(o + 1))
            w, g = got[face, tpc + UP], got[face, tpc + DIFF]
        else:
            w = jnp.where(upper == 1, got[0, tpc + UP], across[0])
            g = jnp.where(upper == 1, got[0, tpc + DIFF], across[1])
        open_face = wet * wet_next
        w = sign * w * open_face
        g = g * open_face / (0.5 * (dz + dz_next))
        dz_min = jnp.minimum(dz, dz_next)
        pos, neg = dz_min * jnp.maximum(w, 0.0), dz_min * jnp.minimum(w, 0.0)
        inner = -g / dz
        tin = pos / dz
        mid = wet + add_mid + neg / dz
        alpha = 1.0 / (1.0 - outer - inner - outer * cin)
        cin_new = inner * alpha
        east = got[slot, tpc + EAST] * wet * pltpu.roll(wet, LANES - 1, 1)
        east = jnp.where(lane == LANES - 1, 0.0, east)
        north = got[slot, tpc + NORTH] * wet * pltpu.roll(wet, ROWS - 1, 0)
        north = jnp.where(row == ROWS - 1, 0.0, north)
        e_pos, e_neg = jnp.maximum(east, 0.0), jnp.minimum(east, 0.0)
        n_pos, n_neg = jnp.maximum(north, 0.0), jnp.minimum(north, 0.0)
        edges = got[slot, tpc + EDGE]
        last = o + 1 == half
        prev_slot = slot_of(o - 1) if o else None
        next_slot = None if last else slot_of(o + 1)
        tout_next = -neg / dz_next
        outer_next = -g / dz_next

        def body(t, _, o=o, k=k, slot=slot, wet=wet, mid=mid, tin=tin, tout=tout, outer=outer,
                 alpha=alpha, e_pos=e_pos, e_neg=e_neg, n_pos=n_pos, n_neg=n_neg, edges=edges,
                 last=last, prev_slot=prev_slot, next_slot=next_slot, tout_next=tout_next,
                 outer_next=outer_next):
            c = got[slot, t]
            rate = rates[group[chunk * tpc + t], k]
            star = c * (mid - rate * wet)
            if o:
                star += tout * got[prev_slot, t]
            if not last:
                star += tin * got[next_slot, t]
            fe = e_pos * c + e_neg * pltpu.roll(c, LANES - 1, 1)
            fn = n_pos * c + n_neg * pltpu.roll(c, ROWS - 1, 0)
            star -= fe - pltpu.roll(fe, 1, 1)
            star -= fn - pltpu.roll(fn, 1, 0)
            star += jnp.where(ends, pltpu.roll(edges, (LANES - 2 * t) % LANES, 1), 0.0)
            if o:
                star -= outer * f_out[o - 1, t]
            f = alpha * star
            f_out[o, t] = f
            if last:
                message[t] = tout_next * c - outer_next * f
            return 0

        lax.fori_loop(0, tpc, body, 0, unroll=8)
        cin_out[o] = cin_new
        if last:
            alpha_out[0] = alpha
            alpha_out[1] = outer_next
            message[tpc] = alpha
        cin, tout, outer, add_mid = cin_new, tout_next, outer_next, -pos / dz_next


def back_kernel(half, tpc, meta, f_in, cin, alpha, sent, got, out):
    upper = meta[0]
    other = cin[half - 1] * got[tpc]
    scale = 1.0 / (1.0 - other * alpha[1])
    mine, theirs = scale * alpha[0], scale * other

    def body(t, _):
        x = f_in[half - 1, t] + (mine * got[t] - theirs * sent[t])
        out[jnp.where(upper == 1, 0, half - 1), t] = x
        for o in range(half - 2, -1, -1):
            x = f_in[o, t] - cin[o] * x
            out[jnp.where(upper == 1, half - 1 - o, o), t] = x
        return 0

    lax.fori_loop(0, tpc, body, 0, unroll=8)


def join_kernel(nb, tc, tpc, got, out):
    for b in range(nb):
        for c in range(tc):
            out[c * tpc : (c + 1) * tpc, 0, :, b * LANES : (b + 1) * LANES] = got[b * tc + c]


def shards(tracer, east_flow, north_flow, up_flow, diffusivity, thickness, kmt, group, group_rate):
    ntr, ldev, ny, nx = tracer.shape
    count = lax.axis_size("lev")
    half = count // 2
    nb = nx // LANES
    tc = half // nb
    tpc = ntr // tc
    assert ldev == 1 and ny == ROWS and nb * LANES == nx and tc * nb == half and tpc * tc == ntr
    index = lax.axis_index("lev").astype(jnp.int32)
    upper, rank = index // half, index % half
    meta = jnp.stack([upper, rank // tc, rank % tc, index])
    vm = pl.BlockSpec(memory_space=pltpu.VMEM)
    sm = pl.BlockSpec(memory_space=pltpu.SMEM)
    params = pltpu.CompilerParams(vmem_limit_bytes=VMEM_LIMIT)
    groups = [[h * half + i for i in range(half)] for h in range(2)]

    pieces = pl.pallas_call(
        functools.partial(pack_kernel, nb, tc, tpc),
        out_shape=jax.ShapeDtypeStruct((half, tpc + EXTRA, ROWS, LANES), f32),
        in_specs=[sm] + [vm] * 6,
        out_specs=vm,
        compiler_params=params,
        name="pack",
    )(index[None], tracer, east_flow, north_flow, up_flow, diffusivity, kmt)
    got = lax.all_to_all(pieces, "lev", 0, 0, axis_index_groups=groups, tiled=True)

    fields = jnp.concatenate([up_flow, diffusivity], 0)
    across = jnp.zeros((2, ROWS, LANES), f32)
    for r in range(half):
        cols = lax.slice_in_dim(fields, (r // tc) * LANES, (r // tc + 1) * LANES, axis=2)
        across = across + lax.ppermute(cols, "lev", [(half, r)])

    tile = (ROWS, LANES)
    f, cin, alpha, message = pl.pallas_call(
        functools.partial(solve_kernel, half, tpc),
        out_shape=(
            jax.ShapeDtypeStruct((half, tpc) + tile, f32),
            jax.ShapeDtypeStruct((half,) + tile, f32),
            jax.ShapeDtypeStruct((2,) + tile, f32),
            jax.ShapeDtypeStruct((tpc + 1,) + tile, f32),
        ),
        in_specs=[sm, sm, sm, sm, vm, vm, vm],
        out_specs=(vm, vm, vm, vm),
        compiler_params=params,
        name="solve",
    )(meta, thickness, group, group_rate, got, kmt, across)
    theirs = lax.ppermute(
        message, "lev", [(i, (i + half) % count) for i in range(count)]
    )
    solved = pl.pallas_call(
        functools.partial(back_kernel, half, tpc),
        out_shape=jax.ShapeDtypeStruct((half, tpc) + tile, f32),
        in_specs=[sm, vm, vm, vm, vm, vm],
        out_specs=vm,
        compiler_params=params,
        name="back",
    )(meta, f, cin, alpha, message, theirs)
    back = lax.all_to_all(solved, "lev", 0, 0, axis_index_groups=groups, tiled=True)
    return pl.pallas_call(
        functools.partial(join_kernel, nb, tc, tpc),
        out_shape=jax.ShapeDtypeStruct(tracer.shape, f32),
        in_specs=[vm],
        out_specs=vm,
        compiler_params=params,
        name="join",
    )(back)


def solution(mesh):
    placed = (
        P(None, "lev", "band", None),
        P("lev", "band", None),
        P("lev", "band", None),
        P("lev", "band", None),
        P("lev", "band", None),
        P(),
        P("band", None),
        P(),
        P(),
    )
    return jax.shard_map(
        shards, mesh=mesh, in_specs=placed, out_specs=P(None, "lev", "band", None), check_vma=False
    )
```

time: 125 us -> 63 us (0.50)
  other arithmetic: 27.2 us -> 0.09 us
  local copies, waits for them, and re-layouts: 25.9 us -> 4.85 us
  blocking collectives: 33.7 us -> 17 us
  Pallas kernels: 0 us -> 9.65 us
  waiting for transfers between devices: 20 us -> 16.8 us
  starting transfers between devices: 15.2 us -> 13.6 us
    all_to_all x1, blocking collectives: 33.7 us -> 17 us  [shards(): lax.all_to_all(solved, 'lev', 0, 0, axis_index_groups=groups, tiled=True)]
    all_to_all x2 -> x1, waiting for transfers between devices: 20 us -> 7.1 us  [shards(): lax.all_to_all(pieces, 'lev', 0, 0, axis_index_groups=groups, tiled=True)]
    ppermute x2 -> x9, waiting for transfers between devices: 0.01 us -> 9.72 us  [the longest x1 6.47 us: shards(): lax.ppermute(message, 'lev', [(i, (i + half) % count) for i in range(coun...]
    pallas_call x0 -> x4, Pallas kernels: none -> 9.65 us  [the longest x1 6.09 us: shards(): pl.pallas_call(functools.partial(solve_kernel, half, tpc), out_shape=(jax...]
    unnamed x27 -> x25, local copies, waits for them, and re-layouts: 13.7 us -> 4.84 us
    all_to_all x3 -> x0, other arithmetic: 7.29 us -> none  [the longest x1 3.23 us: block_step(): lax.all_to_all(tracer, 'lev', split_axis=3, concat_axis=1, tiled=True)]
    add x2 -> x1, other arithmetic: 7.26 us -> 0.01 us  [shards(): across = across + lax.ppermute(cols, 'lev', [(half, r)])]
    all_to_all x2 -> x1, starting transfers between devices: 11.2 us -> 5.4 us  [shards(): lax.all_to_all(pieces, 'lev', 0, 0, axis_index_groups=groups, tiled=True)]
  transfers between devices with their start and end apart: 4 -> 10, of which waited for: 2 -> 3; matrix products, arithmetic and copies ran while one was open for 10% -> 0% of each run, Pallas kernels for 0% -> 0%
where the time goes in v1:
time: 63 us; the launch traced here: 62.3 us
  blocking collectives  17 us (27%)
  waiting for transfers between devices  16.8 us (27%)
  starting transfers between devices  13.6 us (22%)
  Pallas kernels  9.65 us (15%)
  local copies, waits for them, and re-layouts  4.85 us (8%)
    all_to_all x1, blocking collectives, shards(): lax.all_to_all(solved, 'lev', 0, 0, axis_index_groups=groups, tiled=True)  17 us
    all_to_all x1, waiting for transfers between devices, shards(): lax.all_to_all(pieces, 'lev', 0, 0, axis_index_groups=groups, tiled=True)  7.1 us
    ppermute x1, waiting for transfers between devices, shards(): lax.ppermute(message, 'lev', [(i, (i + half) % count) for i in range(coun...  6.47 us
    pallas_call x1, Pallas kernels, shards(): pl.pallas_call(functools.partial(solve_kernel, half, tpc), out_shape=(jax...  6.09 us
    ppermute x8, starting transfers between devices, shards(): across = across + lax.ppermute(cols, 'lev', [(half, r)])  5.91 us
    all_to_all x1, starting transfers between devices, shards(): lax.all_to_all(pieces, 'lev', 0, 0, axis_index_groups=groups, tiled=True)  5.4 us
    unnamed x25, local copies, waits for them, and re-layouts  4.84 us
    ppermute x8, waiting for transfers between devices, shards(): across = across + lax.ppermute(cols, 'lev', [(half, r)])  3.26 us
  transfers between devices with their start and end apart: 10, of which 3 were waited for; matrix products, arithmetic and copies ran while one was open for 0% of the time, Pallas kernels for 0%

profile of v1, /device:TPU:0, one launch (start us, length us, event | category | flops | bytes accessed | tf_op | source)
XLA Modules:
  0.0 62.3 jit_solution(12354124844009185669)
XLA Ops:
  0.0 0.0 copy-start
  0.0 1.2 %copy-done = f32[64,1,8,512]{3,2,1,0:T(8,128)S(1)} copy-done((f32[64,1,8,512]{3,2,1,0:T(8,128)S(1)}, f32[64,1,8,512]{3,2,1,0:T(8,128)}, u32[]{:S(2)}) %copy-start) | copy-done | bytes 1048600
  1.2 0.0 copy-start.1
  1.2 0.7 %copy-done.1 = f32[1,8,512]{2,1,0:T(8,128)S(1)} copy-done((f32[1,8,512]{2,1,0:T(8,128)S(1)}, f32[1,8,512]{2,1,0:T(8,128)}, u32[]{:S(2)}) %copy-start.1) | copy-done | bytes 16408
  1.9 0.0 copy-start.3
  1.9 0.7 %copy-done.3 = f32[1,8,512]{2,1,0:T(8,128)S(1)} copy-done((f32[1,8,512]{2,1,0:T(8,128)S(1)}, f32[1,8,512]{2,1,0:T(8,128)}, u32[]{:S(2)}) %copy-start.3) | copy-done | bytes 16408
  2.7 0.0 copy-start.5
  2.7 0.7 %copy-done.5 = s32[8,512]{1,0:T(8,128)S(1)} copy-done((s32[8,512]{1,0:T(8,128)S(1)}, s32[8,512]{1,0:T(8,128)}, u32[]{:S(2)}) %copy-start.5) | copy-done | bytes 16408
  3.4 0.0 copy-start.7
  3.4 0.7 %copy-done.7 = f32[1,8,512]{2,1,0:T(8,128)S(1)} copy-done((f32[1,8,512]{2,1,0:T(8,128)S(1)}, f32[1,8,512]{2,1,0:T(8,128)}, u32[]{:S(2)}) %copy-start.7) | copy-done | bytes 16408
  4.1 0.0 copy-start.8
  4.1 0.7 %copy-done.8 = f32[1,8,512]{2,1,0:T(8,128)S(1)} copy-done((f32[1,8,512]{2,1,0:T(8,128)S(1)}, f32[1,8,512]{2,1,0:T(8,128)}, u32[]{:S(2)}) %copy-start.8) | copy-done | bytes 16408
  4.8 1.7 %pack.1 = f32[8,37,8,128]{3,2,1,0:T(8,128)} custom-call(s32[1]{0:T(128)} %bitcast.3.meta, f32[64,1,8,512]{3,2,1,0:T(8,128)S(1)} %copy-done, f32[1,8,512]{2,1,0:T(8,128)S(1)} %copy-done.7, f32[1,8,512]{2,1,0:T(8,128)S(1)} %copy-done.8, f32[1,8,512]{2,1,0:T(8,128)S(1)} %copy-done.1, f32[1,8,512]{2,1,0:T(8,128)S(1)} %copy-done.3, s32[8,512]{1,0:T(8,128)S(1)} %copy-done.5), custom_call_target="tpu_custom_call" | custom-call | tf_op jit(solution)/shard_map/pack/pallas_call | solution.py:188
  6.5 0.0 copy-start.2
  6.5 0.0 copy-start.4
  6.5 0.0 copy-start.6
  6.5 0.0 copy-start.9
  6.5 0.0 copy-start.10
  6.5 0.0 copy-start.11
  6.5 5.4 %all-to-all-start = ((f32[8,37,8,128]{3,2,1,0:T(8,128)}), f32[8,37,8,128]{3,2,1,0:T(8,128)S(1)}, u32[]{:S(2)}, u32[]{:S(2)}) async-start(f32[8,37,8,128]{3,2,1,0:T(8,128)} %pack.1), calls=%async_computation | async-start | bytes 2424832 | tf_op jit(solution)/shard_map/all_to_all | solution.py:196
  11.9 0.0 copy-done.2
  12.0 0.0 copy-done.4
  12.0 0.7 %collective-permute-start.1 = (f32[2,8,128]{2,1,0:T(8,128)S(1)}, f32[2,8,128]{2,1,0:T(8,128)S(1)}, u32[]{:S(2)}, u32[]{:S(2)}) collective-permute-start(f32[2,8,128]{2,1,0:T(8,128)S(1)} %get-tuple-element.13), channel_id=1, source_target_pairs={{8,1},{24,17}} | collective-permute-start | bytes 24584 | tf_op jit(solution)/shard_map/ppermute | solution.py:202
  12.7 1.3 %collective-permute-start = (f32[2,8,128]{2,1,0:T(8,128)S(1)}, f32[2,8,128]{2,1,0:T(8,128)S(1)}, u32[]{:S(2)}, u32[]{:S(2)}) collective-permute-start(f32[2,8,128]{2,1,0:T(8,128)S(1)} %get-tuple-element.13), channel_id=1, source_target_pairs={{8,0},{24,16}} | collective-permute-start | bytes 24584 | tf_op jit(solution)/shard_map/ppermute | solution.py:202
  14.0 0.7 %collective-permute-start.7 = (f32[2,8,128]{2,1,0:T(8,128)S(1)}, f32[2,8,128]{2,1,0:T(8,128)S(1)}, u32[]{:S(2)}, u32[]{:S(2)}) collective-permute-start(f32[2,8,128]{2,1,0:T(8,128)S(1)} %get-tuple-element.14), channel_id=1, source_target_pairs={{8,7},{24,23}} | collective-permute-start | bytes 24584 | tf_op jit(solution)/shard_map/ppermute | solution.py:202
  14.6 0.7 %collective-permute-start.6 = (f32[2,8,128]{2,1,0:T(8,128)S(1)}, f32[2,8,128]{2,1,0:T(8,128)S(1)}, u32[]{:S(2)}, u32[]{:S(2)}) collective-permute-start(f32[2,8,128]{2,1,0:T(8,128)S(1)} %get-tuple-element.14), channel_id=1, source_target_pairs={{8,6},{24,22}} | collective-permute-start | bytes 24584 | tf_op jit(solution)/shard_map/ppermute | solution.py:202
  15.3 0.7 %collective-permute-start.5 = (f32[2,8,128]{2,1,0:T(8,128)S(1)}, f32[2,8,128]{2,1,0:T(8,128)S(1)}, u32[]{:S(2)}, u32[]{:S(2)}) collective-permute-start(f32[2,8,128]{2,1,0:T(8,128)S(1)} %get-tuple-element.15), channel_id=1, source_target_pairs={{8,5},{24,21}} | collective-permute-start | bytes 24584 | tf_op jit(solution)/shard_map/ppermute | solution.py:202
  16.0 0.0 collective-permute-done.1
  16.0 0.7 %collective-permute-start.4 = (f32[2,8,128]{2,1,0:T(8,128)S(1)}, f32[2,8,128]{2,1,0:T(8,128)S(1)}, u32[]{:S(2)}, u32[]{:S(2)}) collective-permute-start(f32[2,8,128]{2,1,0:T(8,128)S(1)} %get-tuple-element.15), channel_id=1, source_target_pairs={{8,4},{24,20}} | collective-permute-start | bytes 24584 | tf_op jit(solution)/shard_map/ppermute | solution.py:202
  16.7 3.2 %collective-permute-done = f32[2,8,128]{2,1,0:T(8,128)S(1)} collective-permute-done((f32[2,8,128]{2,1,0:T(8,128)S(1)}, f32[2,8,128]{2,1,0:T(8,128)S(1)}, u32[]{:S(2)}, u32[]{:S(2)}) %collective-permute-start) | collective-permute-done | bytes 8224 | tf_op jit(solution)/shard_map/ppermute | solution.py:202
  19.9 0.7 %collective-permute-start.3 = (f32[2,8,128]{2,1,0:T(8,128)S(1)}, f32[2,8,128]{2,1,0:T(8,128)S(1)}, u32[]{:S(2)}, u32[]{:S(2)}) collective-permute-start(f32[2,8,128]{2,1,0:T(8,128)S(1)} %get-tuple-element.16), channel_id=1, source_target_pairs={{8,3},{24,19}} | collective-permute-start | bytes 24584 | tf_op jit(solution)/shard_map/ppermute | solution.py:202
  20.6 0.0 collective-permute-done.7
  20.6 0.7 %collective-permute-start.2 = (f32[2,8,128]{2,1,0:T(8,128)S(1)}, f32[2,8,128]{2,1,0:T(8,128)S(1)}, u32[]{:S(2)}, u32[]{:S(2)}) collective-permute-start(f32[2,8,128]{2,1,0:T(8,128)S(1)} %get-tuple-element.16), channel_id=1, source_target_pairs={{8,2},{24,18}} | collective-permute-start | bytes 24584 | tf_op jit(solution)/shard_map/ppermute | solution.py:202
  21.3 0.1 pad_add_fusion.meta
  21.3 0.0 collective-permute-done.6
  21.4 0.0 collective-permute-done.5
  21.4 0.0 collective-permute-done.4
  21.4 0.0 collective-permute-done.3
  21.4 0.0 collective-permute-done.2
  21.4 7.1 %all-to-all-done.got = f32[8,37,8,128]{3,2,1,0:T(8,128)S(1)} async-done(((f32[8,37,8,128]{3,2,1,0:T(8,128)}), f32[8,37,8,128]{3,2,1,0:T(8,128)S(1)}, u32[]{:S(2)}, u32[]{:S(2)}) %all-to-all-start) | async-done | bytes 1212448 | tf_op jit(solution)/shard_map/all_to_all | solution.py:196
  28.5 0.0 copy-done.6
  28.5 0.0 copy-done.9
  28.5 0.0 copy-done.10
  28.5 0.0 copy-done.11
  28.5 6.1 %solve.1 = (f32[8,32,8,128]{3,2,1,0:T(8,128)S(1)}, f32[8,8,128]{2,1,0:T(8,128)S(1)}, f32[2,8,128]{2,1,0:T(8,128)S(1)}, f32[33,8,128]{2,1,0:T(8,128)S(1)}) custom-call(s32[4]{0:T(128)S(1)} %pad_add_fusion.meta, f32[16]{0:T(128)S(1)} %copy-done.10, s32[64]{0:T(128)S(1)} %copy-done.11, f32[8,16]{1,0:T(8,128)S(1)} %copy-done.9, ...), custom_call_target="tpu_custom_call" | custom-call | tf_op jit(solution)/shard_map/solve/pallas_call | solution.py:205
  34.6 2.3 %collective-permute-start.8 = (f32[33,8,128]{2,1,0:T(8,128)S(1)}, f32[33,8,128]{2,1,0:T(8,128)S(1)}, u32[]{:S(2)}, u32[]{:S(2)}) collective-permute-start(f32[33,8,128]{2,1,0:T(8,128)S(1)} %get-tuple-element.12.sent), channel_id=1, source_target_pairs={{0,8},{1,9},{2,10},{3,11},{4,12},{5,13},{6,14},{7,15},{8,0},{9,1},... | collective-permute-start | bytes 405512 | tf_op jit(solution)/shard_map/ppermute | solution.py:218
  36.9 6.5 %collective-permute-done.8.got = f32[33,8,128]{2,1,0:T(8,128)S(1)} collective-permute-done((f32[33,8,128]{2,1,0:T(8,128)S(1)}, f32[33,8,128]{2,1,0:T(8,128)S(1)}, u32[]{:S(2)}, u32[]{:S(2)}) %collective-permute-start.8) | collective-permute-done | bytes 135200 | tf_op jit(solution)/shard_map/ppermute | solution.py:218
  43.4 0.8 %back.1 = f32[8,32,8,128]{3,2,1,0:T(8,128)S(1)} custom-call(s32[4]{0:T(128)S(1)} %pad_add_fusion.meta, f32[8,32,8,128]{3,2,1,0:T(8,128)S(1)} %get-tuple-element.9.f_in, f32[8,8,128]{2,1,0:T(8,128)S(1)} %get-tuple-element.10.cin, f32[2,8,128]{2,1,0:T(8,128)S(1)} %get-tuple-element.11.alpha, f32[33,8,128]{2,1,0:T(8,128)S(1)} %get-tuple-element.12.sent, ...), custom_call_target="tpu_custom_call" | custom-call | tf_op jit(solution)/shard_map/back/pallas_call | solution.py:221
  44.2 17.0 %all_to_all.10.got = f32[8,32,8,128]{3,2,1,0:T(8,128)S(1)} all-to-all(f32[8,32,8,128]{3,2,1,0:T(8,128)S(1)} %back.1), channel_id=1, replica_groups={{0,1,2,3,4,5,6,7},{8,9,10,11,12,13,14,15},{16,17,18,19,20,21,22,23},{24..., dimensions={0} | all-to-all | bytes 2097152 | tf_op jit(solution)/shard_map/all_to_all | solution.py:229
  61.2 1.1 %join.1 = f32[64,1,8,512]{3,2,1,0:T(8,128)} custom-call(f32[8,32,8,128]{3,2,1,0:T(8,128)S(1)} %all_to_all.10.got), custom_call_target="tpu_custom_call" | custom-call | tf_op jit(solution)/shard_map/join/pallas_call | solution.py:230
  (4 shorter events, 0.0 us)
Async XLA Ops:
  0.0 1.2 %copy-start = (f32[64,1,8,512]{3,2,1,0:T(8,128)S(1)}, f32[64,1,8,512]{3,2,1,0:T(8,128)}, u32[]{:S(2)}) copy-start(f32[64,1,8,512]{3,2,1,0:T(8,128)} %tracer.1) | copy-start | bytes 3145732
  1.2 0.7 %copy-start.1 = (f32[1,8,512]{2,1,0:T(8,128)S(1)}, f32[1,8,512]{2,1,0:T(8,128)}, u32[]{:S(2)}) copy-start(f32[1,8,512]{2,1,0:T(8,128)} %up.1) | copy-start | bytes 49156
  1.9 0.7 %copy-start.3 = (f32[1,8,512]{2,1,0:T(8,128)S(1)}, f32[1,8,512]{2,1,0:T(8,128)}, u32[]{:S(2)}) copy-start(f32[1,8,512]{2,1,0:T(8,128)} %diff.1) | copy-start | bytes 49156
  2.7 0.7 %copy-start.5 = (s32[8,512]{1,0:T(8,128)S(1)}, s32[8,512]{1,0:T(8,128)}, u32[]{:S(2)}) copy-start(s32[8,512]{1,0:T(8,128)} %kmt_all.1) | copy-start | bytes 49156
  3.4 0.7 %copy-start.7 = (f32[1,8,512]{2,1,0:T(8,128)S(1)}, f32[1,8,512]{2,1,0:T(8,128)}, u32[]{:S(2)}) copy-start(f32[1,8,512]{2,1,0:T(8,128)} %east.1) | copy-start | bytes 49156
  4.1 0.7 %copy-start.8 = (f32[1,8,512]{2,1,0:T(8,128)S(1)}, f32[1,8,512]{2,1,0:T(8,128)}, u32[]{:S(2)}) copy-start(f32[1,8,512]{2,1,0:T(8,128)} %north.1) | copy-start | bytes 49156
  6.5 5.4 %copy-start.2 = (f32[1,8,512]{2,1,0:T(8,128)S(1)}, f32[1,8,512]{2,1,0:T(8,128)}, u32[]{:S(2)}) copy-start(f32[1,8,512]{2,1,0:T(8,128)} %up.1) | copy-start | bytes 49156
  6.5 5.5 %copy-start.4 = (f32[1,8,512]{2,1,0:T(8,128)S(1)}, f32[1,8,512]{2,1,0:T(8,128)}, u32[]{:S(2)}) copy-start(f32[1,8,512]{2,1,0:T(8,128)} %diff.1) | copy-start | bytes 49156
  6.5 22.0 %copy-start.6 = (s32[8,512]{1,0:T(8,128)S(1)}, s32[8,512]{1,0:T(8,128)}, u32[]{:S(2)}) copy-start(s32[8,512]{1,0:T(8,128)} %kmt_all.1) | copy-start | bytes 49156
  6.5 22.0 %copy-start.9 = (f32[8,16]{1,0:T(8,128)S(1)}, f32[8,16]{1,0:T(8,128)}, u32[]{:S(2)}) copy-start(f32[8,16]{1,0:T(8,128)} %rates.1) | copy-start | bytes 1540
  6.5 22.0 %copy-start.10 = (f32[16]{0:T(128)S(1)}, f32[16]{0:T(128)}, u32[]{:S(2)}) copy-start(f32[16]{0:T(128)} %thickness.1) | copy-start | bytes 196
  6.5 22.0 %copy-start.11 = (s32[64]{0:T(128)S(1)}, s32[64]{0:T(128)}, u32[]{:S(2)}) copy-start(s32[64]{0:T(128)} %group.1) | copy-start | bytes 772
  6.5 22.0 %all-to-all-start = ((f32[8,37,8,128]{3,2,1,0:T(8,128)}), f32[8,37,8,128]{3,2,1,0:T(8,128)S(1)}, u32[]{:S(2)}, u32[]{:S(2)}) async-start(f32[8,37,8,128]{3,2,1,0:T(8,128)} %pack.1), calls=%async_computation | async-start | bytes 2424832 | tf_op jit(solution)/shard_map/all_to_all | solution.py:196
  12.0 4.0 %collective-permute-start.1 = (f32[2,8,128]{2,1,0:T(8,128)S(1)}, f32[2,8,128]{2,1,0:T(8,128)S(1)}, u32[]{:S(2)}, u32[]{:S(2)}) collective-permute-start(f32[2,8,128]{2,1,0:T(8,128)S(1)} %get-tuple-element.13), channel_id=1, source_target_pairs={{8,1},{24,17}} | collective-permute-start | bytes 24584 | tf_op jit(solution)/shard_map/ppermute | solution.py:202
  12.7 7.3 %collective-permute-start = (f32[2,8,128]{2,1,0:T(8,128)S(1)}, f32[2,8,128]{2,1,0:T(8,128)S(1)}, u32[]{:S(2)}, u32[]{:S(2)}) collective-permute-start(f32[2,8,128]{2,1,0:T(8,128)S(1)} %get-tuple-element.13), channel_id=1, source_target_pairs={{8,0},{24,16}} | collective-permute-start | bytes 24584 | tf_op jit(solution)/shard_map/ppermute | solution.py:202
  14.0 6.6 %collective-permute-start.7 = (f32[2,8,128]{2,1,0:T(8,128)S(1)}, f32[2,8,128]{2,1,0:T(8,128)S(1)}, u32[]{:S(2)}, u32[]{:S(2)}) collective-permute-start(f32[2,8,128]{2,1,0:T(8,128)S(1)} %get-tuple-element.14), channel_id=1, source_target_pairs={{8,7},{24,23}} | collective-permute-start | bytes 24584 | tf_op jit(solution)/shard_map/ppermute | solution.py:202
  14.6 6.7 %collective-permute-start.6 = (f32[2,8,128]{2,1,0:T(8,128)S(1)}, f32[2,8,128]{2,1,0:T(8,128)S(1)}, u32[]{:S(2)}, u32[]{:S(2)}) collective-permute-start(f32[2,8,128]{2,1,0:T(8,128)S(1)} %get-tuple-element.14), channel_id=1, source_target_pairs={{8,6},{24,22}} | collective-permute-start | bytes 24584 | tf_op jit(solution)/shard_map/ppermute | solution.py:202
  15.3 6.1 %collective-permute-start.5 = (f32[2,8,128]{2,1,0:T(8,128)S(1)}, f32[2,8,128]{2,1,0:T(8,128)S(1)}, u32[]{:S(2)}, u32[]{:S(2)}) collective-permute-start(f32[2,8,128]{2,1,0:T(8,128)S(1)} %get-tuple-element.15), channel_id=1, source_target_pairs={{8,5},{24,21}} | collective-permute-start | bytes 24584 | tf_op jit(solution)/shard_map/ppermute | solution.py:202
  16.0 5.3 %collective-permute-start.4 = (f32[2,8,128]{2,1,0:T(8,128)S(1)}, f32[2,8,128]{2,1,0:T(8,128)S(1)}, u32[]{:S(2)}, u32[]{:S(2)}) collective-permute-start(f32[2,8,128]{2,1,0:T(8,128)S(1)} %get-tuple-element.15), channel_id=1, source_target_pairs={{8,4},{24,20}} | collective-permute-start | bytes 24584 | tf_op jit(solution)/shard_map/ppermute | solution.py:202
  19.9 1.4 %collective-permute-start.3 = (f32[2,8,128]{2,1,0:T(8,128)S(1)}, f32[2,8,128]{2,1,0:T(8,128)S(1)}, u32[]{:S(2)}, u32[]{:S(2)}) collective-permute-start(f32[2,8,128]{2,1,0:T(8,128)S(1)} %get-tuple-element.16), channel_id=1, source_target_pairs={{8,3},{24,19}} | collective-permute-start | bytes 24584 | tf_op jit(solution)/shard_map/ppermute | solution.py:202
  20.6 0.8 %collective-permute-start.2 = (f32[2,8,128]{2,1,0:T(8,128)S(1)}, f32[2,8,128]{2,1,0:T(8,128)S(1)}, u32[]{:S(2)}, u32[]{:S(2)}) collective-permute-start(f32[2,8,128]{2,1,0:T(8,128)S(1)} %get-tuple-element.16), channel_id=1, source_target_pairs={{8,2},{24,18}} | collective-permute-start | bytes 24584 | tf_op jit(solution)/shard_map/ppermute | solution.py:202
  34.6 8.8 %collective-permute-start.8 = (f32[33,8,128]{2,1,0:T(8,128)S(1)}, f32[33,8,128]{2,1,0:T(8,128)S(1)}, u32[]{:S(2)}, u32[]{:S(2)}) collective-permute-start(f32[33,8,128]{2,1,0:T(8,128)S(1)} %get-tuple-element.12.sent), channel_id=1, source_target_pairs={{0,8},{1,9},{2,10},{3,11},{4,12},{5,13},{6,14},{7,15},{8,0},{9,1},... | collective-permute-start | bytes 405512 | tf_op jit(solution)/shard_map/ppermute | solution.py:218

commit v2 on v1

--- a/solution.py
+++ b/solution.py
@@ -22,40 +22,70 @@
     return lax.broadcasted_iota(jnp.int32, (ROWS, LANES), 0)
 
 
-def pack_kernel(nb, tc, tpc, meta, tracer, east, north, up, diff, kmt, out):
+def pack_kernel(
+    nb, tc, tpc, meta, tracer, east, north, up, diff, kmt, out, cells, fields, depth, extra, sem
+):
+    loads = [
+        pltpu.make_async_copy(kmt, depth, sem.at[0]),
+        pltpu.make_async_copy(east, fields.at[pl.ds(EAST, 1)], sem.at[1]),
+        pltpu.make_async_copy(north, fields.at[pl.ds(NORTH, 1)], sem.at[2]),
+        pltpu.make_async_copy(up, fields.at[pl.ds(UP, 1)], sem.at[3]),
+        pltpu.make_async_copy(diff, fields.at[pl.ds(DIFF, 1)], sem.at[4]),
+    ]
+    chunks = [
+        pltpu.make_async_copy(
+            tracer.at[pl.ds(c * tpc, tpc), 0], cells.at[pl.ds(c * tpc, tpc)], sem.at[5 + c]
+        )
+        for c in range(tc)
+    ]
+    for copy in loads + chunks:
+        copy.start()
+    for copy in loads:
+        copy.wait()
     level = meta[0]
     lane = lanes_iota()
-    wet = [
-        (level < kmt[:, b * LANES : (b + 1) * LANES]).astype(f32) for b in range(nb)
-    ]
+    cols = [slice(b * LANES, (b + 1) * LANES) for b in range(nb)]
+    wet = [(level < depth[:, cols[b]]).astype(f32) for b in range(nb)]
     flow = [None]
     for b in range(1, nb):
-        ends = east[0, :, b * LANES - LANES : b * LANES][:, LANES - 1 :]
+        ends = fields[EAST, :, cols[b - 1]][:, LANES - 1 :]
         ends = ends * wet[b - 1][:, LANES - 1 :] * wet[b][:, :1]
         flow.append(jnp.broadcast_to(ends, (ROWS, LANES)))
+    stores = []
     for c in range(tc):
+        chunks[c].wait()
+        for b in range(nb):
+            r = b * tc + c
+            copy = pltpu.make_async_copy(
+                cells.at[pl.ds(c * tpc, tpc), :, pl.ds(b * LANES, LANES)],
+                out.at[r, pl.ds(0, tpc)],
+                sem.at[5 + tc + 2 * r],
+            )
+            copy.start()
+            stores.append(copy)
         faces = [jnp.zeros((ROWS, LANES), f32) for _ in range(nb)]
         for t in range(tpc):
-            tiles = [tracer[c * tpc + t, 0, :, b * LANES : (b + 1) * LANES] for b in range(nb)]
-            for b in range(nb):
-                out[b * tc + c, t] = tiles[b]
             for b in range(1, nb):
-                west = pltpu.roll(tiles[b - 1], (2 * t + 1) % LANES, 1)
-                here = pltpu.roll(tiles[b], 2 * t, 1) if t else tiles[b]
+                west = pltpu.roll(cells[c * tpc + t, :, cols[b - 1]], (2 * t + 1) % LANES, 1)
+                here = cells[c * tpc + t, :, cols[b]]
+                here = pltpu.roll(here, 2 * t, 1) if t else here
                 face = jnp.maximum(flow[b], 0.0) * west + jnp.minimum(flow[b], 0.0) * here
                 faces[b] = jnp.where(lane == 2 * t, face, faces[b])
         for b in range(nb):
+            r = b * tc + c
             edge = faces[b]
             if b + 1 < nb:
                 edge = edge - pltpu.roll(faces[b + 1], LANES - 1, 1)
-            out[b * tc + c, tpc + EDGE] = edge
-    for b in range(nb):
-        cols = slice(b * LANES, (b + 1) * LANES)
-        for c in range(tc):
-            out[b * tc + c, tpc + EAST] = east[0, :, cols]
-            out[b * tc + c, tpc + NORTH] = north[0, :, cols]
-            out[b * tc + c, tpc + UP] = up[0, :, cols]
-            out[b * tc + c, tpc + DIFF] = diff[0, :, cols]
+            for i in range(4):
+                extra[r, i] = fields[i, :, cols[b]]
+            extra[r, EDGE] = edge
+            copy = pltpu.make_async_copy(
+                extra.at[r], out.at[r, pl.ds(tpc, EXTRA)], sem.at[6 + tc + 2 * r]
+            )
+            copy.start()
+            stores.append(copy)
+    for copy in stores:
+        copy.wait()
 
 
 def solve_kernel(
@@ -106,17 +136,15 @@
         north = jnp.where(row == ROWS - 1, 0.0, north)
         e_pos, e_neg = jnp.maximum(east, 0.0), jnp.minimum(east, 0.0)
         n_pos, n_neg = jnp.maximum(north, 0.0), jnp.minimum(north, 0.0)
+        mid = mid - e_pos - n_pos + pltpu.roll(e_neg, 1, 1) + pltpu.roll(n_neg, 1, 0)
+        e_pos, n_pos = pltpu.roll(e_pos, 1, 1), pltpu.roll(n_pos, 1, 0)
         edges = got[slot, tpc + EDGE]
         last = o + 1 == half
         prev_slot = slot_of(o - 1) if o else None
         next_slot = None if last else slot_of(o + 1)
         tout_next = -neg / dz_next
         outer_next = -g / dz_next
-
-        def body(t, _, o=o, k=k, slot=slot, wet=wet, mid=mid, tin=tin, tout=tout, outer=outer,
-                 alpha=alpha, e_pos=e_pos, e_neg=e_neg, n_pos=n_pos, n_neg=n_neg, edges=edges,
-                 last=last, prev_slot=prev_slot, next_slot=next_slot, tout_next=tout_next,
-                 outer_next=outer_next):
+        for t in range(tpc):
             c = got[slot, t]
             rate = rates[group[chunk * tpc + t], k]
             star = c * (mid - rate * wet)
@@ -124,20 +152,16 @@
                 star += tout * got[prev_slot, t]
             if not last:
                 star += tin * got[next_slot, t]
-            fe = e_pos * c + e_neg * pltpu.roll(c, LANES - 1, 1)
-            fn = n_pos * c + n_neg * pltpu.roll(c, ROWS - 1, 0)
-            star -= fe - pltpu.roll(fe, 1, 1)
-            star -= fn - pltpu.roll(fn, 1, 0)
-            star += jnp.where(ends, pltpu.roll(edges, (LANES - 2 * t) % LANES, 1), 0.0)
+            star += e_pos * pltpu.roll(c, 1, 1) - e_neg * pltpu.roll(c, LANES - 1, 1)
+            star += n_pos * pltpu.roll(c, 1, 0) - n_neg * pltpu.roll(c, ROWS - 1, 0)
+            edge = pltpu.roll(edges, LANES - 2 * t, 1) if t else edges
+            star += jnp.where(ends, edge, 0.0)
             if o:
                 star -= outer * f_out[o - 1, t]
             f = alpha * star
             f_out[o, t] = f
             if last:
                 message[t] = tout_next * c - outer_next * f
-            return 0
-
-        lax.fori_loop(0, tpc, body, 0, unroll=8)
         cin_out[o] = cin_new
         if last:
             alpha_out[0] = alpha
@@ -148,25 +172,34 @@
 
 def back_kernel(half, tpc, meta, f_in, cin, alpha, sent, got, out):
     upper = meta[0]
+    slots = [jnp.where(upper == 1, half - 1 - o, o) for o in range(half)]
     other = cin[half - 1] * got[tpc]
     scale = 1.0 / (1.0 - other * alpha[1])
     mine, theirs = scale * alpha[0], scale * other
-
-    def body(t, _):
+    for t in range(tpc):
         x = f_in[half - 1, t] + (mine * got[t] - theirs * sent[t])
-        out[jnp.where(upper == 1, 0, half - 1), t] = x
+        out[slots[half - 1], t] = x
         for o in range(half - 2, -1, -1):
             x = f_in[o, t] - cin[o] * x
-            out[jnp.where(upper == 1, half - 1 - o, o), t] = x
-        return 0
-
-    lax.fori_loop(0, tpc, body, 0, unroll=8)
-
-
-def join_kernel(nb, tc, tpc, got, out):
+            out[slots[o], t] = x
+
+
+def join_kernel(nb, tc, tpc, got, out, sem):
+    copies = []
     for b in range(nb):
         for c in range(tc):
-            out[c * tpc : (c + 1) * tpc, 0, :, b * LANES : (b + 1) * LANES] = got[b * tc + c]
+            r = b * tc + c
+            copies.append(
+                pltpu.make_async_copy(
+                    got.at[r],
+                    out.at[pl.ds(c * tpc, tpc), 0, :, pl.ds(b * LANES, LANES)],
+                    sem.at[r],
+                )
+            )
+    for copy in copies:
+        copy.start()
+    for copy in copies:
+        copy.wait()
 
 
 def shards(tracer, east_flow, north_flow, up_flow, diffusivity, thickness, kmt, group, group_rate):
@@ -182,14 +215,22 @@
     meta = jnp.stack([upper, rank // tc, rank % tc, index])
     vm = pl.BlockSpec(memory_space=pltpu.VMEM)
     sm = pl.BlockSpec(memory_space=pltpu.SMEM)
+    hbm = pl.BlockSpec(memory_space=pltpu.HBM)
     params = pltpu.CompilerParams(vmem_limit_bytes=VMEM_LIMIT)
     groups = [[h * half + i for i in range(half)] for h in range(2)]
 
     pieces = pl.pallas_call(
         functools.partial(pack_kernel, nb, tc, tpc),
         out_shape=jax.ShapeDtypeStruct((half, tpc + EXTRA, ROWS, LANES), f32),
-        in_specs=[sm] + [vm] * 6,
-        out_specs=vm,
+        in_specs=[sm] + [hbm] * 6,
+        out_specs=hbm,
+        scratch_shapes=[
+            pltpu.VMEM((ntr, ny, nx), f32),
+            pltpu.VMEM((4, ny, nx), f32),
+            pltpu.VMEM((ny, nx), jnp.int32),
+            pltpu.VMEM((half, EXTRA, ROWS, LANES), f32),
+            pltpu.SemaphoreType.DMA((5 + tc + 2 * half,)),
+        ],
         compiler_params=params,
         name="pack",
     )(index[None], tracer, east_flow, north_flow, up_flow, diffusivity, kmt)
@@ -231,7 +272,8 @@
         functools.partial(join_kernel, nb, tc, tpc),
         out_shape=jax.ShapeDtypeStruct(tracer.shape, f32),
         in_specs=[vm],
-        out_specs=vm,
+        out_specs=hbm,
+        scratch_shapes=[pltpu.SemaphoreType.DMA((half,))],
         compiler_params=params,
         name="join",
     )(back)

time: 63 us -> 58.8 us (0.933)
  Pallas kernels: 9.65 us -> 5.34 us
    pallas_call x1, Pallas kernels: 6.09 us -> 1.81 us  [shards(): pl.pallas_call(functools.partial(solve_kernel, half, tpc), out_shape=(jax...]
where the time goes in v2:
time: 58.8 us; the launch traced here: 58 us
  blocking collectives  17 us (29%)
  waiting for transfers between devices  16.8 us (29%)
  starting transfers between devices  13.6 us (23%)
  Pallas kernels  5.34 us (9%)
  local copies, waits for them, and re-layouts  4.86 us (8%)
    all_to_all x1, blocking collectives, shards(): lax.all_to_all(solved, 'lev', 0, 0, axis_index_groups=groups, tiled=True)  17 us
    all_to_all x1, waiting for transfers between devices, shards(): lax.all_to_all(pieces, 'lev', 0, 0, axis_index_groups=groups, tiled=True)  7.1 us
    ppermute x1, waiting for transfers between devices, shards(): lax.ppermute(message, 'lev', [(i, (i + half) % count) for i in range(coun...  6.47 us
    ppermute x8, starting transfers between devices, shards(): across = across + lax.ppermute(cols, 'lev', [(half, r)])  5.91 us
    all_to_all x1, starting transfers between devices, shards(): lax.all_to_all(pieces, 'lev', 0, 0, axis_index_groups=groups, tiled=True)  5.4 us
    unnamed x25, local copies, waits for them, and re-layouts  4.85 us
    ppermute x8, waiting for transfers between devices, shards(): across = across + lax.ppermute(cols, 'lev', [(half, r)])  3.26 us
    ppermute x1, starting transfers between devices, shards(): lax.ppermute(message, 'lev', [(i, (i + half) % count) for i in range(coun...  2.3 us
  transfers between devices with their start and end apart: 10, of which 3 were waited for; matrix products, arithmetic and copies ran while one was open for 0% of the time, Pallas kernels for 0%

profile of v2, /device:TPU:0, one launch (start us, length us, event | category | flops | bytes accessed | tf_op | source)
XLA Modules:
  0.0 58.0 jit_solution(18326960713352048165)
XLA Ops:
  0.0 0.0 copy-start
  0.0 1.2 %copy-done = f32[64,1,8,512]{3,2,1,0:T(8,128)S(1)} copy-done((f32[64,1,8,512]{3,2,1,0:T(8,128)S(1)}, f32[64,1,8,512]{3,2,1,0:T(8,128)}, u32[]{:S(2)}) %copy-start) | copy-done | bytes 1048600
  1.2 0.0 copy-start.1
  1.2 0.7 %copy-done.1 = f32[1,8,512]{2,1,0:T(8,128)S(1)} copy-done((f32[1,8,512]{2,1,0:T(8,128)S(1)}, f32[1,8,512]{2,1,0:T(8,128)}, u32[]{:S(2)}) %copy-start.1) | copy-done | bytes 16408
  1.9 0.0 copy-start.3
  1.9 0.7 %copy-done.3 = f32[1,8,512]{2,1,0:T(8,128)S(1)} copy-done((f32[1,8,512]{2,1,0:T(8,128)S(1)}, f32[1,8,512]{2,1,0:T(8,128)}, u32[]{:S(2)}) %copy-start.3) | copy-done | bytes 16408
  2.7 0.0 copy-start.5
  2.7 0.7 %copy-done.5 = s32[8,512]{1,0:T(8,128)S(1)} copy-done((s32[8,512]{1,0:T(8,128)S(1)}, s32[8,512]{1,0:T(8,128)}, u32[]{:S(2)}) %copy-start.5) | copy-done | bytes 16408
  3.4 0.0 copy-start.7
  3.4 0.7 %copy-done.7 = f32[1,8,512]{2,1,0:T(8,128)S(1)} copy-done((f32[1,8,512]{2,1,0:T(8,128)S(1)}, f32[1,8,512]{2,1,0:T(8,128)}, u32[]{:S(2)}) %copy-start.7) | copy-done | bytes 16408
  4.1 0.0 copy-start.8
  4.1 0.7 %copy-done.8 = f32[1,8,512]{2,1,0:T(8,128)S(1)} copy-done((f32[1,8,512]{2,1,0:T(8,128)S(1)}, f32[1,8,512]{2,1,0:T(8,128)}, u32[]{:S(2)}) %copy-start.8) | copy-done | bytes 16408
  4.8 1.8 %pack.1 = f32[8,37,8,128]{3,2,1,0:T(8,128)} custom-call(s32[1]{0:T(128)} %bitcast.3.meta, f32[64,1,8,512]{3,2,1,0:T(8,128)S(1)} %copy-done, f32[1,8,512]{2,1,0:T(8,128)S(1)} %copy-done.7, f32[1,8,512]{2,1,0:T(8,128)S(1)} %copy-done.8, f32[1,8,512]{2,1,0:T(8,128)S(1)} %copy-done.1, f32[1,8,512]{2,1,0:T(8,128)S(1)} %copy-done.3, s32[8,512]{1,0:T(8,128)S(1)} %copy-done.5), custom_call_target="tpu_custom_call" | custom-call | tf_op jit(solution)/shard_map/pack/pallas_call | solution.py:222
  6.6 0.0 copy-start.2
  6.7 0.0 copy-start.4
  6.7 0.0 copy-start.6
  6.7 0.0 copy-start.9
  6.7 0.0 copy-start.10
  6.7 0.0 copy-start.11
  6.7 5.4 %all-to-all-start = ((f32[8,37,8,128]{3,2,1,0:T(8,128)}), f32[8,37,8,128]{3,2,1,0:T(8,128)S(1)}, u32[]{:S(2)}, u32[]{:S(2)}) async-start(f32[8,37,8,128]{3,2,1,0:T(8,128)} %pack.1), calls=%async_computation | async-start | bytes 2424832 | tf_op jit(solution)/shard_map/all_to_all | solution.py:237
  12.1 0.0 copy-done.2
  12.1 0.0 copy-done.4
  12.2 0.7 %collective-permute-start.1 = (f32[2,8,128]{2,1,0:T(8,128)S(1)}, f32[2,8,128]{2,1,0:T(8,128)S(1)}, u32[]{:S(2)}, u32[]{:S(2)}) collective-permute-start(f32[2,8,128]{2,1,0:T(8,128)S(1)} %get-tuple-element.13), channel_id=1, source_target_pairs={{8,1},{24,17}} | collective-permute-start | bytes 24584 | tf_op jit(solution)/shard_map/ppermute | solution.py:243
  12.8 1.3 %collective-permute-start = (f32[2,8,128]{2,1,0:T(8,128)S(1)}, f32[2,8,128]{2,1,0:T(8,128)S(1)}, u32[]{:S(2)}, u32[]{:S(2)}) collective-permute-start(f32[2,8,128]{2,1,0:T(8,128)S(1)} %get-tuple-element.13), channel_id=1, source_target_pairs={{8,0},{24,16}} | collective-permute-start | bytes 24584 | tf_op jit(solution)/shard_map/ppermute | solution.py:243
  14.1 0.7 %collective-permute-start.7 = (f32[2,8,128]{2,1,0:T(8,128)S(1)}, f32[2,8,128]{2,1,0:T(8,128)S(1)}, u32[]{:S(2)}, u32[]{:S(2)}) collective-permute-start(f32[2,8,128]{2,1,0:T(8,128)S(1)} %get-tuple-element.14), channel_id=1, source_target_pairs={{8,7},{24,23}} | collective-permute-start | bytes 24584 | tf_op jit(solution)/shard_map/ppermute | solution.py:243
  14.8 0.7 %collective-permute-start.6 = (f32[2,8,128]{2,1,0:T(8,128)S(1)}, f32[2,8,128]{2,1,0:T(8,128)S(1)}, u32[]{:S(2)}, u32[]{:S(2)}) collective-permute-start(f32[2,8,128]{2,1,0:T(8,128)S(1)} %get-tuple-element.14), channel_id=1, source_target_pairs={{8,6},{24,22}} | collective-permute-start | bytes 24584 | tf_op jit(solution)/shard_map/ppermute | solution.py:243
  15.5 0.7 %collective-permute-start.5 = (f32[2,8,128]{2,1,0:T(8,128)S(1)}, f32[2,8,128]{2,1,0:T(8,128)S(1)}, u32[]{:S(2)}, u32[]{:S(2)}) collective-permute-start(f32[2,8,128]{2,1,0:T(8,128)S(1)} %get-tuple-element.15), channel_id=1, source_target_pairs={{8,5},{24,21}} | collective-permute-start | bytes 24584 | tf_op jit(solution)/shard_map/ppermute | solution.py:243
  16.2 0.0 collective-permute-done.1
  16.2 0.7 %collective-permute-start.4 = (f32[2,8,128]{2,1,0:T(8,128)S(1)}, f32[2,8,128]{2,1,0:T(8,128)S(1)}, u32[]{:S(2)}, u32[]{:S(2)}) collective-permute-start(f32[2,8,128]{2,1,0:T(8,128)S(1)} %get-tuple-element.15), channel_id=1, source_target_pairs={{8,4},{24,20}} | collective-permute-start | bytes 24584 | tf_op jit(solution)/shard_map/ppermute | solution.py:243
  16.9 3.2 %collective-permute-done = f32[2,8,128]{2,1,0:T(8,128)S(1)} collective-permute-done((f32[2,8,128]{2,1,0:T(8,128)S(1)}, f32[2,8,128]{2,1,0:T(8,128)S(1)}, u32[]{:S(2)}, u32[]{:S(2)}) %collective-permute-start) | collective-permute-done | bytes 8224 | tf_op jit(solution)/shard_map/ppermute | solution.py:243
  20.1 0.7 %collective-permute-start.3 = (f32[2,8,128]{2,1,0:T(8,128)S(1)}, f32[2,8,128]{2,1,0:T(8,128)S(1)}, u32[]{:S(2)}, u32[]{:S(2)}) collective-permute-start(f32[2,8,128]{2,1,0:T(8,128)S(1)} %get-tuple-element.16), channel_id=1, source_target_pairs={{8,3},{24,19}} | collective-permute-start | bytes 24584 | tf_op jit(solution)/shard_map/ppermute | solution.py:243
  20.8 0.0 collective-permute-done.7
  20.8 0.7 %collective-permute-start.2 = (f32[2,8,128]{2,1,0:T(8,128)S(1)}, f32[2,8,128]{2,1,0:T(8,128)S(1)}, u32[]{:S(2)}, u32[]{:S(2)}) collective-permute-start(f32[2,8,128]{2,1,0:T(8,128)S(1)} %get-tuple-element.16), channel_id=1, source_target_pairs={{8,2},{24,18}} | collective-permute-start | bytes 24584 | tf_op jit(solution)/shard_map/ppermute | solution.py:243
  21.4 0.1 pad_add_fusion.meta
  21.5 0.0 collective-permute-done.6
  21.5 0.0 collective-permute-done.5
  21.5 0.0 collective-permute-done.4
  21.5 0.0 collective-permute-done.3
  21.6 0.0 collective-permute-done.2
  21.6 7.1 %all-to-all-done.got = f32[8,37,8,128]{3,2,1,0:T(8,128)S(1)} async-done(((f32[8,37,8,128]{3,2,1,0:T(8,128)}), f32[8,37,8,128]{3,2,1,0:T(8,128)S(1)}, u32[]{:S(2)}, u32[]{:S(2)}) %all-to-all-start) | async-done | bytes 1212448 | tf_op jit(solution)/shard_map/all_to_all | solution.py:237
  28.7 0.0 copy-done.6
  28.7 0.0 copy-done.9
  28.7 0.0 copy-done.10
  28.7 0.0 copy-done.11
  28.7 1.8 %solve.1 = (f32[8,32,8,128]{3,2,1,0:T(8,128)S(1)}, f32[8,8,128]{2,1,0:T(8,128)S(1)}, f32[2,8,128]{2,1,0:T(8,128)S(1)}, f32[33,8,128]{2,1,0:T(8,128)S(1)}) custom-call(s32[4]{0:T(128)S(1)} %pad_add_fusion.meta, f32[16]{0:T(128)S(1)} %copy-done.10, s32[64]{0:T(128)S(1)} %copy-done.11, f32[8,16]{1,0:T(8,128)S(1)} %copy-done.9, ...), custom_call_target="tpu_custom_call" | custom-call | tf_op jit(solution)/shard_map/solve/pallas_call | solution.py:246
  30.5 2.3 %collective-permute-start.8 = (f32[33,8,128]{2,1,0:T(8,128)S(1)}, f32[33,8,128]{2,1,0:T(8,128)S(1)}, u32[]{:S(2)}, u32[]{:S(2)}) collective-permute-start(f32[33,8,128]{2,1,0:T(8,128)S(1)} %get-tuple-element.12.sent), channel_id=1, source_target_pairs={{0,8},{1,9},{2,10},{3,11},{4,12},{5,13},{6,14},{7,15},{8,0},{9,1},... | collective-permute-start | bytes 405512 | tf_op jit(solution)/shard_map/ppermute | solution.py:259
  32.8 6.5 %collective-permute-done.8.got = f32[33,8,128]{2,1,0:T(8,128)S(1)} collective-permute-done((f32[33,8,128]{2,1,0:T(8,128)S(1)}, f32[33,8,128]{2,1,0:T(8,128)S(1)}, u32[]{:S(2)}, u32[]{:S(2)}) %collective-permute-start.8) | collective-permute-done | bytes 135200 | tf_op jit(solution)/shard_map/ppermute | solution.py:259
  39.3 0.7 %back.1 = f32[8,32,8,128]{3,2,1,0:T(8,128)S(1)} custom-call(s32[4]{0:T(128)S(1)} %pad_add_fusion.meta, f32[8,32,8,128]{3,2,1,0:T(8,128)S(1)} %get-tuple-element.9.f_in, f32[8,8,128]{2,1,0:T(8,128)S(1)} %get-tuple-element.10.cin, f32[2,8,128]{2,1,0:T(8,128)S(1)} %get-tuple-element.11.alpha, f32[33,8,128]{2,1,0:T(8,128)S(1)} %get-tuple-element.12.sent, ...), custom_call_target="tpu_custom_call" | custom-call | tf_op jit(solution)/shard_map/back/pallas_call | solution.py:262
  40.0 17.0 %all_to_all.10.got = f32[8,32,8,128]{3,2,1,0:T(8,128)S(1)} all-to-all(f32[8,32,8,128]{3,2,1,0:T(8,128)S(1)} %back.1), channel_id=1, replica_groups={{0,1,2,3,4,5,6,7},{8,9,10,11,12,13,14,15},{16,17,18,19,20,21,22,23},{24..., dimensions={0} | all-to-all | bytes 2097152 | tf_op jit(solution)/shard_map/all_to_all | solution.py:270
  57.0 1.0 %join.1 = f32[64,1,8,512]{3,2,1,0:T(8,128)} custom-call(f32[8,32,8,128]{3,2,1,0:T(8,128)S(1)} %all_to_all.10.got), custom_call_target="tpu_custom_call" | custom-call | tf_op jit(solution)/shard_map/join/pallas_call | solution.py:271
  (4 shorter events, 0.0 us)
Async XLA Ops:
  0.0 1.2 %copy-start = (f32[64,1,8,512]{3,2,1,0:T(8,128)S(1)}, f32[64,1,8,512]{3,2,1,0:T(8,128)}, u32[]{:S(2)}) copy-start(f32[64,1,8,512]{3,2,1,0:T(8,128)} %tracer.1) | copy-start | bytes 3145732
  1.2 0.7 %copy-start.1 = (f32[1,8,512]{2,1,0:T(8,128)S(1)}, f32[1,8,512]{2,1,0:T(8,128)}, u32[]{:S(2)}) copy-start(f32[1,8,512]{2,1,0:T(8,128)} %up.1) | copy-start | bytes 49156
  1.9 0.7 %copy-start.3 = (f32[1,8,512]{2,1,0:T(8,128)S(1)}, f32[1,8,512]{2,1,0:T(8,128)}, u32[]{:S(2)}) copy-start(f32[1,8,512]{2,1,0:T(8,128)} %diff.1) | copy-start | bytes 49156
  2.7 0.7 %copy-start.5 = (s32[8,512]{1,0:T(8,128)S(1)}, s32[8,512]{1,0:T(8,128)}, u32[]{:S(2)}) copy-start(s32[8,512]{1,0:T(8,128)} %kmt_all.1) | copy-start | bytes 49156
  3.4 0.7 %copy-start.7 = (f32[1,8,512]{2,1,0:T(8,128)S(1)}, f32[1,8,512]{2,1,0:T(8,128)}, u32[]{:S(2)}) copy-start(f32[1,8,512]{2,1,0:T(8,128)} %east.1) | copy-start | bytes 49156
  4.1 0.7 %copy-start.8 = (f32[1,8,512]{2,1,0:T(8,128)S(1)}, f32[1,8,512]{2,1,0:T(8,128)}, u32[]{:S(2)}) copy-start(f32[1,8,512]{2,1,0:T(8,128)} %north.1) | copy-start | bytes 49156
  6.6 5.5 %copy-start.2 = (f32[1,8,512]{2,1,0:T(8,128)S(1)}, f32[1,8,512]{2,1,0:T(8,128)}, u32[]{:S(2)}) copy-start(f32[1,8,512]{2,1,0:T(8,128)} %up.1) | copy-start | bytes 49156
  6.7 5.5 %copy-start.4 = (f32[1,8,512]{2,1,0:T(8,128)S(1)}, f32[1,8,512]{2,1,0:T(8,128)}, u32[]{:S(2)}) copy-start(f32[1,8,512]{2,1,0:T(8,128)} %diff.1) | copy-start | bytes 49156
  6.7 22.0 %copy-start.6 = (s32[8,512]{1,0:T(8,128)S(1)}, s32[8,512]{1,0:T(8,128)}, u32[]{:S(2)}) copy-start(s32[8,512]{1,0:T(8,128)} %kmt_all.1) | copy-start | bytes 49156
  6.7 22.0 %copy-start.9 = (f32[8,16]{1,0:T(8,128)S(1)}, f32[8,16]{1,0:T(8,128)}, u32[]{:S(2)}) copy-start(f32[8,16]{1,0:T(8,128)} %rates.1) | copy-start | bytes 1540
  6.7 22.0 %copy-start.10 = (f32[16]{0:T(128)S(1)}, f32[16]{0:T(128)}, u32[]{:S(2)}) copy-start(f32[16]{0:T(128)} %thickness.1) | copy-start | bytes 196
  6.7 22.0 %copy-start.11 = (s32[64]{0:T(128)S(1)}, s32[64]{0:T(128)}, u32[]{:S(2)}) copy-start(s32[64]{0:T(128)} %group.1) | copy-start | bytes 772
  6.7 22.0 %all-to-all-start = ((f32[8,37,8,128]{3,2,1,0:T(8,128)}), f32[8,37,8,128]{3,2,1,0:T(8,128)S(1)}, u32[]{:S(2)}, u32[]{:S(2)}) async-start(f32[8,37,8,128]{3,2,1,0:T(8,128)} %pack.1), calls=%async_computation | async-start | bytes 2424832 | tf_op jit(solution)/shard_map/all_to_all | solution.py:237
  12.2 4.0 %collective-permute-start.1 = (f32[2,8,128]{2,1,0:T(8,128)S(1)}, f32[2,8,128]{2,1,0:T(8,128)S(1)}, u32[]{:S(2)}, u32[]{:S(2)}) collective-permute-start(f32[2,8,128]{2,1,0:T(8,128)S(1)} %get-tuple-element.13), channel_id=1, source_target_pairs={{8,1},{24,17}} | collective-permute-start | bytes 24584 | tf_op jit(solution)/shard_map/ppermute | solution.py:243
  12.8 7.3 %collective-permute-start = (f32[2,8,128]{2,1,0:T(8,128)S(1)}, f32[2,8,128]{2,1,0:T(8,128)S(1)}, u32[]{:S(2)}, u32[]{:S(2)}) collective-permute-start(f32[2,8,128]{2,1,0:T(8,128)S(1)} %get-tuple-element.13), channel_id=1, source_target_pairs={{8,0},{24,16}} | collective-permute-start | bytes 24584 | tf_op jit(solution)/shard_map/ppermute | solution.py:243
  14.1 6.6 %collective-permute-start.7 = (f32[2,8,128]{2,1,0:T(8,128)S(1)}, f32[2,8,128]{2,1,0:T(8,128)S(1)}, u32[]{:S(2)}, u32[]{:S(2)}) collective-permute-start(f32[2,8,128]{2,1,0:T(8,128)S(1)} %get-tuple-element.14), channel_id=1, source_target_pairs={{8,7},{24,23}} | collective-permute-start | bytes 24584 | tf_op jit(solution)/shard_map/ppermute | solution.py:243
  14.8 6.7 %collective-permute-start.6 = (f32[2,8,128]{2,1,0:T(8,128)S(1)}, f32[2,8,128]{2,1,0:T(8,128)S(1)}, u32[]{:S(2)}, u32[]{:S(2)}) collective-permute-start(f32[2,8,128]{2,1,0:T(8,128)S(1)} %get-tuple-element.14), channel_id=1, source_target_pairs={{8,6},{24,22}} | collective-permute-start | bytes 24584 | tf_op jit(solution)/shard_map/ppermute | solution.py:243
  15.5 6.1 %collective-permute-start.5 = (f32[2,8,128]{2,1,0:T(8,128)S(1)}, f32[2,8,128]{2,1,0:T(8,128)S(1)}, u32[]{:S(2)}, u32[]{:S(2)}) collective-permute-start(f32[2,8,128]{2,1,0:T(8,128)S(1)} %get-tuple-element.15), channel_id=1, source_target_pairs={{8,5},{24,21}} | collective-permute-start | bytes 24584 | tf_op jit(solution)/shard_map/ppermute | solution.py:243
  16.2 5.3 %collective-permute-start.4 = (f32[2,8,128]{2,1,0:T(8,128)S(1)}, f32[2,8,128]{2,1,0:T(8,128)S(1)}, u32[]{:S(2)}, u32[]{:S(2)}) collective-permute-start(f32[2,8,128]{2,1,0:T(8,128)S(1)} %get-tuple-element.15), channel_id=1, source_target_pairs={{8,4},{24,20}} | collective-permute-start | bytes 24584 | tf_op jit(solution)/shard_map/ppermute | solution.py:243
  20.1 1.4 %collective-permute-start.3 = (f32[2,8,128]{2,1,0:T(8,128)S(1)}, f32[2,8,128]{2,1,0:T(8,128)S(1)}, u32[]{:S(2)}, u32[]{:S(2)}) collective-permute-start(f32[2,8,128]{2,1,0:T(8,128)S(1)} %get-tuple-element.16), channel_id=1, source_target_pairs={{8,3},{24,19}} | collective-permute-start | bytes 24584 | tf_op jit(solution)/shard_map/ppermute | solution.py:243
  20.8 0.8 %collective-permute-start.2 = (f32[2,8,128]{2,1,0:T(8,128)S(1)}, f32[2,8,128]{2,1,0:T(8,128)S(1)}, u32[]{:S(2)}, u32[]{:S(2)}) collective-permute-start(f32[2,8,128]{2,1,0:T(8,128)S(1)} %get-tuple-element.16), channel_id=1, source_target_pairs={{8,2},{24,18}} | collective-permute-start | bytes 24584 | tf_op jit(solution)/shard_map/ppermute | solution.py:243
  30.5 8.8 %collective-permute-start.8 = (f32[33,8,128]{2,1,0:T(8,128)S(1)}, f32[33,8,128]{2,1,0:T(8,128)S(1)}, u32[]{:S(2)}, u32[]{:S(2)}) collective-permute-start(f32[33,8,128]{2,1,0:T(8,128)S(1)} %get-tuple-element.12.sent), channel_id=1, source_target_pairs={{0,8},{1,9},{2,10},{3,11},{4,12},{5,13},{6,14},{7,15},{8,0},{9,1},... | collective-permute-start | bytes 405512 | tf_op jit(solution)/shard_map/ppermute | solution.py:259

commit v3 on v2

v3 whole, which is shorter than its diff:
```python
import functools

import jax
import jax.numpy as jnp
from jax import lax
from jax.experimental import pallas as pl
from jax.experimental.pallas import tpu as pltpu
from jax.sharding import PartitionSpec as P

LANES = 128
ROWS = 8
EAST, NORTH, UP, DIFF, EDGE, EXTRA = 0, 1, 2, 3, 4, 5
f32 = jnp.float32
VMEM_LIMIT = 16 * 1024 * 1024
PACK_LIMIT = 60 * 1024 * 1024


def lanes_iota():
    return lax.broadcasted_iota(jnp.int32, (ROWS, LANES), 1)


def rows_iota():
    return lax.broadcasted_iota(jnp.int32, (ROWS, LANES), 0)


def start_order(half):
    far, near = half // 2, half // 4
    kind = lambda d: -((d & far) > 0) - ((d & near) > 0)
    return sorted(range(1, half), key=lambda d: (d < 2, kind(d), d & 1, -d)) + [0]


def place(index, nb, tc):
    half = nb * tc
    rank = lax.rem(index, half)
    return lax.div(index, half), rank, lax.div(rank, tc), lax.rem(rank, tc)


def pack_kernel(nb, tc, tpc, index, tracer, east, north, up, diff, kmt, *refs):
    half = nb * tc
    out, (cells, fields, depth, extra, sem) = refs[:half], refs[half:]
    _, rank, _, _ = place(index[0], nb, tc)
    loads = [
        pltpu.make_async_copy(kmt, depth, sem.at[0]),
        pltpu.make_async_copy(east, fields.at[pl.ds(EAST, 1)], sem.at[1]),
        pltpu.make_async_copy(north, fields.at[pl.ds(NORTH, 1)], sem.at[2]),
        pltpu.make_async_copy(up, fields.at[pl.ds(UP, 1)], sem.at[3]),
        pltpu.make_async_copy(diff, fields.at[pl.ds(DIFF, 1)], sem.at[4]),
    ]
    chunks = [
        pltpu.make_async_copy(
            tracer.at[pl.ds(c * tpc, tpc), 0], cells.at[pl.ds(c * tpc, tpc)], sem.at[5 + c]
        )
        for c in range(tc)
    ]
    for copy in chunks + loads:
        copy.start()
    for copy in chunks:
        copy.wait()
    stores = []
    for i, d in enumerate(start_order(half)):
        r = rank ^ d
        cut = pl.ds(pl.multiple_of(lax.div(r, tc) * LANES, LANES), LANES)
        copy = pltpu.make_async_copy(
            cells.at[pl.ds(lax.rem(r, tc) * tpc, tpc), :, cut],
            out[d].at[pl.ds(0, tpc)],
            sem.at[5 + tc + i],
        )
        copy.start()
        stores.append(copy)
    for copy in loads:
        copy.wait()
    lane = lanes_iota()
    cols = [slice(b * LANES, (b + 1) * LANES) for b in range(nb)]
    wet = [(index[0] < depth[:, cols[b]]).astype(f32) for b in range(nb)]
    flow = [None]
    for b in range(1, nb):
        ends = fields[EAST, :, cols[b - 1]][:, LANES - 1 :]
        ends = ends * wet[b - 1][:, LANES - 1 :] * wet[b][:, :1]
        flow.append(jnp.broadcast_to(ends, (ROWS, LANES)))
    for c in range(tc):
        faces = [jnp.zeros((ROWS, LANES), f32) for _ in range(nb)]
        for t in range(tpc):
            for b in range(1, nb):
                west = pltpu.roll(cells[c * tpc + t, :, cols[b - 1]], (2 * t + 1) % LANES, 1)
                here = cells[c * tpc + t, :, cols[b]]
                here = pltpu.roll(here, 2 * t, 1) if t else here
                face = jnp.maximum(flow[b], 0.0) * west + jnp.minimum(flow[b], 0.0) * here
                faces[b] = jnp.where(lane == 2 * t, face, faces[b])
        for b in range(nb):
            edge = faces[b]
            if b + 1 < nb:
                edge = edge - pltpu.roll(faces[b + 1], LANES - 1, 1)
            for i in range(4):
                extra[b * tc + c, i] = fields[i, :, cols[b]]
            extra[b * tc + c, EDGE] = edge
    for d in range(half):
        copy = pltpu.make_async_copy(
            extra.at[rank ^ d], out[d].at[pl.ds(tpc, EXTRA)], sem.at[5 + tc + half + d]
        )
        copy.start()
        stores.append(copy)
    for copy in stores:
        copy.wait()


def keep_kernel(piece, own, sem):
    copy = pltpu.make_async_copy(piece, own, sem.at[0])
    copy.start()
    copy.wait()


def pick_kernel(nb, tc, tpc, index, *refs):
    arrived, out = refs[:-1], refs[-1]
    _, rank, _, _ = place(index[0], nb, tc)
    for i in range(2):
        field = arrived[0][tpc + UP + i]
        for d, piece in zip(start_order(nb * tc)[1:], arrived[1:]):
            field = jnp.where(rank == d, piece[tpc + UP + i], field)
        out[i] = field


def solve_kernel(nb, tc, tpc, index, thickness, group, rates, kmt_all, *refs):
    half = nb * tc
    arrived, (f_out, cin_out, base_out, cells_out, got) = refs[:half], refs[half:]
    upper, rank, block, chunk = place(index[0], nb, tc)
    for d, piece in zip(start_order(half), arrived):
        for t in range(tpc + EXTRA):
            got[rank ^ d, t] = piece[t]
    sign = 1.0 - 2.0 * upper.astype(f32)
    kmt = kmt_all[:, pl.ds(pl.multiple_of(block * LANES, LANES), LANES)]
    lane, row = lanes_iota(), rows_iota()
    ends = jnp.logical_or(lane == 0, lane == LANES - 1)
    first = jnp.where(upper == 1, 2 * half - 1, 0)
    step = 1 - 2 * upper

    def level_of(o):
        return first + step * o

    def slot_of(o):
        return jnp.where(upper == 1, half - 1 - o, o)

    zero = jnp.zeros((ROWS, LANES), f32)
    cin = tout = outer = add_mid = zero
    for o in range(half):
        k = level_of(o)
        slot = slot_of(o)
        dz, dz_next = thickness[k], thickness[level_of(o + 1)]
        wet = (k < kmt).astype(f32)
        wet_next = (level_of(o + 1) < kmt).astype(f32)
        last = o + 1 == half
        mid = wet + add_mid
        denom = 1.0 - outer - outer * cin
        if not last:
            face = jnp.where(upper == 1, slot, slot_of(o + 1))
            pos, neg, g = interface(
                got[face, tpc + UP], got[face, tpc + DIFF], sign, wet * wet_next, dz, dz_next
            )
            mid = mid + neg / dz
            tin = pos / dz
            inner = -g / dz
            alpha = 1.0 / (denom - inner)
        east = got[slot, tpc + EAST] * wet * pltpu.roll(wet, LANES - 1, 1)
        east = jnp.where(lane == LANES - 1, 0.0, east)
        north = got[slot, tpc + NORTH] * wet * pltpu.roll(wet, ROWS - 1, 0)
        north = jnp.where(row == ROWS - 1, 0.0, north)
        e_pos, e_neg = jnp.maximum(east, 0.0), jnp.minimum(east, 0.0)
        n_pos, n_neg = jnp.maximum(north, 0.0), jnp.minimum(north, 0.0)
        mid = mid - e_pos - n_pos + pltpu.roll(e_neg, 1, 1) + pltpu.roll(n_neg, 1, 0)
        e_pos, n_pos = pltpu.roll(e_pos, 1, 1), pltpu.roll(n_pos, 1, 0)
        edges = got[slot, tpc + EDGE]
        prev_slot = slot_of(o - 1) if o else None
        next_slot = None if last else slot_of(o + 1)
        for t in range(tpc):
            c = got[slot, t]
            rate = rates[group[chunk * tpc + t], k]
            star = c * (mid - rate * wet)
            if o:
                star += tout * got[prev_slot, t]
            if not last:
                star += tin * got[next_slot, t]
            star += e_pos * pltpu.roll(c, 1, 1) - e_neg * pltpu.roll(c, LANES - 1, 1)
            star += n_pos * pltpu.roll(c, 1, 0) - n_neg * pltpu.roll(c, ROWS - 1, 0)
            edge = pltpu.roll(edges, LANES - 2 * t, 1) if t else edges
            star += jnp.where(ends, edge, 0.0)
            if o:
                star -= outer * f_out[o - 1, t]
            f_out[o, t] = star if last else alpha * star
            if last:
                cells_out[t] = c
        if last:
            base_out[0] = denom
            base_out[1] = wet * wet_next
        else:
            cin = inner * alpha
            cin_out[o] = cin
            tout, outer, add_mid = -neg / dz_next, -g / dz_next, -pos / dz_next


def interface(w, g, sign, open_face, dz, dz_next):
    w = sign * w * open_face
    dz_min = jnp.minimum(dz, dz_next)
    g = g * open_face / (0.5 * (dz + dz_next))
    return dz_min * jnp.maximum(w, 0.0), dz_min * jnp.minimum(w, 0.0), g


def seam_kernel(nb, tc, tpc, index, thickness, star, cells, base, own, other, f_out, coef_out, message):
    half = nb * tc
    upper, _, _, _ = place(index[0], nb, tc)
    sign = 1.0 - 2.0 * upper.astype(f32)
    dz = thickness[half - 1 + upper]
    dz_next = thickness[half - upper]
    w = jnp.where(upper == 1, own[0], other[0])
    g = jnp.where(upper == 1, own[1], other[1])
    pos, neg, g = interface(w, g, sign, base[1], dz, dz_next)
    inner, outer_next = -g / dz, -g / dz_next
    mid, tout_next = neg / dz, -neg / dz_next
    alpha = 1.0 / (base[0] - inner)
    for t in range(tpc):
        c = cells[t]
        f = alpha * (star[half - 1, t] + mid * c)
        f_out[t] = f
        message[t] = tout_next * c - outer_next * f
    coef_out[0] = inner * alpha
    coef_out[1] = alpha
    coef_out[2] = outer_next
    message[tpc] = alpha


def back_kernel(nb, tc, tpc, index, f_in, cin, f_last, coef, sent, got, *refs):
    half = nb * tc
    out, (solved,) = refs[:half], refs[half:]
    upper, rank, _, _ = place(index[0], nb, tc)
    slots = [jnp.where(upper == 1, half - 1 - o, o) for o in range(half)]
    other = coef[0] * got[tpc]
    scale = 1.0 / (1.0 - other * coef[2])
    mine, theirs = scale * coef[1], scale * other
    for t in range(tpc):
        x = f_last[t] + (mine * got[t] - theirs * sent[t])
        solved[slots[half - 1], t] = x
        for o in range(half - 2, -1, -1):
            x = f_in[o, t] - cin[o] * x
            solved[slots[o], t] = x
    for d in range(half):
        for t in range(tpc):
            out[d][t] = solved[rank ^ d, t]


def join_kernel(nb, tc, tpc, index, *refs):
    arrived, out, sem = refs[:-2], refs[-2], refs[-1]
    copies = []
    _, rank, _, _ = place(index[0], nb, tc)
    for d, piece in zip(start_order(len(arrived)), arrived):
        r = rank ^ d
        cols = pl.ds(pl.multiple_of(lax.div(r, tc) * LANES, LANES), LANES)
        copies.append(
            pltpu.make_async_copy(
                piece, out.at[pl.ds(lax.rem(r, tc) * tpc, tpc), 0, :, cols], sem.at[d]
            )
        )
    for copy in copies:
        copy.start()
    for copy in copies:
        copy.wait()


def shards(tracer, east_flow, north_flow, up_flow, diffusivity, thickness, kmt, group, group_rate):
    ntr, ldev, ny, nx = tracer.shape
    count = lax.axis_size("lev")
    half = count // 2
    nb = nx // LANES
    tc = half // nb
    tpc = ntr // tc
    assert ldev == 1 and ny == ROWS and nb * LANES == nx and tc * nb == half and tpc * tc == ntr
    index = lax.axis_index("lev").astype(jnp.int32)[None]
    tile = (ROWS, LANES)
    vm = pl.BlockSpec(memory_space=pltpu.VMEM)
    sm = pl.BlockSpec(memory_space=pltpu.SMEM)
    hbm = pl.BlockSpec(memory_space=pltpu.HBM)
    anywhere = pl.BlockSpec(memory_space=pl.ANY)
    params = pltpu.CompilerParams(vmem_limit_bytes=VMEM_LIMIT)

    def flip(value, bits):
        return lax.ppermute(value, "lev", [(i, i ^ bits) for i in range(count)])

    pieces = pl.pallas_call(
        functools.partial(pack_kernel, nb, tc, tpc),
        out_shape=(jax.ShapeDtypeStruct((tpc + EXTRA,) + tile, f32),) * half,
        in_specs=[sm] + [hbm] * 6,
        out_specs=(hbm,) * half,
        scratch_shapes=[
            pltpu.VMEM((ntr, ny, nx), f32),
            pltpu.VMEM((4, ny, nx), f32),
            pltpu.VMEM((ny, nx), jnp.int32),
            pltpu.VMEM((half, EXTRA) + tile, f32),
            pltpu.SemaphoreType.DMA((5 + tc + 2 * half,)),
        ],
        compiler_params=pltpu.CompilerParams(vmem_limit_bytes=PACK_LIMIT),
        name="pack",
    )(index, tracer, east_flow, north_flow, up_flow, diffusivity, kmt)
    order = start_order(half)

    def exchange(values):
        return [flip(values[d], d) if d else values[d] for d in order]

    arrived = exchange(pieces)
    arrived[-1] = pl.pallas_call(
        keep_kernel,
        out_shape=jax.ShapeDtypeStruct((tpc + EXTRA,) + tile, f32),
        in_specs=[anywhere],
        out_specs=vm,
        scratch_shapes=[pltpu.SemaphoreType.DMA((1,))],
        compiler_params=params,
        name="keep",
    )(arrived[-1])
    own = pl.pallas_call(
        functools.partial(pick_kernel, nb, tc, tpc),
        out_shape=jax.ShapeDtypeStruct((2,) + tile, f32),
        in_specs=[sm] + [vm] * half,
        out_specs=vm,
        compiler_params=params,
        name="pick",
    )(index, *arrived)
    other = flip(own, half)
    f, cin, base, cells = pl.pallas_call(
        functools.partial(solve_kernel, nb, tc, tpc),
        out_shape=(
            jax.ShapeDtypeStruct((half, tpc) + tile, f32),
            jax.ShapeDtypeStruct((half - 1,) + tile, f32),
            jax.ShapeDtypeStruct((2,) + tile, f32),
            jax.ShapeDtypeStruct((tpc,) + tile, f32),
        ),
        in_specs=[sm, sm, sm, sm, vm] + [vm] * half,
        out_specs=(vm, vm, vm, vm),
        scratch_shapes=[pltpu.VMEM((half, tpc + EXTRA) + tile, f32)],
        compiler_params=params,
        name="solve",
    )(index, thickness, group, group_rate, kmt, *arrived)
    f_last, coef, message = pl.pallas_call(
        functools.partial(seam_kernel, nb, tc, tpc),
        out_shape=(
            jax.ShapeDtypeStruct((tpc,) + tile, f32),
            jax.ShapeDtypeStruct((3,) + tile, f32),
            jax.ShapeDtypeStruct((tpc + 1,) + tile, f32),
        ),
        in_specs=[sm, sm, vm, vm, vm, vm, vm],
        out_specs=(vm, vm, vm),
        compiler_params=params,
        name="seam",
    )(index, thickness, f, cells, base, own, other)
    theirs = flip(message, half)
    solved = pl.pallas_call(
        functools.partial(back_kernel, nb, tc, tpc),
        out_shape=(jax.ShapeDtypeStruct((tpc,) + tile, f32),) * half,
        in_specs=[sm, vm, vm, vm, vm, vm, vm],
        out_specs=(vm,) * half,
        scratch_shapes=[pltpu.VMEM((half, tpc) + tile, f32)],
        compiler_params=params,
        name="back",
    )(index, f, cin, f_last, coef, message, theirs)
    back = exchange(solved)
    return pl.pallas_call(
        functools.partial(join_kernel, nb, tc, tpc),
        out_shape=jax.ShapeDtypeStruct(tracer.shape, f32),
        in_specs=[sm] + [anywhere] * half,
        out_specs=hbm,
        scratch_shapes=[pltpu.SemaphoreType.DMA((half,))],
        compiler_params=params,
        name="join",
    )(index, *back)


def solution(mesh):
    placed = (
        P(None, "lev", "band", None),
        P("lev", "band", None),
        P("lev", "band", None),
        P("lev", "band", None),
        P("lev", "band", None),
        P(),
        P("band", None),
        P(),
        P(),
    )
    return jax.shard_map(
        shards, mesh=mesh, in_specs=placed, out_specs=P(None, "lev", "band", None), check_vma=False
    )
```

time: 58.8 us -> 50.8 us (0.86)
  blocking collectives: 17 us -> 0 us
  starting transfers between devices: 13.6 us -> 20.5 us
  waiting for transfers between devices: 16.8 us -> 22.5 us
  local copies, waits for them, and re-layouts: 4.86 us -> 0.94 us
  Pallas kernels: 5.34 us -> 6.58 us
    all_to_all x1 -> x0, blocking collectives: 17 us -> none  [shards(): lax.all_to_all(solved, 'lev', 0, 0, axis_index_groups=groups, tiled=True)]
    ppermute x9 -> x16, waiting for transfers between devices: 9.73 us -> 22.5 us  [flip(): return lax.ppermute(value, 'lev', [(i, i ^ bits) for i in range(count)])]
    ppermute x9 -> x16, starting transfers between devices: 8.21 us -> 20.5 us  [flip(): return lax.ppermute(value, 'lev', [(i, i ^ bits) for i in range(count)])]
    all_to_all x1 -> x0, waiting for transfers between devices: 7.1 us -> none  [shards(): lax.all_to_all(pieces, 'lev', 0, 0, axis_index_groups=groups, tiled=True)]
    all_to_all x1 -> x0, starting transfers between devices: 5.4 us -> none  [shards(): lax.all_to_all(pieces, 'lev', 0, 0, axis_index_groups=groups, tiled=True)]
    unnamed x25 -> x10, local copies, waits for them, and re-layouts: 4.85 us -> 0.94 us
    pallas_call x3 -> x6, Pallas kernels: 4.31 us -> 5.55 us  [the longest x1 2.67 us: shards(): pl.pallas_call(functools.partial(pack_kernel, nb, tc, tpc), out_shape=(ja...]
  transfers between devices with their start and end apart: 10 -> 16, of which waited for: 3 -> 10; matrix products, arithmetic and copies ran while one was open for 0% -> 0% of each run, Pallas kernels for 0% -> 4%
where the time goes in v3:
time: 50.8 us; the launch traced here: 50.6 us
  waiting for transfers between devices  22.5 us (44%)
  starting transfers between devices  20.5 us (40%)
  Pallas kernels  6.58 us (13%)
  local copies, waits for them, and re-layouts  0.94 us (2%)
    ppermute x16, waiting for transfers between devices, flip(): return lax.ppermute(value, 'lev', [(i, i ^ bits) for i in range(count)])  22.5 us
    ppermute x16, starting transfers between devices, flip(): return lax.ppermute(value, 'lev', [(i, i ^ bits) for i in range(count)])  20.5 us
    pallas_call x1, Pallas kernels, shards(): pl.pallas_call(functools.partial(pack_kernel, nb, tc, tpc), out_shape=(ja...  2.67 us
    pallas_call x1, Pallas kernels, shards(): pl.pallas_call(functools.partial(solve_kernel, nb, tc, tpc), out_shape=(j...  1.89 us
    pallas_call x1, Pallas kernels, shards(): pl.pallas_call(functools.partial(join_kernel, nb, tc, tpc), out_shape=jax...  1.02 us
  transfers between devices with their start and end apart: 16, of which 10 were waited for; matrix products, arithmetic and copies ran while one was open for 0% of the time, Pallas kernels for 4%

profile of v3, /device:TPU:0, one launch (start us, length us, event | category | flops | bytes accessed | tf_op | source)
XLA Modules:
  0.0 50.6 jit_solution(2761500315714697661)
XLA Ops:
  0.0 2.7 %pack.1 = (f32[37,8,128]{2,1,0:T(8,128)}, f32[37,8,128]{2,1,0:T(8,128)}, f32[37,8,128]{2,1,0:T(8,128)}, f32[37,8,128]{2,1,0:T(8,128)}, f32[37,8,128]{2,1,0:T(8,1...) custom-call(s32[1]{0:T(128)} %bitcast.index, f32[64,1,8,512]{3,2,1,0:T(8,128)} %tracer.1, ...), custom_call_target="tpu_custom_call" | custom-call | tf_op jit(solution)/shard_map/pack/pallas_call | solution.py:285
  2.7 4.0 %collective-permute-start = (f32[37,8,128]{2,1,0:T(8,128)}, f32[37,8,128]{2,1,0:T(8,128)S(1)}, u32[]{:S(2)}, u32[]{:S(2)}) collective-permute-start(f32[37,8,128]{2,1,0:T(8,128)} %get-tuple-element.28), channel_id=1, source_target_pairs={{0,6},{1,7},{2,4},{3,5},{4,2},{5,3},{6,0},{7,1},{8,14},{9,15},{10,... | collective-permute-start | bytes 454664 | tf_op jit(solution)/shard_map/ppermute | solution.py:283
  6.7 0.0 collective-permute-start.1
  6.7 1.1 %collective-permute-start.2 = (f32[37,8,128]{2,1,0:T(8,128)}, f32[37,8,128]{2,1,0:T(8,128)S(1)}, u32[]{:S(2)}, u32[]{:S(2)}) collective-permute-start(f32[37,8,128]{2,1,0:T(8,128)} %get-tuple-element.30), channel_id=1, source_target_pairs={{0,4},{1,5},{2,6},{3,7},{4,0},{5,1},{6,2},{7,3},{8,12},{9,13},{10,... | collective-permute-start | bytes 454664 | tf_op jit(solution)/shard_map/ppermute | solution.py:283
  7.9 1.5 %collective-permute-start.3 = (f32[37,8,128]{2,1,0:T(8,128)}, f32[37,8,128]{2,1,0:T(8,128)S(1)}, u32[]{:S(2)}, u32[]{:S(2)}) collective-permute-start(f32[37,8,128]{2,1,0:T(8,128)} %get-tuple-element.31), channel_id=1, source_target_pairs={{0,2},{1,3},{2,0},{3,1},{4,6},{5,7},{6,4},{7,5},{8,10},{9,11},{10,... | collective-permute-start | bytes 454664 | tf_op jit(solution)/shard_map/ppermute | solution.py:283
  9.4 0.5 collective-permute-start.4
  9.9 1.6 %collective-permute-done.refs_0_ = f32[37,8,128]{2,1,0:T(8,128)S(1)} collective-permute-done((f32[37,8,128]{2,1,0:T(8,128)}, f32[37,8,128]{2,1,0:T(8,128)S(1)}, u32[]{:S(2)}, u32[]{:S(2)}) %collective-permute-start) | collective-permute-done | bytes 151584 | tf_op jit(solution)/shard_map/ppermute | solution.py:283
  11.4 0.0 collective-permute-start.5
  11.4 3.2 %collective-permute-done.1.refs_1_ = f32[37,8,128]{2,1,0:T(8,128)S(1)} collective-permute-done((f32[37,8,128]{2,1,0:T(8,128)}, f32[37,8,128]{2,1,0:T(8,128)S(1)}, u32[]{:S(2)}, u32[]{:S(2)}) %collective-permute-start.1) | collective-permute-done | bytes 151584 | tf_op jit(solution)/shard_map/ppermute | solution.py:283
  14.7 0.0 collective-permute-start.6
  14.7 0.0 copy-start
  14.7 0.9 %copy-done = f32[37,8,128]{2,1,0:T(8,128)S(1)} copy-done((f32[37,8,128]{2,1,0:T(8,128)S(1)}, f32[37,8,128]{2,1,0:T(8,128)}, u32[]{:S(2)}) %copy-start) | copy-done | bytes 151576
  15.6 0.2 keep.1.refs_7_
  15.8 0.0 copy-start.1
  15.8 0.0 copy-start.2
  15.8 0.0 copy-start.3
  15.8 0.0 copy-start.4
  15.8 2.9 %collective-permute-done.2.refs_2_ = f32[37,8,128]{2,1,0:T(8,128)S(1)} collective-permute-done((f32[37,8,128]{2,1,0:T(8,128)}, f32[37,8,128]{2,1,0:T(8,128)S(1)}, u32[]{:S(2)}, u32[]{:S(2)}) %collective-permute-start.2) | collective-permute-done | bytes 151584 | tf_op jit(solution)/shard_map/ppermute | solution.py:283
  18.7 0.0 collective-permute-done.3.refs_3_
  18.7 1.3 %collective-permute-done.4.refs_4_ = f32[37,8,128]{2,1,0:T(8,128)S(1)} collective-permute-done((f32[37,8,128]{2,1,0:T(8,128)}, f32[37,8,128]{2,1,0:T(8,128)S(1)}, u32[]{:S(2)}, u32[]{:S(2)}) %collective-permute-start.4) | collective-permute-done | bytes 151584 | tf_op jit(solution)/shard_map/ppermute | solution.py:283
  20.0 0.6 %collective-permute-done.5.refs_5_ = f32[37,8,128]{2,1,0:T(8,128)S(1)} collective-permute-done((f32[37,8,128]{2,1,0:T(8,128)}, f32[37,8,128]{2,1,0:T(8,128)S(1)}, u32[]{:S(2)}, u32[]{:S(2)}) %collective-permute-start.5) | collective-permute-done | bytes 151584 | tf_op jit(solution)/shard_map/ppermute | solution.py:283
  20.6 0.0 collective-permute-done.6.refs_6_
  20.6 2.8 %collective-permute-start.7 = (f32[2,8,128]{2,1,0:T(8,128)S(1)}, f32[2,8,128]{2,1,0:T(8,128)S(1)}, u32[]{:S(2)}, u32[]{:S(2)}) collective-permute-start(f32[2,8,128]{2,1,0:T(8,128)S(1)} %pick.1.own), channel_id=1, source_target_pairs={{0,8},{1,9},{2,10},{3,11},{4,12},{5,13},{6,14},{7,15},{8,0},{9,1},... | collective-permute-start | bytes 24584 | tf_op jit(solution)/shard_map/ppermute | solution.py:283
  23.4 0.0 copy-done.1
  23.4 0.0 copy-done.2
  23.4 0.0 copy-done.3
  23.4 0.0 copy-done.4
  23.4 1.9 %solve.1 = (f32[8,32,8,128]{3,2,1,0:T(8,128)S(1)}, f32[7,8,128]{2,1,0:T(8,128)S(1)}, f32[2,8,128]{2,1,0:T(8,128)S(1)}, f32[32,8,128]{2,1,0:T(8,128)S(1)}) custom-call(s32[1]{0:T(128)} %bitcast.index, f32[16]{0:T(128)S(1)} %copy-done.3, s32[64]{0:T(128)S(1)} %copy-done.4, f32[8,16]{1,0:T(8,128)S(1)} %copy-done.2, s32[8,512]{1,0:T(8,128)S(1)} %copy-done.1, ...), custom_call_target="tpu_custom_call" | custom-call | tf_op jit(solution)/shard_map/solve/pallas_call | solution.py:324
  25.3 0.0 collective-permute-done.7.other
  25.3 0.6 %seam.1 = (f32[32,8,128]{2,1,0:T(8,128)S(1)}, f32[3,8,128]{2,1,0:T(8,128)S(1)}, f32[33,8,128]{2,1,0:T(8,128)S(1)}) custom-call(s32[1]{0:T(128)} %bitcast.index, f32[16]{0:T(128)S(1)} %copy-done.3, f32[8,32,8,128]{3,2,1,0:T(8,128)S(1)} %get-tuple-element.36.star.f_in, f32[32,8,128]{2,1,0:T(8,128)S(1)} %get-tuple-element.38.cells, ...), custom_call_target="tpu_custom_call" | custom-call | tf_op jit(solution)/shard_map/seam/pallas_call | solution.py:338
  25.9 2.7 %collective-permute-start.8 = (f32[33,8,128]{2,1,0:T(8,128)S(1)}, f32[33,8,128]{2,1,0:T(8,128)S(1)}, u32[]{:S(2)}, u32[]{:S(2)}) collective-permute-start(f32[33,8,128]{2,1,0:T(8,128)S(1)} %get-tuple-element.42.sent), channel_id=1, source_target_pairs={{0,8},{1,9},{2,10},{3,11},{4,12},{5,13},{6,14},{7,15},{8,0},{9,1},... | collective-permute-start | bytes 405512 | tf_op jit(solution)/shard_map/ppermute | solution.py:283
  28.6 6.5 %collective-permute-done.8.got = f32[33,8,128]{2,1,0:T(8,128)S(1)} collective-permute-done((f32[33,8,128]{2,1,0:T(8,128)S(1)}, f32[33,8,128]{2,1,0:T(8,128)S(1)}, u32[]{:S(2)}, u32[]{:S(2)}) %collective-permute-start.8) | collective-permute-done | bytes 135200 | tf_op jit(solution)/shard_map/ppermute | solution.py:283
  35.1 0.2 back.1
  35.3 0.9 %collective-permute-start.9 = (f32[32,8,128]{2,1,0:T(8,128)S(1)}, f32[32,8,128]{2,1,0:T(8,128)S(1)}, u32[]{:S(2)}, u32[]{:S(2)}) collective-permute-start(f32[32,8,128]{2,1,0:T(8,128)S(1)} %get-tuple-element.43), channel_id=1, source_target_pairs={{0,6},{1,7},{2,4},{3,5},{4,2},{5,3},{6,0},{7,1},{8,14},{9,15},{10,... | collective-permute-start | bytes 393224 | tf_op jit(solution)/shard_map/ppermute | solution.py:283
  36.2 0.5 collective-permute-start.10
  36.6 1.7 %collective-permute-start.11 = (f32[32,8,128]{2,1,0:T(8,128)S(1)}, f32[32,8,128]{2,1,0:T(8,128)S(1)}, u32[]{:S(2)}, u32[]{:S(2)}) collective-permute-start(f32[32,8,128]{2,1,0:T(8,128)S(1)} %get-tuple-element.45), channel_id=1, source_target_pairs={{0,4},{1,5},{2,6},{3,7},{4,0},{5,1},{6,2},{7,3},{8,12},{9,13},{10,... | collective-permute-start | bytes 393224 | tf_op jit(solution)/shard_map/ppermute | solution.py:283
  38.3 0.5 %collective-permute-start.12 = (f32[32,8,128]{2,1,0:T(8,128)S(1)}, f32[32,8,128]{2,1,0:T(8,128)S(1)}, u32[]{:S(2)}, u32[]{:S(2)}) collective-permute-start(f32[32,8,128]{2,1,0:T(8,128)S(1)} %get-tuple-element.46), channel_id=1, source_target_pairs={{0,2},{1,3},{2,0},{3,1},{4,6},{5,7},{6,4},{7,5},{8,10},{9,11},{10,... | collective-permute-start | bytes 393224 | tf_op jit(solution)/shard_map/ppermute | solution.py:283
  38.9 2.1 %collective-permute-start.13 = (f32[32,8,128]{2,1,0:T(8,128)S(1)}, f32[32,8,128]{2,1,0:T(8,128)S(1)}, u32[]{:S(2)}, u32[]{:S(2)}) collective-permute-start(f32[32,8,128]{2,1,0:T(8,128)S(1)} %get-tuple-element.47), channel_id=1, source_target_pairs={{0,5},{1,4},{2,7},{3,6},{4,1},{5,0},{6,3},{7,2},{8,13},{9,12},{10,... | collective-permute-start | bytes 393224 | tf_op jit(solution)/shard_map/ppermute | solution.py:283
  41.0 1.5 %collective-permute-done.9.refs_0_ = f32[32,8,128]{2,1,0:T(8,128)S(1)} collective-permute-done((f32[32,8,128]{2,1,0:T(8,128)S(1)}, f32[32,8,128]{2,1,0:T(8,128)S(1)}, u32[]{:S(2)}, u32[]{:S(2)}) %collective-permute-start.9) | collective-permute-done | bytes 131104 | tf_op jit(solution)/shard_map/ppermute | solution.py:283
  42.5 0.0 collective-permute-start.14
  42.5 0.4 collective-permute-done.10.refs_1_
  42.9 2.1 %collective-permute-start.15 = (f32[32,8,128]{2,1,0:T(8,128)S(1)}, f32[32,8,128]{2,1,0:T(8,128)S(1)}, u32[]{:S(2)}, u32[]{:S(2)}) collective-permute-start(f32[32,8,128]{2,1,0:T(8,128)S(1)} %get-tuple-element.49), channel_id=1, source_target_pairs={{0,1},{1,0},{2,3},{3,2},{4,5},{5,4},{6,7},{7,6},{8,9},{9,8},{10,11... | collective-permute-start | bytes 393224 | tf_op jit(solution)/shard_map/ppermute | solution.py:283
  45.1 2.7 %collective-permute-done.11.refs_2_ = f32[32,8,128]{2,1,0:T(8,128)S(1)} collective-permute-done((f32[32,8,128]{2,1,0:T(8,128)S(1)}, f32[32,8,128]{2,1,0:T(8,128)S(1)}, u32[]{:S(2)}, u32[]{:S(2)}) %collective-permute-start.11) | collective-permute-done | bytes 131104 | tf_op jit(solution)/shard_map/ppermute | solution.py:283
  47.8 0.0 collective-permute-done.12.refs_3_
  47.8 0.0 collective-permute-done.13.refs_4_
  47.8 1.8 %collective-permute-done.14.refs_5_ = f32[32,8,128]{2,1,0:T(8,128)S(1)} collective-permute-done((f32[32,8,128]{2,1,0:T(8,128)S(1)}, f32[32,8,128]{2,1,0:T(8,128)S(1)}, u32[]{:S(2)}, u32[]{:S(2)}) %collective-permute-start.14) | collective-permute-done | bytes 131104 | tf_op jit(solution)/shard_map/ppermute | solution.py:283
  49.6 0.0 collective-permute-done.15.refs_6_
  49.6 1.0 %join.1 = f32[64,1,8,512]{3,2,1,0:T(8,128)} custom-call(s32[1]{0:T(128)} %bitcast.index, f32[32,8,128]{2,1,0:T(8,128)S(1)} %collective-permute-done.9.refs_0_, f32[32,8,128]{2,1,0:T(8,128)S(1)} %collective-permute-done.10.refs_1_, f32[32,8,128]{2,1,0:T(8,128)S(1)} %collective-permute-done.11.refs_2_, f32[32,8,128]{2,1,0:T(8,128)S(1)} %collective-permute-done.12.refs_3_, ...), custom_call_target="tpu_custom_call" | custom-call | tf_op jit(solution)/shard_map/join/pallas_call | solution.py:361
  (1 shorter events, 0.0 us)
Async XLA Ops:
  2.7 8.7 %collective-permute-start = (f32[37,8,128]{2,1,0:T(8,128)}, f32[37,8,128]{2,1,0:T(8,128)S(1)}, u32[]{:S(2)}, u32[]{:S(2)}) collective-permute-start(f32[37,8,128]{2,1,0:T(8,128)} %get-tuple-element.28), channel_id=1, source_target_pairs={{0,6},{1,7},{2,4},{3,5},{4,2},{5,3},{6,0},{7,1},{8,14},{9,15},{10,... | collective-permute-start | bytes 454664 | tf_op jit(solution)/shard_map/ppermute | solution.py:283
  6.7 7.9 %collective-permute-start.1 = (f32[37,8,128]{2,1,0:T(8,128)}, f32[37,8,128]{2,1,0:T(8,128)S(1)}, u32[]{:S(2)}, u32[]{:S(2)}) collective-permute-start(f32[37,8,128]{2,1,0:T(8,128)} %get-tuple-element.29), channel_id=1, source_target_pairs={{0,7},{1,6},{2,5},{3,4},{4,3},{5,2},{6,1},{7,0},{8,15},{9,14},{10,... | collective-permute-start | bytes 454664 | tf_op jit(solution)/shard_map/ppermute | solution.py:283
  6.7 12.0 %collective-permute-start.2 = (f32[37,8,128]{2,1,0:T(8,128)}, f32[37,8,128]{2,1,0:T(8,128)S(1)}, u32[]{:S(2)}, u32[]{:S(2)}) collective-permute-start(f32[37,8,128]{2,1,0:T(8,128)} %get-tuple-element.30), channel_id=1, source_target_pairs={{0,4},{1,5},{2,6},{3,7},{4,0},{5,1},{6,2},{7,3},{8,12},{9,13},{10,... | collective-permute-start | bytes 454664 | tf_op jit(solution)/shard_map/ppermute | solution.py:283
  7.9 10.9 %collective-permute-start.3 = (f32[37,8,128]{2,1,0:T(8,128)}, f32[37,8,128]{2,1,0:T(8,128)S(1)}, u32[]{:S(2)}, u32[]{:S(2)}) collective-permute-start(f32[37,8,128]{2,1,0:T(8,128)} %get-tuple-element.31), channel_id=1, source_target_pairs={{0,2},{1,3},{2,0},{3,1},{4,6},{5,7},{6,4},{7,5},{8,10},{9,11},{10,... | collective-permute-start | bytes 454664 | tf_op jit(solution)/shard_map/ppermute | solution.py:283
  9.4 10.6 %collective-permute-start.4 = (f32[37,8,128]{2,1,0:T(8,128)}, f32[37,8,128]{2,1,0:T(8,128)S(1)}, u32[]{:S(2)}, u32[]{:S(2)}) collective-permute-start(f32[37,8,128]{2,1,0:T(8,128)} %get-tuple-element.32), channel_id=1, source_target_pairs={{0,5},{1,4},{2,7},{3,6},{4,1},{5,0},{6,3},{7,2},{8,13},{9,12},{10,... | collective-permute-start | bytes 454664 | tf_op jit(solution)/shard_map/ppermute | solution.py:283
  11.4 9.2 %collective-permute-start.5 = (f32[37,8,128]{2,1,0:T(8,128)}, f32[37,8,128]{2,1,0:T(8,128)S(1)}, u32[]{:S(2)}, u32[]{:S(2)}) collective-permute-start(f32[37,8,128]{2,1,0:T(8,128)} %get-tuple-element.33), channel_id=1, source_target_pairs={{0,3},{1,2},{2,1},{3,0},{4,7},{5,6},{6,5},{7,4},{8,11},{9,10},{10,... | collective-permute-start | bytes 454664 | tf_op jit(solution)/shard_map/ppermute | solution.py:283
  14.7 5.9 %collective-permute-start.6 = (f32[37,8,128]{2,1,0:T(8,128)}, f32[37,8,128]{2,1,0:T(8,128)S(1)}, u32[]{:S(2)}, u32[]{:S(2)}) collective-permute-start(f32[37,8,128]{2,1,0:T(8,128)} %get-tuple-element.34), channel_id=1, source_target_pairs={{0,1},{1,0},{2,3},{3,2},{4,5},{5,4},{6,7},{7,6},{8,9},{9,8},{10,11... | collective-permute-start | bytes 454664 | tf_op jit(solution)/shard_map/ppermute | solution.py:283
  14.7 0.9 %copy-start = (f32[37,8,128]{2,1,0:T(8,128)S(1)}, f32[37,8,128]{2,1,0:T(8,128)}, u32[]{:S(2)}) copy-start(f32[37,8,128]{2,1,0:T(8,128)} %get-tuple-element.35.piece) | copy-start | bytes 454660
  15.8 7.6 %copy-start.1 = (s32[8,512]{1,0:T(8,128)S(1)}, s32[8,512]{1,0:T(8,128)}, u32[]{:S(2)}) copy-start(s32[8,512]{1,0:T(8,128)} %kmt_all.1) | copy-start | bytes 49156
  15.8 7.6 %copy-start.2 = (f32[8,16]{1,0:T(8,128)S(1)}, f32[8,16]{1,0:T(8,128)}, u32[]{:S(2)}) copy-start(f32[8,16]{1,0:T(8,128)} %rates.1) | copy-start | bytes 1540
  15.8 7.6 %copy-start.3 = (f32[16]{0:T(128)S(1)}, f32[16]{0:T(128)}, u32[]{:S(2)}) copy-start(f32[16]{0:T(128)} %thickness.3) | copy-start | bytes 196
  15.8 7.6 %copy-start.4 = (s32[64]{0:T(128)S(1)}, s32[64]{0:T(128)}, u32[]{:S(2)}) copy-start(s32[64]{0:T(128)} %group.1) | copy-start | bytes 772
  20.6 4.7 %collective-permute-start.7 = (f32[2,8,128]{2,1,0:T(8,128)S(1)}, f32[2,8,128]{2,1,0:T(8,128)S(1)}, u32[]{:S(2)}, u32[]{:S(2)}) collective-permute-start(f32[2,8,128]{2,1,0:T(8,128)S(1)} %pick.1.own), channel_id=1, source_target_pairs={{0,8},{1,9},{2,10},{3,11},{4,12},{5,13},{6,14},{7,15},{8,0},{9,1},... | collective-permute-start | bytes 24584 | tf_op jit(solution)/shard_map/ppermute | solution.py:283
  25.9 9.2 %collective-permute-start.8 = (f32[33,8,128]{2,1,0:T(8,128)S(1)}, f32[33,8,128]{2,1,0:T(8,128)S(1)}, u32[]{:S(2)}, u32[]{:S(2)}) collective-permute-start(f32[33,8,128]{2,1,0:T(8,128)S(1)} %get-tuple-element.42.sent), channel_id=1, source_target_pairs={{0,8},{1,9},{2,10},{3,11},{4,12},{5,13},{6,14},{7,15},{8,0},{9,1},... | collective-permute-start | bytes 405512 | tf_op jit(solution)/shard_map/ppermute | solution.py:283
  35.3 7.2 %collective-permute-start.9 = (f32[32,8,128]{2,1,0:T(8,128)S(1)}, f32[32,8,128]{2,1,0:T(8,128)S(1)}, u32[]{:S(2)}, u32[]{:S(2)}) collective-permute-start(f32[32,8,128]{2,1,0:T(8,128)S(1)} %get-tuple-element.43), channel_id=1, source_target_pairs={{0,6},{1,7},{2,4},{3,5},{4,2},{5,3},{6,0},{7,1},{8,14},{9,15},{10,... | collective-permute-start | bytes 393224 | tf_op jit(solution)/shard_map/ppermute | solution.py:283
  36.2 6.8 %collective-permute-start.10 = (f32[32,8,128]{2,1,0:T(8,128)S(1)}, f32[32,8,128]{2,1,0:T(8,128)S(1)}, u32[]{:S(2)}, u32[]{:S(2)}) collective-permute-start(f32[32,8,128]{2,1,0:T(8,128)S(1)} %get-tuple-element.44), channel_id=1, source_target_pairs={{0,7},{1,6},{2,5},{3,4},{4,3},{5,2},{6,1},{7,0},{8,15},{9,14},{10,... | collective-permute-start | bytes 393224 | tf_op jit(solution)/shard_map/ppermute | solution.py:283
  36.6 11.2 %collective-permute-start.11 = (f32[32,8,128]{2,1,0:T(8,128)S(1)}, f32[32,8,128]{2,1,0:T(8,128)S(1)}, u32[]{:S(2)}, u32[]{:S(2)}) collective-permute-start(f32[32,8,128]{2,1,0:T(8,128)S(1)} %get-tuple-element.45), channel_id=1, source_target_pairs={{0,4},{1,5},{2,6},{3,7},{4,0},{5,1},{6,2},{7,3},{8,12},{9,13},{10,... | collective-permute-start | bytes 393224 | tf_op jit(solution)/shard_map/ppermute | solution.py:283
  38.3 9.5 %collective-permute-start.12 = (f32[32,8,128]{2,1,0:T(8,128)S(1)}, f32[32,8,128]{2,1,0:T(8,128)S(1)}, u32[]{:S(2)}, u32[]{:S(2)}) collective-permute-start(f32[32,8,128]{2,1,0:T(8,128)S(1)} %get-tuple-element.46), channel_id=1, source_target_pairs={{0,2},{1,3},{2,0},{3,1},{4,6},{5,7},{6,4},{7,5},{8,10},{9,11},{10,... | collective-permute-start | bytes 393224 | tf_op jit(solution)/shard_map/ppermute | solution.py:283
  38.9 9.0 %collective-permute-start.13 = (f32[32,8,128]{2,1,0:T(8,128)S(1)}, f32[32,8,128]{2,1,0:T(8,128)S(1)}, u32[]{:S(2)}, u32[]{:S(2)}) collective-permute-start(f32[32,8,128]{2,1,0:T(8,128)S(1)} %get-tuple-element.47), channel_id=1, source_target_pairs={{0,5},{1,4},{2,7},{3,6},{4,1},{5,0},{6,3},{7,2},{8,13},{9,12},{10,... | collective-permute-start | bytes 393224 | tf_op jit(solution)/shard_map/ppermute | solution.py:283
  42.5 7.1 %collective-permute-start.14 = (f32[32,8,128]{2,1,0:T(8,128)S(1)}, f32[32,8,128]{2,1,0:T(8,128)S(1)}, u32[]{:S(2)}, u32[]{:S(2)}) collective-permute-start(f32[32,8,128]{2,1,0:T(8,128)S(1)} %get-tuple-element.48), channel_id=1, source_target_pairs={{0,3},{1,2},{2,1},{3,0},{4,7},{5,6},{6,5},{7,4},{8,11},{9,10},{10,... | collective-permute-start | bytes 393224 | tf_op jit(solution)/shard_map/ppermute | solution.py:283
  42.9 6.6 %collective-permute-start.15 = (f32[32,8,128]{2,1,0:T(8,128)S(1)}, f32[32,8,128]{2,1,0:T(8,128)S(1)}, u32[]{:S(2)}, u32[]{:S(2)}) collective-permute-start(f32[32,8,128]{2,1,0:T(8,128)S(1)} %get-tuple-element.49), channel_id=1, source_target_pairs={{0,1},{1,0},{2,3},{3,2},{4,5},{5,4},{6,7},{7,6},{8,9},{9,8},{10,11... | collective-permute-start | bytes 393224 | tf_op jit(solution)/shard_map/ppermute | solution.py:283

commit v4 on v3

v4 whole, which is shorter than its diff:
```python
import functools

import jax
import jax.numpy as jnp
from jax import lax
from jax.experimental import pallas as pl
from jax.experimental.pallas import tpu as pltpu
from jax.sharding import PartitionSpec as P

LANES = 128
ROWS = 8
THERE, HOME = "none", "none"
WAIT = 1
EAST, NORTH, UP, DIFF, EDGE, EXTRA = 0, 1, 2, 3, 4, 5
f32 = jnp.float32
VMEM_LIMIT = 16 * 1024 * 1024
PACK_LIMIT = 60 * 1024 * 1024


def lanes_iota():
    return lax.broadcasted_iota(jnp.int32, (ROWS, LANES), 1)


def rows_iota():
    return lax.broadcasted_iota(jnp.int32, (ROWS, LANES), 0)


def devices(half):
    far, near = half // 2, half // 4
    crossed = lambda d: ((d & far) > 0) + ((d & near) > 0)
    return sorted(range(1, half), key=lambda d: (d < 2, d & 1, -crossed(d), -d)) + [0]


def pairing(half, which):
    if which == "none":
        return ()
    far = half // 2 | half // 4
    return tuple(d for d in range(2, half, 2) if which == "all" or d & far == far)


def sends(half, paired):
    order = [(d, d in paired) for d in devices(half) if d > 1 and (d % 2 == 0 or d - 1 not in paired)]
    return order + [(0, True)] if paired else order + [(1, False), (0, False)]


def by_level(half, paired, refs, rank):
    order = sends(half, paired)
    direct = [(rank ^ d, refs[j].at[0] if both else refs[j]) for j, (d, both) in enumerate(order)]
    swapped = [d ^ 1 for d, both in order if both]
    return direct + [(rank ^ d, refs[len(order)].at[j]) for j, d in enumerate(swapped)]


def n_arrived(half, paired):
    return len(sends(half, paired)) + (1 if paired else 0)


def place(nb, tc):
    half = nb * tc
    index = lax.axis_index("lev")
    rank = lax.rem(index, half)
    return lax.div(index, half), rank, lax.div(rank, tc), lax.rem(rank, tc)


def pack_kernel(nb, tc, tpc, paired, tracer, east, north, up, diff, kmt, *refs):
    half = nb * tc
    _, rank, _, _ = place(nb, tc)
    order = sends(half, paired)
    out = {}
    for j, (d, both) in enumerate(order):
        if both:
            out[d], out[d ^ 1] = refs[j].at[0], refs[j].at[1]
        else:
            out[d] = refs[j]
    cells, fields, depth, extra, sem, store_sem = refs[len(order) :]
    loads = [
        pltpu.make_async_copy(kmt, depth, sem.at[0]),
        pltpu.make_async_copy(east, fields.at[pl.ds(EAST, 1)], sem.at[1]),
        pltpu.make_async_copy(north, fields.at[pl.ds(NORTH, 1)], sem.at[2]),
        pltpu.make_async_copy(up, fields.at[pl.ds(UP, 1)], sem.at[3]),
        pltpu.make_async_copy(diff, fields.at[pl.ds(DIFF, 1)], sem.at[4]),
    ]
    chunks = [
        pltpu.make_async_copy(
            tracer.at[pl.ds(c * tpc, tpc), 0], cells.at[pl.ds(c * tpc, tpc)], sem.at[5 + c]
        )
        for c in range(tc)
    ]
    for copy in chunks + loads:
        copy.start()
    for copy in chunks:
        copy.wait()
    stores = []
    for d in devices(half):
        r = rank ^ d
        cut = pl.ds(pl.multiple_of(lax.div(r, tc) * LANES, LANES), LANES)
        copy = pltpu.make_async_copy(
            cells.at[pl.ds(lax.rem(r, tc) * tpc, tpc), :, cut], out[d].at[pl.ds(0, tpc)], store_sem.at[0, d]
        )
        copy.start()
        stores.append(copy)
    for copy in loads:
        copy.wait()
    lane = lanes_iota()
    cols = [slice(b * LANES, (b + 1) * LANES) for b in range(nb)]
    wet = [(lax.axis_index("lev") < depth[:, cols[b]]).astype(f32) for b in range(nb)]
    flow = [None]
    for b in range(1, nb):
        ends = fields[EAST, :, cols[b - 1]][:, LANES - 1 :]
        ends = ends * wet[b - 1][:, LANES - 1 :] * wet[b][:, :1]
        flow.append(jnp.broadcast_to(ends, (ROWS, LANES)))
    for c in range(tc):
        faces = [jnp.zeros((ROWS, LANES), f32) for _ in range(nb)]
        for t in range(tpc):
            for b in range(1, nb):
                west = pltpu.roll(cells[c * tpc + t, :, cols[b - 1]], (2 * t + 1) % LANES, 1)
                here = cells[c * tpc + t, :, cols[b]]
                here = pltpu.roll(here, 2 * t, 1) if t else here
                face = jnp.maximum(flow[b], 0.0) * west + jnp.minimum(flow[b], 0.0) * here
                faces[b] = jnp.where(lane == 2 * t, face, faces[b])
        for b in range(nb):
            edge = faces[b]
            if b + 1 < nb:
                edge = edge - pltpu.roll(faces[b + 1], LANES - 1, 1)
            for i in range(4):
                extra[b * tc + c, i] = fields[i, :, cols[b]]
            extra[b * tc + c, EDGE] = edge
    for d in devices(half):
        copy = pltpu.make_async_copy(
            extra.at[rank ^ d], out[d].at[pl.ds(tpc, EXTRA)], store_sem.at[1, d]
        )
        copy.start()
        stores.append(copy)
    for copy in stores:
        copy.wait()


def keep_kernel(prepared, piece, own, sem):
    del prepared
    copy = pltpu.make_async_copy(piece, own, sem.at[0])
    copy.start()
    copy.wait()


def relay_kernel(nb, tc, tpc, up, diff, *refs):
    half = nb * tc
    arrived, out = refs[:-1], refs[-1]
    _, rank, block, _ = place(nb, tc)
    cols = pl.ds(pl.multiple_of(block * LANES, LANES), LANES)
    for i, level in enumerate((up, diff)):
        field = level[0, :, cols]
        for d, even in zip(devices(half), arrived):
            field = jnp.where(rank == d, even[tpc + UP + i], field)
        out[i] = field


def pick_kernel(nb, tc, relayed, arrived, own):
    _, rank, _, _ = place(nb, tc)
    for i in range(2):
        own[i] = jnp.where(lax.rem(rank, 2) == 1, arrived[i], relayed[i])


def prep_kernel(nb, tc, tpc, thickness, group, rates, kmt_all, wet, depth, decay):
    half = nb * tc
    upper, _, block, chunk = place(nb, tc)
    kmt = kmt_all[:, pl.ds(pl.multiple_of(block * LANES, LANES), LANES)]
    for o in range(half + 1):
        k = jnp.where(upper == 1, 2 * half - 1 - o, o)
        wet[o] = (k < kmt).astype(f32)
        depth[o] = jnp.full((ROWS, LANES), thickness[k], f32)
        if o < half:
            for t in range(tpc):
                decay[o, pl.ds(t, 1)] = jnp.full((1, LANES), rates[group[chunk * tpc + t], k], f32)


def solve_kernel(nb, tc, tpc, paired, wets, depths, decay, *refs):
    half = nb * tc
    arrived = refs[: n_arrived(half, paired)]
    f_out, cells_out, cin_out, base_out, got = refs[-5:]
    upper, rank, _, _ = place(nb, tc)
    for slot, piece in by_level(half, paired, arrived, rank):
        for t in range(tpc + EXTRA):
            got[slot, t] = piece[t]
    sign = 1.0 - 2.0 * upper.astype(f32)
    lane, row = lanes_iota(), rows_iota()
    ends = jnp.logical_or(lane == 0, lane == LANES - 1)

    def slot_of(o):
        return jnp.where(upper == 1, half - 1 - o, o)

    zero = jnp.zeros((ROWS, LANES), f32)
    cin = tout = outer = add_mid = zero
    for o in range(half):
        slot = slot_of(o)
        dz, dz_next = depths[o], depths[o + 1]
        wet, wet_next = wets[o], wets[o + 1]
        last = o + 1 == half
        mid = wet + add_mid
        denom = 1.0 - outer - outer * cin
        if not last:
            face = jnp.where(upper == 1, slot, slot_of(o + 1))
            pos, neg, g = interface(
                got[face, tpc + UP], got[face, tpc + DIFF], sign, wet * wet_next, dz, dz_next
            )
            mid = mid + neg / dz
            tin = pos / dz
            inner = -g / dz
            alpha = 1.0 / (denom - inner)
        east = got[slot, tpc + EAST] * wet * pltpu.roll(wet, LANES - 1, 1)
        east = jnp.where(lane == LANES - 1, 0.0, east)
        north = got[slot, tpc + NORTH] * wet * pltpu.roll(wet, ROWS - 1, 0)
        north = jnp.where(row == ROWS - 1, 0.0, north)
        e_pos, e_neg = jnp.maximum(east, 0.0), jnp.minimum(east, 0.0)
        n_pos, n_neg = jnp.maximum(north, 0.0), jnp.minimum(north, 0.0)
        mid = mid - e_pos - n_pos + pltpu.roll(e_neg, 1, 1) + pltpu.roll(n_neg, 1, 0)
        e_pos, n_pos = pltpu.roll(e_pos, 1, 1), pltpu.roll(n_pos, 1, 0)
        edges = got[slot, tpc + EDGE]
        prev_slot = slot_of(o - 1) if o else None
        next_slot = None if last else slot_of(o + 1)
        for t in range(tpc):
            c = got[slot, t]
            star = c * (mid - decay[o, pl.ds(t, 1)] * wet)
            if o:
                star += tout * got[prev_slot, t]
            if not last:
                star += tin * got[next_slot, t]
            star += e_pos * pltpu.roll(c, 1, 1) - e_neg * pltpu.roll(c, LANES - 1, 1)
            star += n_pos * pltpu.roll(c, 1, 0) - n_neg * pltpu.roll(c, ROWS - 1, 0)
            edge = pltpu.roll(edges, LANES - 2 * t, 1) if t else edges
            star += jnp.where(ends, edge, 0.0)
            if o:
                star -= outer * f_out[o - 1, t]
            f_out[o, t] = star if last else alpha * star
            if last:
                cells_out[t] = c
        if last:
            base_out[0] = denom
            base_out[1] = wet * wet_next
            base_out[2] = jnp.full((ROWS, LANES), sign, f32)
            base_out[3] = dz
            base_out[4] = dz_next
        else:
            cin = inner * alpha
            cin_out[o] = cin
            tout, outer, add_mid = -neg / dz_next, -g / dz_next, -pos / dz_next


def interface(w, g, sign, open_face, dz, dz_next):
    w = sign * w * open_face
    dz_min = jnp.minimum(dz, dz_next)
    g = g * open_face / (0.5 * (dz + dz_next))
    return dz_min * jnp.maximum(w, 0.0), dz_min * jnp.minimum(w, 0.0), g


def seam_kernel(half, count, star, cells, base, own, other, f_out, coef_out, message):
    sign, dz, dz_next = base[2], base[3], base[4]
    w = jnp.where(sign < 0.0, own[0], other[0])
    g = jnp.where(sign < 0.0, own[1], other[1])
    pos, neg, g = interface(w, g, sign, base[1], dz, dz_next)
    inner, outer_next = -g / dz, -g / dz_next
    mid, tout_next = neg / dz, -neg / dz_next
    alpha = 1.0 / (base[0] - inner)
    for t in range(count):
        c = cells[t]
        f = alpha * (star[half - 1, t] + mid * c)
        f_out[t] = f
        message[t] = tout_next * c - outer_next * f
    coef_out[0] = inner * alpha
    coef_out[1] = alpha
    coef_out[2] = outer_next
    message[count] = alpha


def back_kernel(nb, tc, tpc, paired, f_in, cin, f_last, coef, sent, got, *refs):
    half = nb * tc
    out, solved = refs[:-1], refs[-1]
    upper, rank, _, _ = place(nb, tc)
    slots = [jnp.where(upper == 1, half - 1 - o, o) for o in range(half)]
    other = coef[0] * got[tpc]
    scale = 1.0 / (1.0 - other * coef[2])
    mine, theirs = scale * coef[1], scale * other
    for t in range(tpc):
        x = f_last[t] + (mine * got[t] - theirs * sent[t])
        solved[slots[half - 1], t] = x
        for o in range(half - 2, -1, -1):
            x = f_in[o, t] - cin[o] * x
            solved[slots[o], t] = x
    for (d, both), piece in zip(sends(half, paired), out):
        for t in range(tpc):
            if both:
                piece[0, t] = solved[rank ^ d, t]
                piece[1, t] = solved[rank ^ d ^ 1, t]
            else:
                piece[t] = solved[rank ^ d, t]


def join_kernel(nb, tc, tpc, paired, *refs):
    half = nb * tc
    arrived, out, sem = refs[:-2], refs[-2], refs[-1]
    copies = []
    _, rank, _, _ = place(nb, tc)
    for i, (r, piece) in enumerate(by_level(half, paired, arrived, rank)):
        cols = pl.ds(pl.multiple_of(lax.div(r, tc) * LANES, LANES), LANES)
        copies.append(
            pltpu.make_async_copy(
                piece, out.at[pl.ds(lax.rem(r, tc) * tpc, tpc), 0, :, cols], sem.at[i]
            )
        )
    for copy in copies:
        copy.start()
    for copy in copies:
        copy.wait()


def shards(tracer, east_flow, north_flow, up_flow, diffusivity, thickness, kmt, group, group_rate):
    ntr, ldev, ny, nx = tracer.shape
    count = lax.axis_size("lev")
    half = count // 2
    nb = nx // LANES
    tc = half // nb
    tpc = ntr // tc
    assert ldev == 1 and ny == ROWS and nb * LANES == nx and tc * nb == half and tpc * tc == ntr
    tile = (ROWS, LANES)
    vm = pl.BlockSpec(memory_space=pltpu.VMEM)
    sm = pl.BlockSpec(memory_space=pltpu.SMEM)
    hbm = pl.BlockSpec(memory_space=pltpu.HBM)
    anywhere = pl.BlockSpec(memory_space=pl.ANY)
    params = pltpu.CompilerParams(vmem_limit_bytes=VMEM_LIMIT)

    def flip(value, bits):
        return lax.ppermute(value, "lev", [(i, i ^ bits) for i in range(count)])

    def struct(*shape):
        return jax.ShapeDtypeStruct(shape + tile, f32)

    def outgoing(paired, n):
        return tuple(struct(2, n) if both else struct(n) for _, both in sends(half, paired))

    def exchange(values, paired):
        order = sends(half, paired)
        moved = [flip(piece, d) if d else piece for (d, _), piece in zip(order, values)]
        if not paired:
            return moved
        other = [piece for (_, both), piece in zip(order, moved) if both]
        after = [piece for (_, both), piece in zip(order, moved) if not both][:WAIT]
        grouped = pl.pallas_call(
            regroup_kernel,
            out_shape=jax.ShapeDtypeStruct((len(other),) + other[0].shape[1:], f32),
            in_specs=[vm] * len(other) + [anywhere] * len(after),
            out_specs=vm,
            compiler_params=params,
            name="regroup",
        )(*other, *after)
        return moved + [flip(grouped, 1)]

    there, home = pairing(half, THERE), pairing(half, HOME)
    pieces = pl.pallas_call(
        functools.partial(pack_kernel, nb, tc, tpc, there),
        out_shape=outgoing(there, tpc + EXTRA),
        in_specs=[hbm] * 6,
        out_specs=(hbm,) * len(sends(half, there)),
        scratch_shapes=[
            pltpu.VMEM((ntr, ny, nx), f32),
            pltpu.VMEM((4, ny, nx), f32),
            pltpu.VMEM((ny, nx), jnp.int32),
            pltpu.VMEM((half, EXTRA) + tile, f32),
            pltpu.SemaphoreType.DMA((5 + tc,)),
            pltpu.SemaphoreType.DMA((2, half)),
        ],
        compiler_params=pltpu.CompilerParams(vmem_limit_bytes=PACK_LIMIT),
        name="pack",
    )(tracer, east_flow, north_flow, up_flow, diffusivity, kmt)
    wet, depth, decay = pl.pallas_call(
        functools.partial(prep_kernel, nb, tc, tpc),
        out_shape=(
            struct(half + 1),
            struct(half + 1),
            jax.ShapeDtypeStruct((half, tpc, LANES), f32),
        ),
        in_specs=[sm, sm, sm, vm],
        out_specs=(vm,) * 3,
        compiler_params=params,
        name="prep",
    )(thickness, group, group_rate, kmt)
    kept = pl.pallas_call(
        keep_kernel,
        out_shape=struct(tpc + EXTRA),
        in_specs=[anywhere] * 2,
        out_specs=vm,
        scratch_shapes=[pltpu.SemaphoreType.DMA((1,))],
        compiler_params=params,
        name="keep",
    )(wet, pieces[-1])
    arrived = exchange(pieces[:-1] + (kept,), there)
    evens = half // 2 - 1
    relayed = pl.pallas_call(
        functools.partial(relay_kernel, nb, tc, tpc),
        out_shape=struct(2),
        in_specs=[vm] * (2 + evens),
        out_specs=vm,
        compiler_params=params,
        name="relay",
    )(up_flow, diffusivity, *arrived[:evens])
    own = pl.pallas_call(
        functools.partial(pick_kernel, nb, tc),
        out_shape=struct(2),
        in_specs=[vm, vm],
        out_specs=vm,
        compiler_params=params,
        name="pick",
    )(relayed, flip(relayed, 1))
    other = flip(own, half)
    f, cells, cin, base = pl.pallas_call(
        functools.partial(solve_kernel, nb, tc, tpc, there),
        out_shape=(struct(half, tpc), struct(tpc), struct(half - 1), struct(5)),
        in_specs=[vm] * (3 + len(arrived)),
        out_specs=(vm,) * 4,
        scratch_shapes=[pltpu.VMEM((half, tpc + EXTRA) + tile, f32)],
        compiler_params=params,
        name="solve",
    )(wet, depth, decay, *arrived)
    f_last, coef, message = pl.pallas_call(
        functools.partial(seam_kernel, half, tpc),
        out_shape=(struct(tpc), struct(3), struct(tpc + 1)),
        in_specs=[vm] * 5,
        out_specs=(vm,) * 3,
        compiler_params=params,
        name="seam",
    )(f, cells, base, own, other)
    solved = pl.pallas_call(
        functools.partial(back_kernel, nb, tc, tpc, home),
        out_shape=outgoing(home, tpc),
        in_specs=[vm] * 6,
        out_specs=(vm,) * len(sends(half, home)),
        scratch_shapes=[pltpu.VMEM((half, tpc) + tile, f32)],
        compiler_params=params,
        name="back",
    )(f, cin, f_last, coef, message, flip(message, half))
    back = exchange(solved, home)
    return pl.pallas_call(
        functools.partial(join_kernel, nb, tc, tpc, home),
        out_shape=jax.ShapeDtypeStruct(tracer.shape, f32),
        in_specs=[anywhere] * len(back),
        out_specs=hbm,
        scratch_shapes=[pltpu.SemaphoreType.DMA((half,))],
        compiler_params=params,
        name="join",
    )(*back)


def solution(mesh):
    placed = (
        P(None, "lev", "band", None),
        P("lev", "band", None),
        P("lev", "band", None),
        P("lev", "band", None),
        P("lev", "band", None),
        P(),
        P("band", None),
        P(),
        P(),
    )
    return jax.shard_map(
        shards, mesh=mesh, in_specs=placed, out_specs=P(None, "lev", "band", None), check_vma=False
    )
```

time: 50.8 us -> 47.4 us (0.933)
  waiting for transfers between devices: 22.5 us -> 20.8 us
  starting transfers between devices: 20.5 us -> 19.4 us
  local copies, waits for them, and re-layouts: 0.94 us -> 0.04 us
    ppermute x16 -> x17, waiting for transfers between devices: 22.5 us -> 20.8 us  [flip(): return lax.ppermute(value, 'lev', [(i, i ^ bits) for i in range(count)])]
    ppermute x16 -> x17, starting transfers between devices: 20.5 us -> 19.4 us  [flip(): return lax.ppermute(value, 'lev', [(i, i ^ bits) for i in range(count)])]
    unnamed x10 -> x14, local copies, waits for them, and re-layouts: 0.94 us -> 0.04 us
    pallas_call x7 -> x9, Pallas kernels: 6.58 us -> 6.82 us  [the longest x1 2.69 us: shards(): pl.pallas_call(functools.partial(pack_kernel, nb, tc, tpc, there), out_sh...]
  transfers between devices with their start and end apart: 16 -> 17, of which waited for: 10 -> 10; matrix products, arithmetic and copies ran while one was open for 0% -> 0% of each run, Pallas kernels for 4% -> 6%
where the time goes in v4:
time: 47.4 us; the launch traced here: 47.2 us
  waiting for transfers between devices  20.8 us (44%)
  starting transfers between devices  19.4 us (41%)
  Pallas kernels  6.82 us (14%)
    ppermute x17, waiting for transfers between devices, flip(): return lax.ppermute(value, 'lev', [(i, i ^ bits) for i in range(count)])  20.8 us
    ppermute x17, starting transfers between devices, flip(): return lax.ppermute(value, 'lev', [(i, i ^ bits) for i in range(count)])  19.4 us
    pallas_call x1, Pallas kernels, shards(): pl.pallas_call(functools.partial(pack_kernel, nb, tc, tpc, there), out_sh...  2.69 us
    pallas_call x1, Pallas kernels, shards(): pl.pallas_call(functools.partial(solve_kernel, nb, tc, tpc, there), out_s...  1.52 us
    pallas_call x1, Pallas kernels, shards(): pl.pallas_call(functools.partial(prep_kernel, nb, tc, tpc), out_shape=(st...  1.1 us
    pallas_call x1, Pallas kernels, shards(): pl.pallas_call(functools.partial(join_kernel, nb, tc, tpc, home), out_sha...  1.02 us
  transfers between devices with their start and end apart: 17, of which 10 were waited for; matrix products, arithmetic and copies ran while one was open for 0% of the time, Pallas kernels for 6%

profile of v4, /device:TPU:0, one launch (start us, length us, event | category | flops | bytes accessed | tf_op | source)
XLA Modules:
  0.0 47.2 jit_solution(18175505212333713258)
XLA Ops:
  0.0 0.0 copy-start.1
  0.0 0.0 copy-start.2
  0.0 2.7 %pack.1 = (f32[37,8,128]{2,1,0:T(8,128)}, f32[37,8,128]{2,1,0:T(8,128)}, f32[37,8,128]{2,1,0:T(8,128)}, f32[37,8,128]{2,1,0:T(8,128)}, f32[37,8,128]{2,1,0:T(8,1...) custom-call(f32[64,1,8,512]{3,2,1,0:T(8,128)} %tracer.1, f32[1,8,512]{2,1,0:T(8,128)} %east.1, ...), custom_call_target="tpu_custom_call" | custom-call | tf_op jit(solution)/shard_map/pack/pallas_call | solution.py:356
  2.7 4.0 %collective-permute-start = (f32[37,8,128]{2,1,0:T(8,128)}, f32[37,8,128]{2,1,0:T(8,128)S(1)}, u32[]{:S(2)}, u32[]{:S(2)}) collective-permute-start(f32[37,8,128]{2,1,0:T(8,128)} %get-tuple-element.34), channel_id=1, source_target_pairs={{0,6},{1,7},{2,4},{3,5},{4,2},{5,3},{6,0},{7,1},{8,14},{9,15},{10,... | collective-permute-start | bytes 454664 | tf_op jit(solution)/shard_map/ppermute | solution.py:330
  6.8 0.4 collective-permute-start.1
  7.2 0.2 collective-permute-start.2
  7.4 1.4 %collective-permute-start.3 = (f32[37,8,128]{2,1,0:T(8,128)}, f32[37,8,128]{2,1,0:T(8,128)S(1)}, u32[]{:S(2)}, u32[]{:S(2)}) collective-permute-start(f32[37,8,128]{2,1,0:T(8,128)} %get-tuple-element.37), channel_id=1, source_target_pairs={{0,7},{1,6},{2,5},{3,4},{4,3},{5,2},{6,1},{7,0},{8,15},{9,14},{10,... | collective-permute-start | bytes 454664 | tf_op jit(solution)/shard_map/ppermute | solution.py:330
  8.8 1.6 %collective-permute-start.4 = (f32[37,8,128]{2,1,0:T(8,128)}, f32[37,8,128]{2,1,0:T(8,128)S(1)}, u32[]{:S(2)}, u32[]{:S(2)}) collective-permute-start(f32[37,8,128]{2,1,0:T(8,128)} %get-tuple-element.38), channel_id=1, source_target_pairs={{0,5},{1,4},{2,7},{3,6},{4,1},{5,0},{6,3},{7,2},{8,13},{9,12},{10,... | collective-permute-start | bytes 454664 | tf_op jit(solution)/shard_map/ppermute | solution.py:330
  10.4 1.3 %collective-permute-done.refs_0_ = f32[37,8,128]{2,1,0:T(8,128)S(1)} collective-permute-done((f32[37,8,128]{2,1,0:T(8,128)}, f32[37,8,128]{2,1,0:T(8,128)S(1)}, u32[]{:S(2)}, u32[]{:S(2)}) %collective-permute-start) | collective-permute-done | bytes 151584 | tf_op jit(solution)/shard_map/ppermute | solution.py:330
  11.7 0.0 collective-permute-start.5
  11.7 3.7 %collective-permute-done.1.refs_1_ = f32[37,8,128]{2,1,0:T(8,128)S(1)} collective-permute-done((f32[37,8,128]{2,1,0:T(8,128)}, f32[37,8,128]{2,1,0:T(8,128)S(1)}, u32[]{:S(2)}, u32[]{:S(2)}) %collective-permute-start.1) | collective-permute-done | bytes 151584 | tf_op jit(solution)/shard_map/ppermute | solution.py:330
  15.5 0.0 copy-start
  15.5 0.0 collective-permute-start.6
  15.5 0.0 collective-permute-done.2.refs_2_
  15.5 0.0 copy-done.1
  15.5 0.0 copy-done.2
  15.5 0.0 copy-start.3
  15.5 0.0 copy-start.4
  15.6 0.0 copy-start.5
  15.6 0.0 copy-start.6
  15.6 0.6 %collective-permute-start.7 = (f32[2,8,128]{2,1,0:T(8,128)S(1)}, f32[2,8,128]{2,1,0:T(8,128)S(1)}, u32[]{:S(2)}, u32[]{:S(2)}) collective-permute-start(f32[2,8,128]{2,1,0:T(8,128)S(1)} %relay.1.relayed), channel_id=1, source_target_pairs={{0,1},{1,0},{2,3},{3,2},{4,5},{5,4},{6,7},{7,6},{8,9},{9,8},{10,11... | collective-permute-start | bytes 24584 | tf_op jit(solution)/shard_map/ppermute | solution.py:330
  16.1 0.8 %collective-permute-done.7.arrived = f32[2,8,128]{2,1,0:T(8,128)S(1)} collective-permute-done((f32[2,8,128]{2,1,0:T(8,128)S(1)}, f32[2,8,128]{2,1,0:T(8,128)S(1)}, u32[]{:S(2)}, u32[]{:S(2)}) %collective-permute-start.7) | collective-permute-done | bytes 8224 | tf_op jit(solution)/shard_map/ppermute | solution.py:330
  17.0 2.6 %collective-permute-start.8 = (f32[2,8,128]{2,1,0:T(8,128)S(1)}, f32[2,8,128]{2,1,0:T(8,128)S(1)}, u32[]{:S(2)}, u32[]{:S(2)}) collective-permute-start(f32[2,8,128]{2,1,0:T(8,128)S(1)} %pick.1.own), channel_id=1, source_target_pairs={{0,8},{1,9},{2,10},{3,11},{4,12},{5,13},{6,14},{7,15},{8,0},{9,1},... | collective-permute-start | bytes 24584 | tf_op jit(solution)/shard_map/ppermute | solution.py:330
  19.6 0.0 copy-done.3
  19.6 0.0 copy-done.4
  19.6 0.0 copy-done.5
  19.6 0.0 copy-done.6
  19.6 1.1 %prep.1 = (f32[9,8,128]{2,1,0:T(8,128)S(1)}, f32[9,8,128]{2,1,0:T(8,128)S(1)}, f32[8,32,128]{2,1,0:T(8,128)S(1)}) custom-call(f32[16]{0:T(128)S(1)} %copy-done.5, s32[64]{0:T(128)S(1)} %copy-done.6, f32[8,16]{1,0:T(8,128)S(1)} %copy-done.4, s32[8,512]{1,0:T(8,128)S(1)} %copy-done.3), custom_call_target="tpu_custom_call" | custom-call | tf_op jit(solution)/shard_map/prep/pallas_call | solution.py:372
  20.7 0.0 copy-done
  20.7 0.2 keep.1.refs_7_
  20.9 0.0 collective-permute-done.3.refs_3_
  20.9 0.0 collective-permute-done.4.refs_4_
  20.9 0.0 collective-permute-done.5.refs_5_
  20.9 0.0 collective-permute-done.6.refs_6_
  20.9 1.5 %solve.1 = (f32[8,32,8,128]{3,2,1,0:T(8,128)S(1)}, f32[32,8,128]{2,1,0:T(8,128)S(1)}, f32[7,8,128]{2,1,0:T(8,128)S(1)}, f32[5,8,128]{2,1,0:T(8,128)S(1)}) custom-call(f32[9,8,128]{2,1,0:T(8,128)S(1)} %get-tuple-element.31.prepared.wets, f32[9,8,128]{2,1,0:T(8,128)S(1)} %get-tuple-element.32.depths, f32[8,32,128]{2,1,0:T(8,128)S(1)} %get-tuple-element.33.decay, ...), custom_call_target="tpu_custom_call" | custom-call | tf_op jit(solution)/shard_map/solve/pallas_call | solution.py:412
  22.5 0.0 collective-permute-done.8.other
  22.5 2.5 %collective-permute-start.9 = (f32[33,8,128]{2,1,0:T(8,128)S(1)}, f32[33,8,128]{2,1,0:T(8,128)S(1)}, u32[]{:S(2)}, u32[]{:S(2)}) collective-permute-start(f32[33,8,128]{2,1,0:T(8,128)S(1)} %get-tuple-element.48.sent), channel_id=1, source_target_pairs={{0,8},{1,9},{2,10},{3,11},{4,12},{5,13},{6,14},{7,15},{8,0},{9,1},... | collective-permute-start | bytes 405512 | tf_op jit(solution)/shard_map/ppermute | solution.py:330
  25.0 6.9 %collective-permute-done.9.got = f32[33,8,128]{2,1,0:T(8,128)S(1)} collective-permute-done((f32[33,8,128]{2,1,0:T(8,128)S(1)}, f32[33,8,128]{2,1,0:T(8,128)S(1)}, u32[]{:S(2)}, u32[]{:S(2)}) %collective-permute-start.9) | collective-permute-done | bytes 135200 | tf_op jit(solution)/shard_map/ppermute | solution.py:330
  31.9 0.2 back.1
  32.2 1.5 %collective-permute-start.10 = (f32[32,8,128]{2,1,0:T(8,128)S(1)}, f32[32,8,128]{2,1,0:T(8,128)S(1)}, u32[]{:S(2)}, u32[]{:S(2)}) collective-permute-start(f32[32,8,128]{2,1,0:T(8,128)S(1)} %get-tuple-element.49), channel_id=1, source_target_pairs={{0,6},{1,7},{2,4},{3,5},{4,2},{5,3},{6,0},{7,1},{8,14},{9,15},{10,... | collective-permute-start | bytes 393224 | tf_op jit(solution)/shard_map/ppermute | solution.py:330
  33.7 1.3 %collective-permute-start.11 = (f32[32,8,128]{2,1,0:T(8,128)S(1)}, f32[32,8,128]{2,1,0:T(8,128)S(1)}, u32[]{:S(2)}, u32[]{:S(2)}) collective-permute-start(f32[32,8,128]{2,1,0:T(8,128)S(1)} %get-tuple-element.50), channel_id=1, source_target_pairs={{0,4},{1,5},{2,6},{3,7},{4,0},{5,1},{6,2},{7,3},{8,12},{9,13},{10,... | collective-permute-start | bytes 393224 | tf_op jit(solution)/shard_map/ppermute | solution.py:330
  35.0 0.7 %collective-permute-start.12 = (f32[32,8,128]{2,1,0:T(8,128)S(1)}, f32[32,8,128]{2,1,0:T(8,128)S(1)}, u32[]{:S(2)}, u32[]{:S(2)}) collective-permute-start(f32[32,8,128]{2,1,0:T(8,128)S(1)} %get-tuple-element.51), channel_id=1, source_target_pairs={{0,2},{1,3},{2,0},{3,1},{4,6},{5,7},{6,4},{7,5},{8,10},{9,11},{10,... | collective-permute-start | bytes 393224 | tf_op jit(solution)/shard_map/ppermute | solution.py:330
  35.7 0.2 collective-permute-start.13
  35.9 2.3 %collective-permute-start.14 = (f32[32,8,128]{2,1,0:T(8,128)S(1)}, f32[32,8,128]{2,1,0:T(8,128)S(1)}, u32[]{:S(2)}, u32[]{:S(2)}) collective-permute-start(f32[32,8,128]{2,1,0:T(8,128)S(1)} %get-tuple-element.53), channel_id=1, source_target_pairs={{0,5},{1,4},{2,7},{3,6},{4,1},{5,0},{6,3},{7,2},{8,13},{9,12},{10,... | collective-permute-start | bytes 393224 | tf_op jit(solution)/shard_map/ppermute | solution.py:330
  38.2 1.0 %collective-permute-done.10.refs_0_ = f32[32,8,128]{2,1,0:T(8,128)S(1)} collective-permute-done((f32[32,8,128]{2,1,0:T(8,128)S(1)}, f32[32,8,128]{2,1,0:T(8,128)S(1)}, u32[]{:S(2)}, u32[]{:S(2)}) %collective-permute-start.10) | collective-permute-done | bytes 131104 | tf_op jit(solution)/shard_map/ppermute | solution.py:330
  39.2 0.0 collective-permute-start.15
  39.2 2.1 %collective-permute-done.11.refs_1_ = f32[32,8,128]{2,1,0:T(8,128)S(1)} collective-permute-done((f32[32,8,128]{2,1,0:T(8,128)S(1)}, f32[32,8,128]{2,1,0:T(8,128)S(1)}, u32[]{:S(2)}, u32[]{:S(2)}) %collective-permute-start.11) | collective-permute-done | bytes 131104 | tf_op jit(solution)/shard_map/ppermute | solution.py:330
  41.3 0.0 collective-permute-start.16
  41.3 0.2 collective-permute-done.12.refs_2_
  41.4 1.7 %collective-permute-done.13.refs_3_ = f32[32,8,128]{2,1,0:T(8,128)S(1)} collective-permute-done((f32[32,8,128]{2,1,0:T(8,128)S(1)}, f32[32,8,128]{2,1,0:T(8,128)S(1)}, u32[]{:S(2)}, u32[]{:S(2)}) %collective-permute-start.13) | collective-permute-done | bytes 131104 | tf_op jit(solution)/shard_map/ppermute | solution.py:330
  43.2 2.0 %collective-permute-done.14.refs_4_ = f32[32,8,128]{2,1,0:T(8,128)S(1)} collective-permute-done((f32[32,8,128]{2,1,0:T(8,128)S(1)}, f32[32,8,128]{2,1,0:T(8,128)S(1)}, u32[]{:S(2)}, u32[]{:S(2)}) %collective-permute-start.14) | collective-permute-done | bytes 131104 | tf_op jit(solution)/shard_map/ppermute | solution.py:330
  45.1 1.0 %collective-permute-done.15.refs_5_ = f32[32,8,128]{2,1,0:T(8,128)S(1)} collective-permute-done((f32[32,8,128]{2,1,0:T(8,128)S(1)}, f32[32,8,128]{2,1,0:T(8,128)S(1)}, u32[]{:S(2)}, u32[]{:S(2)}) %collective-permute-start.15) | collective-permute-done | bytes 131104 | tf_op jit(solution)/shard_map/ppermute | solution.py:330
  46.2 0.0 collective-permute-done.16.refs_6_
  46.2 1.0 %join.1 = f32[64,1,8,512]{3,2,1,0:T(8,128)} custom-call(f32[32,8,128]{2,1,0:T(8,128)S(1)} %collective-permute-done.10.refs_0_, f32[32,8,128]{2,1,0:T(8,128)S(1)} %collective-permute-done.11.refs_1_, f32[32,8,128]{2,1,0:T(8,128)S(1)} %collective-permute-done.12.refs_2_, f32[32,8,128]{2,1,0:T(8,128)S(1)} %collective-permute-done.13.refs_3_, ...), custom_call_target="tpu_custom_call" | custom-call | tf_op jit(solution)/shard_map/join/pallas_call | solution.py:439
  (3 shorter events, 0.1 us)
Async XLA Ops:
  0.0 15.5 %copy-start.1 = (f32[1,8,512]{2,1,0:T(8,128)S(1)}, f32[1,8,512]{2,1,0:T(8,128)}, u32[]{:S(2)}) copy-start(f32[1,8,512]{2,1,0:T(8,128)} %up.3) | copy-start | bytes 49156
  0.0 15.5 %copy-start.2 = (f32[1,8,512]{2,1,0:T(8,128)S(1)}, f32[1,8,512]{2,1,0:T(8,128)}, u32[]{:S(2)}) copy-start(f32[1,8,512]{2,1,0:T(8,128)} %diff.3) | copy-start | bytes 49156
  2.7 9.0 %collective-permute-start = (f32[37,8,128]{2,1,0:T(8,128)}, f32[37,8,128]{2,1,0:T(8,128)S(1)}, u32[]{:S(2)}, u32[]{:S(2)}) collective-permute-start(f32[37,8,128]{2,1,0:T(8,128)} %get-tuple-element.34), channel_id=1, source_target_pairs={{0,6},{1,7},{2,4},{3,5},{4,2},{5,3},{6,0},{7,1},{8,14},{9,15},{10,... | collective-permute-start | bytes 454664 | tf_op jit(solution)/shard_map/ppermute | solution.py:330
  6.8 8.7 %collective-permute-start.1 = (f32[37,8,128]{2,1,0:T(8,128)}, f32[37,8,128]{2,1,0:T(8,128)S(1)}, u32[]{:S(2)}, u32[]{:S(2)}) collective-permute-start(f32[37,8,128]{2,1,0:T(8,128)} %get-tuple-element.35), channel_id=1, source_target_pairs={{0,4},{1,5},{2,6},{3,7},{4,0},{5,1},{6,2},{7,3},{8,12},{9,13},{10,... | collective-permute-start | bytes 454664 | tf_op jit(solution)/shard_map/ppermute | solution.py:330
  7.2 8.3 %collective-permute-start.2 = (f32[37,8,128]{2,1,0:T(8,128)}, f32[37,8,128]{2,1,0:T(8,128)S(1)}, u32[]{:S(2)}, u32[]{:S(2)}) collective-permute-start(f32[37,8,128]{2,1,0:T(8,128)} %get-tuple-element.36), channel_id=1, source_target_pairs={{0,2},{1,3},{2,0},{3,1},{4,6},{5,7},{6,4},{7,5},{8,10},{9,11},{10,... | collective-permute-start | bytes 454664 | tf_op jit(solution)/shard_map/ppermute | solution.py:330
  7.4 13.5 %collective-permute-start.3 = (f32[37,8,128]{2,1,0:T(8,128)}, f32[37,8,128]{2,1,0:T(8,128)S(1)}, u32[]{:S(2)}, u32[]{:S(2)}) collective-permute-start(f32[37,8,128]{2,1,0:T(8,128)} %get-tuple-element.37), channel_id=1, source_target_pairs={{0,7},{1,6},{2,5},{3,4},{4,3},{5,2},{6,1},{7,0},{8,15},{9,14},{10,... | collective-permute-start | bytes 454664 | tf_op jit(solution)/shard_map/ppermute | solution.py:330
  8.8 12.1 %collective-permute-start.4 = (f32[37,8,128]{2,1,0:T(8,128)}, f32[37,8,128]{2,1,0:T(8,128)S(1)}, u32[]{:S(2)}, u32[]{:S(2)}) collective-permute-start(f32[37,8,128]{2,1,0:T(8,128)} %get-tuple-element.38), channel_id=1, source_target_pairs={{0,5},{1,4},{2,7},{3,6},{4,1},{5,0},{6,3},{7,2},{8,13},{9,12},{10,... | collective-permute-start | bytes 454664 | tf_op jit(solution)/shard_map/ppermute | solution.py:330
  11.7 9.2 %collective-permute-start.5 = (f32[37,8,128]{2,1,0:T(8,128)}, f32[37,8,128]{2,1,0:T(8,128)S(1)}, u32[]{:S(2)}, u32[]{:S(2)}) collective-permute-start(f32[37,8,128]{2,1,0:T(8,128)} %get-tuple-element.39), channel_id=1, source_target_pairs={{0,3},{1,2},{2,1},{3,0},{4,7},{5,6},{6,5},{7,4},{8,11},{9,10},{10,... | collective-permute-start | bytes 454664 | tf_op jit(solution)/shard_map/ppermute | solution.py:330
  15.5 5.2 %copy-start = (f32[37,8,128]{2,1,0:T(8,128)S(1)}, f32[37,8,128]{2,1,0:T(8,128)}, u32[]{:S(2)}) copy-start(f32[37,8,128]{2,1,0:T(8,128)} %get-tuple-element.41.piece) | copy-start | bytes 454660
  15.5 5.5 %collective-permute-start.6 = (f32[37,8,128]{2,1,0:T(8,128)}, f32[37,8,128]{2,1,0:T(8,128)S(1)}, u32[]{:S(2)}, u32[]{:S(2)}) collective-permute-start(f32[37,8,128]{2,1,0:T(8,128)} %get-tuple-element.40), channel_id=1, source_target_pairs={{0,1},{1,0},{2,3},{3,2},{4,5},{5,4},{6,7},{7,6},{8,9},{9,8},{10,11... | collective-permute-start | bytes 454664 | tf_op jit(solution)/shard_map/ppermute | solution.py:330
  15.5 4.0 %copy-start.3 = (s32[8,512]{1,0:T(8,128)S(1)}, s32[8,512]{1,0:T(8,128)}, u32[]{:S(2)}) copy-start(s32[8,512]{1,0:T(8,128)} %kmt.1) | copy-start | bytes 49156
  15.5 4.0 %copy-start.4 = (f32[8,16]{1,0:T(8,128)S(1)}, f32[8,16]{1,0:T(8,128)}, u32[]{:S(2)}) copy-start(f32[8,16]{1,0:T(8,128)} %rates.1) | copy-start | bytes 1540
  15.6 4.0 %copy-start.5 = (f32[16]{0:T(128)S(1)}, f32[16]{0:T(128)}, u32[]{:S(2)}) copy-start(f32[16]{0:T(128)} %thickness.1) | copy-start | bytes 196
  15.6 4.0 %copy-start.6 = (s32[64]{0:T(128)S(1)}, s32[64]{0:T(128)}, u32[]{:S(2)}) copy-start(s32[64]{0:T(128)} %group.1) | copy-start | bytes 772
  15.6 1.4 %collective-permute-start.7 = (f32[2,8,128]{2,1,0:T(8,128)S(1)}, f32[2,8,128]{2,1,0:T(8,128)S(1)}, u32[]{:S(2)}, u32[]{:S(2)}) collective-permute-start(f32[2,8,128]{2,1,0:T(8,128)S(1)} %relay.1.relayed), channel_id=1, source_target_pairs={{0,1},{1,0},{2,3},{3,2},{4,5},{5,4},{6,7},{7,6},{8,9},{9,8},{10,11... | collective-permute-start | bytes 24584 | tf_op jit(solution)/shard_map/ppermute | solution.py:330
  17.0 5.5 %collective-permute-start.8 = (f32[2,8,128]{2,1,0:T(8,128)S(1)}, f32[2,8,128]{2,1,0:T(8,128)S(1)}, u32[]{:S(2)}, u32[]{:S(2)}) collective-permute-start(f32[2,8,128]{2,1,0:T(8,128)S(1)} %pick.1.own), channel_id=1, source_target_pairs={{0,8},{1,9},{2,10},{3,11},{4,12},{5,13},{6,14},{7,15},{8,0},{9,1},... | collective-permute-start | bytes 24584 | tf_op jit(solution)/shard_map/ppermute | solution.py:330
  22.5 9.4 %collective-permute-start.9 = (f32[33,8,128]{2,1,0:T(8,128)S(1)}, f32[33,8,128]{2,1,0:T(8,128)S(1)}, u32[]{:S(2)}, u32[]{:S(2)}) collective-permute-start(f32[33,8,128]{2,1,0:T(8,128)S(1)} %get-tuple-element.48.sent), channel_id=1, source_target_pairs={{0,8},{1,9},{2,10},{3,11},{4,12},{5,13},{6,14},{7,15},{8,0},{9,1},... | collective-permute-start | bytes 405512 | tf_op jit(solution)/shard_map/ppermute | solution.py:330
  32.2 7.0 %collective-permute-start.10 = (f32[32,8,128]{2,1,0:T(8,128)S(1)}, f32[32,8,128]{2,1,0:T(8,128)S(1)}, u32[]{:S(2)}, u32[]{:S(2)}) collective-permute-start(f32[32,8,128]{2,1,0:T(8,128)S(1)} %get-tuple-element.49), channel_id=1, source_target_pairs={{0,6},{1,7},{2,4},{3,5},{4,2},{5,3},{6,0},{7,1},{8,14},{9,15},{10,... | collective-permute-start | bytes 393224 | tf_op jit(solution)/shard_map/ppermute | solution.py:330
  33.7 7.6 %collective-permute-start.11 = (f32[32,8,128]{2,1,0:T(8,128)S(1)}, f32[32,8,128]{2,1,0:T(8,128)S(1)}, u32[]{:S(2)}, u32[]{:S(2)}) collective-permute-start(f32[32,8,128]{2,1,0:T(8,128)S(1)} %get-tuple-element.50), channel_id=1, source_target_pairs={{0,4},{1,5},{2,6},{3,7},{4,0},{5,1},{6,2},{7,3},{8,12},{9,13},{10,... | collective-permute-start | bytes 393224 | tf_op jit(solution)/shard_map/ppermute | solution.py:330
  35.0 6.4 %collective-permute-start.12 = (f32[32,8,128]{2,1,0:T(8,128)S(1)}, f32[32,8,128]{2,1,0:T(8,128)S(1)}, u32[]{:S(2)}, u32[]{:S(2)}) collective-permute-start(f32[32,8,128]{2,1,0:T(8,128)S(1)} %get-tuple-element.51), channel_id=1, source_target_pairs={{0,2},{1,3},{2,0},{3,1},{4,6},{5,7},{6,4},{7,5},{8,10},{9,11},{10,... | collective-permute-start | bytes 393224 | tf_op jit(solution)/shard_map/ppermute | solution.py:330
  35.7 7.5 %collective-permute-start.13 = (f32[32,8,128]{2,1,0:T(8,128)S(1)}, f32[32,8,128]{2,1,0:T(8,128)S(1)}, u32[]{:S(2)}, u32[]{:S(2)}) collective-permute-start(f32[32,8,128]{2,1,0:T(8,128)S(1)} %get-tuple-element.52), channel_id=1, source_target_pairs={{0,7},{1,6},{2,5},{3,4},{4,3},{5,2},{6,1},{7,0},{8,15},{9,14},{10,... | collective-permute-start | bytes 393224 | tf_op jit(solution)/shard_map/ppermute | solution.py:330
  35.9 9.2 %collective-permute-start.14 = (f32[32,8,128]{2,1,0:T(8,128)S(1)}, f32[32,8,128]{2,1,0:T(8,128)S(1)}, u32[]{:S(2)}, u32[]{:S(2)}) collective-permute-start(f32[32,8,128]{2,1,0:T(8,128)S(1)} %get-tuple-element.53), channel_id=1, source_target_pairs={{0,5},{1,4},{2,7},{3,6},{4,1},{5,0},{6,3},{7,2},{8,13},{9,12},{10,... | collective-permute-start | bytes 393224 | tf_op jit(solution)/shard_map/ppermute | solution.py:330
  39.2 7.0 %collective-permute-start.15 = (f32[32,8,128]{2,1,0:T(8,128)S(1)}, f32[32,8,128]{2,1,0:T(8,128)S(1)}, u32[]{:S(2)}, u32[]{:S(2)}) collective-permute-start(f32[32,8,128]{2,1,0:T(8,128)S(1)} %get-tuple-element.54), channel_id=1, source_target_pairs={{0,3},{1,2},{2,1},{3,0},{4,7},{5,6},{6,5},{7,4},{8,11},{9,10},{10,... | collective-permute-start | bytes 393224 | tf_op jit(solution)/shard_map/ppermute | solution.py:330
  41.3 4.9 %collective-permute-start.16 = (f32[32,8,128]{2,1,0:T(8,128)S(1)}, f32[32,8,128]{2,1,0:T(8,128)S(1)}, u32[]{:S(2)}, u32[]{:S(2)}) collective-permute-start(f32[32,8,128]{2,1,0:T(8,128)S(1)} %get-tuple-element.55), channel_id=1, source_target_pairs={{0,1},{1,0},{2,3},{3,2},{4,5},{5,4},{6,7},{7,6},{8,9},{9,8},{10,11... | collective-permute-start | bytes 393224 | tf_op jit(solution)/shard_map/ppermute | solution.py:330

commit v5 on v4

--- a/solution.py
+++ b/solution.py
@@ -11,7 +11,7 @@
 ROWS = 8
 THERE, HOME = "none", "none"
 WAIT = 1
-EAST, NORTH, UP, DIFF, EDGE, EXTRA = 0, 1, 2, 3, 4, 5
+EDGE, EAST, NORTH, UP, DIFF, EXTRA = 0, 1, 2, 3, 4, 5
 f32 = jnp.float32
 VMEM_LIMIT = 16 * 1024 * 1024
 PACK_LIMIT = 60 * 1024 * 1024
@@ -29,6 +29,10 @@
     far, near = half // 2, half // 4
     crossed = lambda d: ((d & far) > 0) + ((d & near) > 0)
     return sorted(range(1, half), key=lambda d: (d < 2, d & 1, -crossed(d), -d)) + [0]
+
+
+def n_extra(d):
+    return 1 if d % 2 else EXTRA
 
 
 def pairing(half, which):
@@ -61,40 +65,31 @@
     return lax.div(index, half), rank, lax.div(rank, tc), lax.rem(rank, tc)
 
 
-def pack_kernel(nb, tc, tpc, paired, tracer, east, north, up, diff, kmt, *refs):
-    half = nb * tc
-    _, rank, _, _ = place(nb, tc)
-    order = sends(half, paired)
-    out = {}
-    for j, (d, both) in enumerate(order):
-        if both:
-            out[d], out[d ^ 1] = refs[j].at[0], refs[j].at[1]
-        else:
-            out[d] = refs[j]
-    cells, fields, depth, extra, sem, store_sem = refs[len(order) :]
-    loads = [
-        pltpu.make_async_copy(kmt, depth, sem.at[0]),
-        pltpu.make_async_copy(east, fields.at[pl.ds(EAST, 1)], sem.at[1]),
-        pltpu.make_async_copy(north, fields.at[pl.ds(NORTH, 1)], sem.at[2]),
-        pltpu.make_async_copy(up, fields.at[pl.ds(UP, 1)], sem.at[3]),
-        pltpu.make_async_copy(diff, fields.at[pl.ds(DIFF, 1)], sem.at[4]),
-    ]
+def pack_kernel(nb, tc, tpc, odd, tracer, east, north, up, diff, kmt, *refs):
+    half = nb * tc
+    _, rank, _, chunk = place(nb, tc)
+    distances = [d for d in devices(half) if d % 2 == odd]
+    turns = range(odd, tc, 2)
+    out = dict(zip(distances, refs))
+    cells, fields, depth, extra, sem, store_sem = refs[len(distances) :]
+    loads = [pltpu.make_async_copy(kmt, depth, sem.at[0])]
+    for i, field in enumerate((east,) if odd else (east, north, up, diff)):
+        loads.append(pltpu.make_async_copy(field, fields.at[pl.ds(i, 1)], sem.at[1 + i]))
     chunks = [
         pltpu.make_async_copy(
-            tracer.at[pl.ds(c * tpc, tpc), 0], cells.at[pl.ds(c * tpc, tpc)], sem.at[5 + c]
+            tracer.at[pl.ds((chunk ^ e) * tpc, tpc), 0], cells.at[pl.ds(e // 2 * tpc, tpc)], sem.at[5 + e // 2]
         )
-        for c in range(tc)
+        for e in turns
     ]
     for copy in chunks + loads:
         copy.start()
     for copy in chunks:
         copy.wait()
     stores = []
-    for d in devices(half):
-        r = rank ^ d
-        cut = pl.ds(pl.multiple_of(lax.div(r, tc) * LANES, LANES), LANES)
+    for d in distances:
+        cut = pl.ds(pl.multiple_of(lax.div(rank ^ d, tc) * LANES, LANES), LANES)
         copy = pltpu.make_async_copy(
-            cells.at[pl.ds(lax.rem(r, tc) * tpc, tpc), :, cut], out[d].at[pl.ds(0, tpc)], store_sem.at[0, d]
+            cells.at[pl.ds(d % tc // 2 * tpc, tpc), :, cut], out[d].at[pl.ds(0, tpc)], store_sem.at[0, d // 2]
         )
         copy.start()
         stores.append(copy)
@@ -105,15 +100,16 @@
     wet = [(lax.axis_index("lev") < depth[:, cols[b]]).astype(f32) for b in range(nb)]
     flow = [None]
     for b in range(1, nb):
-        ends = fields[EAST, :, cols[b - 1]][:, LANES - 1 :]
+        ends = fields[0, :, cols[b - 1]][:, LANES - 1 :]
         ends = ends * wet[b - 1][:, LANES - 1 :] * wet[b][:, :1]
         flow.append(jnp.broadcast_to(ends, (ROWS, LANES)))
-    for c in range(tc):
+    for e in turns:
         faces = [jnp.zeros((ROWS, LANES), f32) for _ in range(nb)]
         for t in range(tpc):
+            at = e // 2 * tpc + t
             for b in range(1, nb):
-                west = pltpu.roll(cells[c * tpc + t, :, cols[b - 1]], (2 * t + 1) % LANES, 1)
-                here = cells[c * tpc + t, :, cols[b]]
+                west = pltpu.roll(cells[at, :, cols[b - 1]], (2 * t + 1) % LANES, 1)
+                here = cells[at, :, cols[b]]
                 here = pltpu.roll(here, 2 * t, 1) if t else here
                 face = jnp.maximum(flow[b], 0.0) * west + jnp.minimum(flow[b], 0.0) * here
                 faces[b] = jnp.where(lane == 2 * t, face, faces[b])
@@ -121,12 +117,15 @@
             edge = faces[b]
             if b + 1 < nb:
                 edge = edge - pltpu.roll(faces[b + 1], LANES - 1, 1)
-            for i in range(4):
-                extra[b * tc + c, i] = fields[i, :, cols[b]]
-            extra[b * tc + c, EDGE] = edge
-    for d in devices(half):
+            extra[e // 2, b, EDGE] = edge
+            if not odd:
+                for i in range(4):
+                    extra[e // 2, b, EAST + i] = fields[i, :, cols[b]]
+    for d in distances:
         copy = pltpu.make_async_copy(
-            extra.at[rank ^ d], out[d].at[pl.ds(tpc, EXTRA)], store_sem.at[1, d]
+            extra.at[d % tc // 2, lax.div(rank ^ d, tc), pl.ds(0, n_extra(d))],
+            out[d].at[pl.ds(tpc, n_extra(d))],
+            store_sem.at[1, d // 2],
         )
         copy.start()
         stores.append(copy)
@@ -141,45 +140,65 @@
     copy.wait()
 
 
-def relay_kernel(nb, tc, tpc, up, diff, *refs):
-    half = nb * tc
-    arrived, out = refs[:-1], refs[-1]
+def relay_kernel(nb, tc, tpc, east, north, up, diff, *refs):
+    half = nb * tc
+    arrived, (out, seam) = refs[:-2], refs[-2:]
     _, rank, block, _ = place(nb, tc)
     cols = pl.ds(pl.multiple_of(block * LANES, LANES), LANES)
-    for i, level in enumerate((up, diff)):
-        field = level[0, :, cols]
+    for j, even in enumerate(arrived):
+        for i in range(4):
+            out[4 * j + i] = even[tpc + EAST + i]
+    own = [level[0, :, cols] for level in (east, north, up, diff)]
+    for i in range(4):
+        out[4 * len(arrived) + i] = own[i]
+    for i in range(2):
+        field = own[UP - EAST + i]
         for d, even in zip(devices(half), arrived):
             field = jnp.where(rank == d, even[tpc + UP + i], field)
-        out[i] = field
-
-
-def pick_kernel(nb, tc, relayed, arrived, own):
+        out[4 * len(arrived) + 4 + i] = field
+        seam[i] = field
+
+
+def pick_kernel(nb, tc, seam, swapped, own):
     _, rank, _, _ = place(nb, tc)
     for i in range(2):
-        own[i] = jnp.where(lax.rem(rank, 2) == 1, arrived[i], relayed[i])
-
-
-def prep_kernel(nb, tc, tpc, thickness, group, rates, kmt_all, wet, depth, decay):
+        own[i] = jnp.where(lax.rem(rank, 2) == 1, swapped[swapped.shape[0] - 2 + i], seam[i])
+
+
+def prep_kernel(nb, tc, tpc, thickness, group, rates, kmt_all, wet, depth, decay, table):
     half = nb * tc
     upper, _, block, chunk = place(nb, tc)
     kmt = kmt_all[:, pl.ds(pl.multiple_of(block * LANES, LANES), LANES)]
-    for o in range(half + 1):
-        k = jnp.where(upper == 1, 2 * half - 1 - o, o)
+    levels = [jnp.where(upper == 1, 2 * half - 1 - o, o) for o in range(half + 1)]
+    for o, k in enumerate(levels):
         wet[o] = (k < kmt).astype(f32)
         depth[o] = jnp.full((ROWS, LANES), thickness[k], f32)
-        if o < half:
-            for t in range(tpc):
-                decay[o, pl.ds(t, 1)] = jnp.full((1, LANES), rates[group[chunk * tpc + t], k], f32)
-
-
-def solve_kernel(nb, tc, tpc, paired, wets, depths, decay, *refs):
+    row = rows_iota()
+    for g in range(rates.shape[0]):
+        for at in range(0, half, ROWS):
+            tile = jnp.zeros((ROWS, LANES), f32)
+            for i in range(min(ROWS, half - at)):
+                tile = jnp.where(row == i, rates[g, levels[at + i]], tile)
+            table[g, at : at + ROWS] = tile[: min(ROWS, half - at)]
+    for t in range(tpc):
+        decay[t] = table[group[chunk * tpc + t]]
+
+
+def solve_kernel(nb, tc, tpc, paired, wets, depths, decay, swapped, *refs):
     half = nb * tc
     arrived = refs[: n_arrived(half, paired)]
     f_out, cells_out, cin_out, base_out, got = refs[-5:]
     upper, rank, _, _ = place(nb, tc)
-    for slot, piece in by_level(half, paired, arrived, rank):
-        for t in range(tpc + EXTRA):
-            got[slot, t] = piece[t]
+    evens = [d for d in devices(half) if d % 2 == 0]
+    for d, piece in zip(devices(half), arrived):
+        for t in range(tpc):
+            got[rank ^ d, t] = piece[t]
+        got[rank ^ d, tpc + EDGE] = piece[tpc + EDGE]
+        for i in range(EAST, EXTRA):
+            if d % 2:
+                got[rank ^ d, tpc + i] = swapped[4 * evens.index(d ^ 1) + i - EAST]
+            else:
+                got[rank ^ d, tpc + i] = piece[tpc + i]
     sign = 1.0 - 2.0 * upper.astype(f32)
     lane, row = lanes_iota(), rows_iota()
     ends = jnp.logical_or(lane == 0, lane == LANES - 1)
@@ -218,7 +237,7 @@
         next_slot = None if last else slot_of(o + 1)
         for t in range(tpc):
             c = got[slot, t]
-            star = c * (mid - decay[o, pl.ds(t, 1)] * wet)
+            star = c * (mid - decay[t, pl.ds(o, 1)] * wet)
             if o:
                 star += tout * got[prev_slot, t]
             if not last:
@@ -318,6 +337,7 @@
     nb = nx // LANES
     tc = half // nb
     tpc = ntr // tc
+    assert tc % 2 == 0 and 2 * tpc <= LANES
     assert ldev == 1 and ny == ROWS and nb * LANES == nx and tc * nb == half and tpc * tc == ntr
     tile = (ROWS, LANES)
     vm = pl.BlockSpec(memory_space=pltpu.VMEM)
@@ -353,31 +373,37 @@
         return moved + [flip(grouped, 1)]
 
     there, home = pairing(half, THERE), pairing(half, HOME)
-    pieces = pl.pallas_call(
-        functools.partial(pack_kernel, nb, tc, tpc, there),
-        out_shape=outgoing(there, tpc + EXTRA),
-        in_specs=[hbm] * 6,
-        out_specs=(hbm,) * len(sends(half, there)),
-        scratch_shapes=[
-            pltpu.VMEM((ntr, ny, nx), f32),
-            pltpu.VMEM((4, ny, nx), f32),
-            pltpu.VMEM((ny, nx), jnp.int32),
-            pltpu.VMEM((half, EXTRA) + tile, f32),
-            pltpu.SemaphoreType.DMA((5 + tc,)),
-            pltpu.SemaphoreType.DMA((2, half)),
-        ],
-        compiler_params=pltpu.CompilerParams(vmem_limit_bytes=PACK_LIMIT),
-        name="pack",
-    )(tracer, east_flow, north_flow, up_flow, diffusivity, kmt)
+    packed = {}
+    for odd in range(2):
+        distances = [d for d in devices(half) if d % 2 == odd]
+        pieces = pl.pallas_call(
+            functools.partial(pack_kernel, nb, tc, tpc, odd),
+            out_shape=tuple(struct(tpc + n_extra(d)) for d in distances),
+            in_specs=[hbm] * 6,
+            out_specs=(hbm,) * len(distances),
+            scratch_shapes=[
+                pltpu.VMEM((ntr // 2, ny, nx), f32),
+                pltpu.VMEM((4, ny, nx), f32),
+                pltpu.VMEM((ny, nx), jnp.int32),
+                pltpu.VMEM((tc // 2, nb, EXTRA) + tile, f32),
+                pltpu.SemaphoreType.DMA((5 + tc // 2,)),
+                pltpu.SemaphoreType.DMA((2, half // 2)),
+            ],
+            compiler_params=pltpu.CompilerParams(vmem_limit_bytes=PACK_LIMIT),
+            name="pack",
+        )(tracer, east_flow, north_flow, up_flow, diffusivity, kmt)
+        packed.update(zip(distances, pieces))
+    pieces = tuple(packed[d] for d in devices(half))
     wet, depth, decay = pl.pallas_call(
         functools.partial(prep_kernel, nb, tc, tpc),
         out_shape=(
             struct(half + 1),
             struct(half + 1),
-            jax.ShapeDtypeStruct((half, tpc, LANES), f32),
+            jax.ShapeDtypeStruct((tpc, half, LANES), f32),
         ),
         in_specs=[sm, sm, sm, vm],
         out_specs=(vm,) * 3,
+        scratch_shapes=[pltpu.VMEM((group_rate.shape[0], half, LANES), f32)],
         compiler_params=params,
         name="prep",
     )(thickness, group, group_rate, kmt)
@@ -392,14 +418,15 @@
     )(wet, pieces[-1])
     arrived = exchange(pieces[:-1] + (kept,), there)
     evens = half // 2 - 1
-    relayed = pl.pallas_call(
+    relayed, seam = pl.pallas_call(
         functools.partial(relay_kernel, nb, tc, tpc),
-        out_shape=struct(2),
-        in_specs=[vm] * (2 + evens),
-        out_specs=vm,
+        out_shape=(struct(4 * (evens + 1) + 2), struct(2)),
+        in_specs=[vm] * (4 + evens),
+        out_specs=(vm, vm),
         compiler_params=params,
         name="relay",
-    )(up_flow, diffusivity, *arrived[:evens])
+    )(east_flow, north_flow, up_flow, diffusivity, *arrived[:evens])
+    swapped = flip(relayed, 1)
     own = pl.pallas_call(
         functools.partial(pick_kernel, nb, tc),
         out_shape=struct(2),
@@ -407,17 +434,17 @@
         out_specs=vm,
         compiler_params=params,
         name="pick",
-    )(relayed, flip(relayed, 1))
+    )(seam, swapped)
     other = flip(own, half)
     f, cells, cin, base = pl.pallas_call(
         functools.partial(solve_kernel, nb, tc, tpc, there),
         out_shape=(struct(half, tpc), struct(tpc), struct(half - 1), struct(5)),
-        in_specs=[vm] * (3 + len(arrived)),
+        in_specs=[vm] * (4 + len(arrived)),
         out_specs=(vm,) * 4,
         scratch_shapes=[pltpu.VMEM((half, tpc + EXTRA) + tile, f32)],
         compiler_params=params,
         name="solve",
-    )(wet, depth, decay, *arrived)
+    )(wet, depth, decay, swapped, *arrived)
     f_last, coef, message = pl.pallas_call(
         functools.partial(seam_kernel, half, tpc),
         out_shape=(struct(tpc), struct(3), struct(tpc + 1)),

time: 47.4 us -> 46.5 us (0.981)
  waiting for transfers between devices: 20.8 us -> 18.2 us
  Pallas kernels: 6.82 us -> 8.1 us
  starting transfers between devices: 19.4 us -> 19.9 us
    ppermute x17, waiting for transfers between devices: 20.8 us -> 18.2 us  [flip(): return lax.ppermute(value, 'lev', [(i, i ^ bits) for i in range(count)])]
    pallas_call x2 -> x3, Pallas kernels: 2.71 us -> 4.34 us  [the longest x2 4.32 us: shards(): pl.pallas_call(functools.partial(pack_kernel, nb, tc, tpc, odd), out_shap...]
    ppermute x17, starting transfers between devices: 19.4 us -> 19.9 us  [flip(): return lax.ppermute(value, 'lev', [(i, i ^ bits) for i in range(count)])]
  transfers between devices with their start and end apart: 17 -> 17, of which waited for: 10 -> 10; matrix products, arithmetic and copies ran while one was open for 0% -> 0% of each run, Pallas kernels for 6% -> 10%
where the time goes in v5:
time: 46.5 us; the launch traced here: 46.3 us
  starting transfers between devices  19.9 us (43%)
  waiting for transfers between devices  18.2 us (39%)
  Pallas kernels  8.1 us (17%)
    ppermute x17, starting transfers between devices, flip(): return lax.ppermute(value, 'lev', [(i, i ^ bits) for i in range(count)])  19.9 us
    ppermute x17, waiting for transfers between devices, flip(): return lax.ppermute(value, 'lev', [(i, i ^ bits) for i in range(count)])  18.2 us
    pallas_call x2, Pallas kernels, shards(): pl.pallas_call(functools.partial(pack_kernel, nb, tc, tpc, odd), out_shap...  4.32 us
    pallas_call x1, Pallas kernels, shards(): pl.pallas_call(functools.partial(solve_kernel, nb, tc, tpc, there), out_s...  1.53 us
    pallas_call x1, Pallas kernels, shards(): pl.pallas_call(functools.partial(join_kernel, nb, tc, tpc, home), out_sha...  1.02 us
  transfers between devices with their start and end apart: 17, of which 10 were waited for; matrix products, arithmetic and copies ran while one was open for 0% of the time, Pallas kernels for 10%

profile of v5, /device:TPU:0, one launch (start us, length us, event | category | flops | bytes accessed | tf_op | source)
XLA Modules:
  0.0 46.3 jit_solution(4583122630414876446)
XLA Ops:
  0.0 2.2 %pack.2 = (f32[37,8,128]{2,1,0:T(8,128)}, f32[37,8,128]{2,1,0:T(8,128)}, f32[37,8,128]{2,1,0:T(8,128)}, f32[37,8,128]{2,1,0:T(8,128)}) custom-call(f32[64,1,8,512]{3,2,1,0:T(8,128)} %tracer.3, f32[1,8,512]{2,1,0:T(8,128)} %east.5, f32[1,8,512]{2,1,0:T(8,128)} %north.5, f32[1,8,512]{2,1,0:T(8,128)} %up.5, f32[1,8,512]{2,1,0:T(8,128)} %diff.5, s32[8,512]{1,0:T(8,128)} %kmt.3), custom_call_target="tpu_custom_call" | custom-call | tf_op jit(solution)/shard_map/pack/pallas_call | solution.py:379
  2.2 4.0 %collective-permute-start = (f32[37,8,128]{2,1,0:T(8,128)}, f32[37,8,128]{2,1,0:T(8,128)S(1)}, u32[]{:S(2)}, u32[]{:S(2)}) collective-permute-start(f32[37,8,128]{2,1,0:T(8,128)} %get-tuple-element.36), channel_id=1, source_target_pairs={{0,6},{1,7},{2,4},{3,5},{4,2},{5,3},{6,0},{7,1},{8,14},{9,15},{10,... | collective-permute-start | bytes 454664 | tf_op jit(solution)/shard_map/ppermute | solution.py:350
  6.2 0.4 collective-permute-start.1
  6.7 0.2 collective-permute-start.2
  6.8 0.0 copy-start.1
  6.8 0.0 copy-start.2
  6.9 0.0 copy-start.3
  6.9 0.0 copy-start.4
  6.9 2.2 %pack.3 = (f32[33,8,128]{2,1,0:T(8,128)}, f32[33,8,128]{2,1,0:T(8,128)}, f32[33,8,128]{2,1,0:T(8,128)}, f32[33,8,128]{2,1,0:T(8,128)}) custom-call(f32[64,1,8,512]{3,2,1,0:T(8,128)} %tracer.3, f32[1,8,512]{2,1,0:T(8,128)} %east.5, f32[1,8,512]{2,1,0:T(8,128)} %north.5, f32[1,8,512]{2,1,0:T(8,128)} %up.5, f32[1,8,512]{2,1,0:T(8,128)} %diff.5, s32[8,512]{1,0:T(8,128)} %kmt.3), custom_call_target="tpu_custom_call" | custom-call | tf_op jit(solution)/shard_map/pack/pallas_call | solution.py:379
  9.0 1.5 %collective-permute-start.4 = (f32[33,8,128]{2,1,0:T(8,128)}, f32[33,8,128]{2,1,0:T(8,128)S(1)}, u32[]{:S(2)}, u32[]{:S(2)}) collective-permute-start(f32[33,8,128]{2,1,0:T(8,128)} %get-tuple-element.40), channel_id=1, source_target_pairs={{0,7},{1,6},{2,5},{3,4},{4,3},{5,2},{6,1},{7,0},{8,15},{9,14},{10,... | collective-permute-start | bytes 405512 | tf_op jit(solution)/shard_map/ppermute | solution.py:350
  10.5 1.6 %collective-permute-start.5 = (f32[33,8,128]{2,1,0:T(8,128)}, f32[33,8,128]{2,1,0:T(8,128)S(1)}, u32[]{:S(2)}, u32[]{:S(2)}) collective-permute-start(f32[33,8,128]{2,1,0:T(8,128)} %get-tuple-element.41), channel_id=1, source_target_pairs={{0,5},{1,4},{2,7},{3,6},{4,1},{5,0},{6,3},{7,2},{8,13},{9,12},{10,... | collective-permute-start | bytes 405512 | tf_op jit(solution)/shard_map/ppermute | solution.py:350
  12.1 0.0 collective-permute-done.refs_0_
  12.1 0.2 collective-permute-start.6
  12.3 1.6 %collective-permute-done.1.refs_1_ = f32[37,8,128]{2,1,0:T(8,128)S(1)} collective-permute-done((f32[37,8,128]{2,1,0:T(8,128)}, f32[37,8,128]{2,1,0:T(8,128)S(1)}, u32[]{:S(2)}, u32[]{:S(2)}) %collective-permute-start.1) | collective-permute-done | bytes 151584 | tf_op jit(solution)/shard_map/ppermute | solution.py:350
  13.9 0.0 collective-permute-start.7
  13.9 0.0 collective-permute-done.2.refs_2_
  13.9 0.0 copy-done.1
  13.9 0.0 copy-done.2
  13.9 0.0 copy-done.3
  14.0 0.0 copy-done.4
  14.0 0.0 copy-start
  14.0 0.6 %collective-permute-start.3 = (f32[18,8,128]{2,1,0:T(8,128)S(1)}, f32[18,8,128]{2,1,0:T(8,128)S(1)}, u32[]{:S(2)}, u32[]{:S(2)}) collective-permute-start(f32[18,8,128]{2,1,0:T(8,128)S(1)} %get-tuple-element.39), channel_id=1, source_target_pairs={{0,1},{1,0},{2,3},{3,2},{4,5},{5,4},{6,7},{7,6},{8,9},{9,8},{10,11... | collective-permute-start | bytes 221192 | tf_op jit(solution)/shard_map/ppermute | solution.py:350
  14.6 0.9 %collective-permute-done.3.swapped = f32[18,8,128]{2,1,0:T(8,128)S(1)} collective-permute-done((f32[18,8,128]{2,1,0:T(8,128)S(1)}, f32[18,8,128]{2,1,0:T(8,128)S(1)}, u32[]{:S(2)}, u32[]{:S(2)}) %collective-permute-start.3) | collective-permute-done | bytes 73760 | tf_op jit(solution)/shard_map/ppermute | solution.py:350
  15.5 0.0 copy-start.5
  15.5 0.0 copy-start.6
  15.5 0.0 copy-start.7
  15.5 0.0 copy-start.8
  15.5 2.7 %collective-permute-start.8 = (f32[2,8,128]{2,1,0:T(8,128)S(1)}, f32[2,8,128]{2,1,0:T(8,128)S(1)}, u32[]{:S(2)}, u32[]{:S(2)}) collective-permute-start(f32[2,8,128]{2,1,0:T(8,128)S(1)} %pick.1.own), channel_id=1, source_target_pairs={{0,8},{1,9},{2,10},{3,11},{4,12},{5,13},{6,14},{7,15},{8,0},{9,1},... | collective-permute-start | bytes 24584 | tf_op jit(solution)/shard_map/ppermute | solution.py:350
  18.2 0.0 copy-done.5
  18.2 0.0 copy-done.6
  18.2 0.0 copy-done.7
  18.2 0.0 copy-done.8
  18.2 0.7 %prep.1 = (f32[9,8,128]{2,1,0:T(8,128)S(1)}, f32[9,8,128]{2,1,0:T(8,128)S(1)}, f32[32,8,128]{2,1,0:T(8,128)S(1)}) custom-call(f32[16]{0:T(128)S(1)} %copy-done.7, s32[64]{0:T(128)S(1)} %copy-done.8, f32[8,16]{1,0:T(8,128)S(1)} %copy-done.6, s32[8,512]{1,0:T(8,128)S(1)} %copy-done.5), custom_call_target="tpu_custom_call" | custom-call | tf_op jit(solution)/shard_map/prep/pallas_call | solution.py:397
  18.9 0.0 copy-done
  18.9 0.2 keep.1.refs_7_
  19.1 0.0 collective-permute-done.4.refs_3_
  19.2 0.3 collective-permute-done.5.refs_4_
  19.5 0.0 collective-permute-done.6.refs_5_
  19.5 0.0 collective-permute-done.7.refs_6_
  19.5 1.5 %solve.1 = (f32[8,32,8,128]{3,2,1,0:T(8,128)S(1)}, f32[32,8,128]{2,1,0:T(8,128)S(1)}, f32[7,8,128]{2,1,0:T(8,128)S(1)}, f32[5,8,128]{2,1,0:T(8,128)S(1)}) custom-call(f32[9,8,128]{2,1,0:T(8,128)S(1)} %get-tuple-element.33.prepared.wets, f32[9,8,128]{2,1,0:T(8,128)S(1)} %get-tuple-element.34.depths, f32[32,8,128]{2,1,0:T(8,128)S(1)} %get-tuple-element.35.decay, ...), custom_call_target="tpu_custom_call" | custom-call | tf_op jit(solution)/shard_map/solve/pallas_call | solution.py:439
  21.0 0.0 collective-permute-done.8.other
  21.0 0.1 seam.1
  21.1 2.7 %collective-permute-start.9 = (f32[33,8,128]{2,1,0:T(8,128)S(1)}, f32[33,8,128]{2,1,0:T(8,128)S(1)}, u32[]{:S(2)}, u32[]{:S(2)}) collective-permute-start(f32[33,8,128]{2,1,0:T(8,128)S(1)} %get-tuple-element.52.sent), channel_id=1, source_target_pairs={{0,8},{1,9},{2,10},{3,11},{4,12},{5,13},{6,14},{7,15},{8,0},{9,1},... | collective-permute-start | bytes 405512 | tf_op jit(solution)/shard_map/ppermute | solution.py:350
  23.7 7.0 %collective-permute-done.9.got = f32[33,8,128]{2,1,0:T(8,128)S(1)} collective-permute-done((f32[33,8,128]{2,1,0:T(8,128)S(1)}, f32[33,8,128]{2,1,0:T(8,128)S(1)}, u32[]{:S(2)}, u32[]{:S(2)}) %collective-permute-start.9) | collective-permute-done | bytes 135200 | tf_op jit(solution)/shard_map/ppermute | solution.py:350
  30.8 0.2 back.1
  31.0 1.5 %collective-permute-start.10 = (f32[32,8,128]{2,1,0:T(8,128)S(1)}, f32[32,8,128]{2,1,0:T(8,128)S(1)}, u32[]{:S(2)}, u32[]{:S(2)}) collective-permute-start(f32[32,8,128]{2,1,0:T(8,128)S(1)} %get-tuple-element.53), channel_id=1, source_target_pairs={{0,6},{1,7},{2,4},{3,5},{4,2},{5,3},{6,0},{7,1},{8,14},{9,15},{10,... | collective-permute-start | bytes 393224 | tf_op jit(solution)/shard_map/ppermute | solution.py:350
  32.5 1.4 %collective-permute-start.11 = (f32[32,8,128]{2,1,0:T(8,128)S(1)}, f32[32,8,128]{2,1,0:T(8,128)S(1)}, u32[]{:S(2)}, u32[]{:S(2)}) collective-permute-start(f32[32,8,128]{2,1,0:T(8,128)S(1)} %get-tuple-element.54), channel_id=1, source_target_pairs={{0,4},{1,5},{2,6},{3,7},{4,0},{5,1},{6,2},{7,3},{8,12},{9,13},{10,... | collective-permute-start | bytes 393224 | tf_op jit(solution)/shard_map/ppermute | solution.py:350
  33.8 0.7 %collective-permute-start.12 = (f32[32,8,128]{2,1,0:T(8,128)S(1)}, f32[32,8,128]{2,1,0:T(8,128)S(1)}, u32[]{:S(2)}, u32[]{:S(2)}) collective-permute-start(f32[32,8,128]{2,1,0:T(8,128)S(1)} %get-tuple-element.55), channel_id=1, source_target_pairs={{0,2},{1,3},{2,0},{3,1},{4,6},{5,7},{6,4},{7,5},{8,10},{9,11},{10,... | collective-permute-start | bytes 393224 | tf_op jit(solution)/shard_map/ppermute | solution.py:350
  34.5 0.2 collective-permute-start.13
  34.7 2.3 %collective-permute-start.14 = (f32[32,8,128]{2,1,0:T(8,128)S(1)}, f32[32,8,128]{2,1,0:T(8,128)S(1)}, u32[]{:S(2)}, u32[]{:S(2)}) collective-permute-start(f32[32,8,128]{2,1,0:T(8,128)S(1)} %get-tuple-element.57), channel_id=1, source_target_pairs={{0,5},{1,4},{2,7},{3,6},{4,1},{5,0},{6,3},{7,2},{8,13},{9,12},{10,... | collective-permute-start | bytes 393224 | tf_op jit(solution)/shard_map/ppermute | solution.py:350
  37.0 1.3 %collective-permute-done.10.refs_0_ = f32[32,8,128]{2,1,0:T(8,128)S(1)} collective-permute-done((f32[32,8,128]{2,1,0:T(8,128)S(1)}, f32[32,8,128]{2,1,0:T(8,128)S(1)}, u32[]{:S(2)}, u32[]{:S(2)}) %collective-permute-start.10) | collective-permute-done | bytes 131104 | tf_op jit(solution)/shard_map/ppermute | solution.py:350
  38.3 0.0 collective-permute-start.15
  38.3 1.9 %collective-permute-done.11.refs_1_ = f32[32,8,128]{2,1,0:T(8,128)S(1)} collective-permute-done((f32[32,8,128]{2,1,0:T(8,128)S(1)}, f32[32,8,128]{2,1,0:T(8,128)S(1)}, u32[]{:S(2)}, u32[]{:S(2)}) %collective-permute-start.11) | collective-permute-done | bytes 131104 | tf_op jit(solution)/shard_map/ppermute | solution.py:350
  40.2 0.0 collective-permute-start.16
  40.2 0.7 %collective-permute-done.12.refs_2_ = f32[32,8,128]{2,1,0:T(8,128)S(1)} collective-permute-done((f32[32,8,128]{2,1,0:T(8,128)S(1)}, f32[32,8,128]{2,1,0:T(8,128)S(1)}, u32[]{:S(2)}, u32[]{:S(2)}) %collective-permute-start.12) | collective-permute-done | bytes 131104 | tf_op jit(solution)/shard_map/ppermute | solution.py:350
  40.9 1.1 %collective-permute-done.13.refs_3_ = f32[32,8,128]{2,1,0:T(8,128)S(1)} collective-permute-done((f32[32,8,128]{2,1,0:T(8,128)S(1)}, f32[32,8,128]{2,1,0:T(8,128)S(1)}, u32[]{:S(2)}, u32[]{:S(2)}) %collective-permute-start.13) | collective-permute-done | bytes 131104 | tf_op jit(solution)/shard_map/ppermute | solution.py:350
  42.0 2.0 %collective-permute-done.14.refs_4_ = f32[32,8,128]{2,1,0:T(8,128)S(1)} collective-permute-done((f32[32,8,128]{2,1,0:T(8,128)S(1)}, f32[32,8,128]{2,1,0:T(8,128)S(1)}, u32[]{:S(2)}, u32[]{:S(2)}) %collective-permute-start.14) | collective-permute-done | bytes 131104 | tf_op jit(solution)/shard_map/ppermute | solution.py:350
  44.0 1.4 %collective-permute-done.15.refs_5_ = f32[32,8,128]{2,1,0:T(8,128)S(1)} collective-permute-done((f32[32,8,128]{2,1,0:T(8,128)S(1)}, f32[32,8,128]{2,1,0:T(8,128)S(1)}, u32[]{:S(2)}, u32[]{:S(2)}) %collective-permute-start.15) | collective-permute-done | bytes 131104 | tf_op jit(solution)/shard_map/ppermute | solution.py:350
  45.3 0.0 collective-permute-done.16.refs_6_
  45.3 1.0 %join.1 = f32[64,1,8,512]{3,2,1,0:T(8,128)} custom-call(f32[32,8,128]{2,1,0:T(8,128)S(1)} %collective-permute-done.10.refs_0_, f32[32,8,128]{2,1,0:T(8,128)S(1)} %collective-permute-done.11.refs_1_, f32[32,8,128]{2,1,0:T(8,128)S(1)} %collective-permute-done.12.refs_2_, f32[32,8,128]{2,1,0:T(8,128)S(1)} %collective-permute-done.13.refs_3_, ...), custom_call_target="tpu_custom_call" | custom-call | tf_op jit(solution)/shard_map/join/pallas_call | solution.py:466
  (2 shorter events, 0.0 us)
Async XLA Ops:
  2.2 10.0 %collective-permute-start = (f32[37,8,128]{2,1,0:T(8,128)}, f32[37,8,128]{2,1,0:T(8,128)S(1)}, u32[]{:S(2)}, u32[]{:S(2)}) collective-permute-start(f32[37,8,128]{2,1,0:T(8,128)} %get-tuple-element.36), channel_id=1, source_target_pairs={{0,6},{1,7},{2,4},{3,5},{4,2},{5,3},{6,0},{7,1},{8,14},{9,15},{10,... | collective-permute-start | bytes 454664 | tf_op jit(solution)/shard_map/ppermute | solution.py:350
  6.2 7.7 %collective-permute-start.1 = (f32[37,8,128]{2,1,0:T(8,128)}, f32[37,8,128]{2,1,0:T(8,128)S(1)}, u32[]{:S(2)}, u32[]{:S(2)}) collective-permute-start(f32[37,8,128]{2,1,0:T(8,128)} %get-tuple-element.37), channel_id=1, source_target_pairs={{0,4},{1,5},{2,6},{3,7},{4,0},{5,1},{6,2},{7,3},{8,12},{9,13},{10,... | collective-permute-start | bytes 454664 | tf_op jit(solution)/shard_map/ppermute | solution.py:350
  6.7 7.3 %collective-permute-start.2 = (f32[37,8,128]{2,1,0:T(8,128)}, f32[37,8,128]{2,1,0:T(8,128)S(1)}, u32[]{:S(2)}, u32[]{:S(2)}) collective-permute-start(f32[37,8,128]{2,1,0:T(8,128)} %get-tuple-element.38), channel_id=1, source_target_pairs={{0,2},{1,3},{2,0},{3,1},{4,6},{5,7},{6,4},{7,5},{8,10},{9,11},{10,... | collective-permute-start | bytes 454664 | tf_op jit(solution)/shard_map/ppermute | solution.py:350
  6.8 7.1 %copy-start.1 = (f32[1,8,512]{2,1,0:T(8,128)S(1)}, f32[1,8,512]{2,1,0:T(8,128)}, u32[]{:S(2)}) copy-start(f32[1,8,512]{2,1,0:T(8,128)} %east.5) | copy-start | bytes 49156
  6.8 7.1 %copy-start.2 = (f32[1,8,512]{2,1,0:T(8,128)S(1)}, f32[1,8,512]{2,1,0:T(8,128)}, u32[]{:S(2)}) copy-start(f32[1,8,512]{2,1,0:T(8,128)} %north.5) | copy-start | bytes 49156
  6.9 7.1 %copy-start.3 = (f32[1,8,512]{2,1,0:T(8,128)S(1)}, f32[1,8,512]{2,1,0:T(8,128)}, u32[]{:S(2)}) copy-start(f32[1,8,512]{2,1,0:T(8,128)} %up.5) | copy-start | bytes 49156
  6.9 7.1 %copy-start.4 = (f32[1,8,512]{2,1,0:T(8,128)S(1)}, f32[1,8,512]{2,1,0:T(8,128)}, u32[]{:S(2)}) copy-start(f32[1,8,512]{2,1,0:T(8,128)} %diff.5) | copy-start | bytes 49156
  9.0 10.1 %collective-permute-start.4 = (f32[33,8,128]{2,1,0:T(8,128)}, f32[33,8,128]{2,1,0:T(8,128)S(1)}, u32[]{:S(2)}, u32[]{:S(2)}) collective-permute-start(f32[33,8,128]{2,1,0:T(8,128)} %get-tuple-element.40), channel_id=1, source_target_pairs={{0,7},{1,6},{2,5},{3,4},{4,3},{5,2},{6,1},{7,0},{8,15},{9,14},{10,... | collective-permute-start | bytes 405512 | tf_op jit(solution)/shard_map/ppermute | solution.py:350
  10.5 8.9 %collective-permute-start.5 = (f32[33,8,128]{2,1,0:T(8,128)}, f32[33,8,128]{2,1,0:T(8,128)S(1)}, u32[]{:S(2)}, u32[]{:S(2)}) collective-permute-start(f32[33,8,128]{2,1,0:T(8,128)} %get-tuple-element.41), channel_id=1, source_target_pairs={{0,5},{1,4},{2,7},{3,6},{4,1},{5,0},{6,3},{7,2},{8,13},{9,12},{10,... | collective-permute-start | bytes 405512 | tf_op jit(solution)/shard_map/ppermute | solution.py:350
  12.1 7.4 %collective-permute-start.6 = (f32[33,8,128]{2,1,0:T(8,128)}, f32[33,8,128]{2,1,0:T(8,128)S(1)}, u32[]{:S(2)}, u32[]{:S(2)}) collective-permute-start(f32[33,8,128]{2,1,0:T(8,128)} %get-tuple-element.42), channel_id=1, source_target_pairs={{0,3},{1,2},{2,1},{3,0},{4,7},{5,6},{6,5},{7,4},{8,11},{9,10},{10,... | collective-permute-start | bytes 405512 | tf_op jit(solution)/shard_map/ppermute | solution.py:350
  13.9 5.6 %collective-permute-start.7 = (f32[33,8,128]{2,1,0:T(8,128)}, f32[33,8,128]{2,1,0:T(8,128)S(1)}, u32[]{:S(2)}, u32[]{:S(2)}) collective-permute-start(f32[33,8,128]{2,1,0:T(8,128)} %get-tuple-element.43), channel_id=1, source_target_pairs={{0,1},{1,0},{2,3},{3,2},{4,5},{5,4},{6,7},{7,6},{8,9},{9,8},{10,11... | collective-permute-start | bytes 405512 | tf_op jit(solution)/shard_map/ppermute | solution.py:350
  14.0 5.0 %copy-start = (f32[37,8,128]{2,1,0:T(8,128)S(1)}, f32[37,8,128]{2,1,0:T(8,128)}, u32[]{:S(2)}) copy-start(f32[37,8,128]{2,1,0:T(8,128)} %get-tuple-element.44.piece) | copy-start | bytes 454660
  14.0 1.5 %collective-permute-start.3 = (f32[18,8,128]{2,1,0:T(8,128)S(1)}, f32[18,8,128]{2,1,0:T(8,128)S(1)}, u32[]{:S(2)}, u32[]{:S(2)}) collective-permute-start(f32[18,8,128]{2,1,0:T(8,128)S(1)} %get-tuple-element.39), channel_id=1, source_target_pairs={{0,1},{1,0},{2,3},{3,2},{4,5},{5,4},{6,7},{7,6},{8,9},{9,8},{10,11... | collective-permute-start | bytes 221192 | tf_op jit(solution)/shard_map/ppermute | solution.py:350
  15.5 2.7 %copy-start.5 = (s32[8,512]{1,0:T(8,128)S(1)}, s32[8,512]{1,0:T(8,128)}, u32[]{:S(2)}) copy-start(s32[8,512]{1,0:T(8,128)} %kmt.3) | copy-start | bytes 49156
  15.5 2.7 %copy-start.6 = (f32[8,16]{1,0:T(8,128)S(1)}, f32[8,16]{1,0:T(8,128)}, u32[]{:S(2)}) copy-start(f32[8,16]{1,0:T(8,128)} %rates.1) | copy-start | bytes 1540
  15.5 2.7 %copy-start.7 = (f32[16]{0:T(128)S(1)}, f32[16]{0:T(128)}, u32[]{:S(2)}) copy-start(f32[16]{0:T(128)} %thickness.1) | copy-start | bytes 196
  15.5 2.7 %copy-start.8 = (s32[64]{0:T(128)S(1)}, s32[64]{0:T(128)}, u32[]{:S(2)}) copy-start(s32[64]{0:T(128)} %group.1) | copy-start | bytes 772
  15.5 5.5 %collective-permute-start.8 = (f32[2,8,128]{2,1,0:T(8,128)S(1)}, f32[2,8,128]{2,1,0:T(8,128)S(1)}, u32[]{:S(2)}, u32[]{:S(2)}) collective-permute-start(f32[2,8,128]{2,1,0:T(8,128)S(1)} %pick.1.own), channel_id=1, source_target_pairs={{0,8},{1,9},{2,10},{3,11},{4,12},{5,13},{6,14},{7,15},{8,0},{9,1},... | collective-permute-start | bytes 24584 | tf_op jit(solution)/shard_map/ppermute | solution.py:350
  21.1 9.7 %collective-permute-start.9 = (f32[33,8,128]{2,1,0:T(8,128)S(1)}, f32[33,8,128]{2,1,0:T(8,128)S(1)}, u32[]{:S(2)}, u32[]{:S(2)}) collective-permute-start(f32[33,8,128]{2,1,0:T(8,128)S(1)} %get-tuple-element.52.sent), channel_id=1, source_target_pairs={{0,8},{1,9},{2,10},{3,11},{4,12},{5,13},{6,14},{7,15},{8,0},{9,1},... | collective-permute-start | bytes 405512 | tf_op jit(solution)/shard_map/ppermute | solution.py:350
  31.0 7.3 %collective-permute-start.10 = (f32[32,8,128]{2,1,0:T(8,128)S(1)}, f32[32,8,128]{2,1,0:T(8,128)S(1)}, u32[]{:S(2)}, u32[]{:S(2)}) collective-permute-start(f32[32,8,128]{2,1,0:T(8,128)S(1)} %get-tuple-element.53), channel_id=1, source_target_pairs={{0,6},{1,7},{2,4},{3,5},{4,2},{5,3},{6,0},{7,1},{8,14},{9,15},{10,... | collective-permute-start | bytes 393224 | tf_op jit(solution)/shard_map/ppermute | solution.py:350
  32.5 7.7 %collective-permute-start.11 = (f32[32,8,128]{2,1,0:T(8,128)S(1)}, f32[32,8,128]{2,1,0:T(8,128)S(1)}, u32[]{:S(2)}, u32[]{:S(2)}) collective-permute-start(f32[32,8,128]{2,1,0:T(8,128)S(1)} %get-tuple-element.54), channel_id=1, source_target_pairs={{0,4},{1,5},{2,6},{3,7},{4,0},{5,1},{6,2},{7,3},{8,12},{9,13},{10,... | collective-permute-start | bytes 393224 | tf_op jit(solution)/shard_map/ppermute | solution.py:350
  33.8 7.1 %collective-permute-start.12 = (f32[32,8,128]{2,1,0:T(8,128)S(1)}, f32[32,8,128]{2,1,0:T(8,128)S(1)}, u32[]{:S(2)}, u32[]{:S(2)}) collective-permute-start(f32[32,8,128]{2,1,0:T(8,128)S(1)} %get-tuple-element.55), channel_id=1, source_target_pairs={{0,2},{1,3},{2,0},{3,1},{4,6},{5,7},{6,4},{7,5},{8,10},{9,11},{10,... | collective-permute-start | bytes 393224 | tf_op jit(solution)/shard_map/ppermute | solution.py:350
  34.5 7.4 %collective-permute-start.13 = (f32[32,8,128]{2,1,0:T(8,128)S(1)}, f32[32,8,128]{2,1,0:T(8,128)S(1)}, u32[]{:S(2)}, u32[]{:S(2)}) collective-permute-start(f32[32,8,128]{2,1,0:T(8,128)S(1)} %get-tuple-element.56), channel_id=1, source_target_pairs={{0,7},{1,6},{2,5},{3,4},{4,3},{5,2},{6,1},{7,0},{8,15},{9,14},{10,... | collective-permute-start | bytes 393224 | tf_op jit(solution)/shard_map/ppermute | solution.py:350
  34.7 9.2 %collective-permute-start.14 = (f32[32,8,128]{2,1,0:T(8,128)S(1)}, f32[32,8,128]{2,1,0:T(8,128)S(1)}, u32[]{:S(2)}, u32[]{:S(2)}) collective-permute-start(f32[32,8,128]{2,1,0:T(8,128)S(1)} %get-tuple-element.57), channel_id=1, source_target_pairs={{0,5},{1,4},{2,7},{3,6},{4,1},{5,0},{6,3},{7,2},{8,13},{9,12},{10,... | collective-permute-start | bytes 393224 | tf_op jit(solution)/shard_map/ppermute | solution.py:350
  38.3 7.0 %collective-permute-start.15 = (f32[32,8,128]{2,1,0:T(8,128)S(1)}, f32[32,8,128]{2,1,0:T(8,128)S(1)}, u32[]{:S(2)}, u32[]{:S(2)}) collective-permute-start(f32[32,8,128]{2,1,0:T(8,128)S(1)} %get-tuple-element.58), channel_id=1, source_target_pairs={{0,3},{1,2},{2,1},{3,0},{4,7},{5,6},{6,5},{7,4},{8,11},{9,10},{10,... | collective-permute-start | bytes 393224 | tf_op jit(solution)/shard_map/ppermute | solution.py:350
  40.2 5.1 %collective-permute-start.16 = (f32[32,8,128]{2,1,0:T(8,128)S(1)}, f32[32,8,128]{2,1,0:T(8,128)S(1)}, u32[]{:S(2)}, u32[]{:S(2)}) collective-permute-start(f32[32,8,128]{2,1,0:T(8,128)S(1)} %get-tuple-element.59), channel_id=1, source_target_pairs={{0,1},{1,0},{2,3},{3,2},{4,5},{5,4},{6,7},{7,6},{8,9},{9,8},{10,11... | collective-permute-start | bytes 393224 | tf_op jit(solution)/shard_map/ppermute | solution.py:350

commit v6 on v5

--- a/solution.py
+++ b/solution.py
@@ -83,17 +83,15 @@
     ]
     for copy in chunks + loads:
         copy.start()
-    for copy in chunks:
-        copy.wait()
     stores = []
     for d in distances:
         cut = pl.ds(pl.multiple_of(lax.div(rank ^ d, tc) * LANES, LANES), LANES)
         copy = pltpu.make_async_copy(
-            cells.at[pl.ds(d % tc // 2 * tpc, tpc), :, cut], out[d].at[pl.ds(0, tpc)], store_sem.at[0, d // 2]
+            tracer.at[pl.ds((chunk ^ d % tc) * tpc, tpc), 0, :, cut], out[d].at[pl.ds(0, tpc)], store_sem.at[d // 2]
         )
         copy.start()
         stores.append(copy)
-    for copy in loads:
+    for copy in chunks + loads:
         copy.wait()
     lane = lanes_iota()
     cols = [slice(b * LANES, (b + 1) * LANES) for b in range(nb)]
@@ -117,27 +115,16 @@
             edge = faces[b]
             if b + 1 < nb:
                 edge = edge - pltpu.roll(faces[b + 1], LANES - 1, 1)
-            extra[e // 2, b, EDGE] = edge
-            if not odd:
-                for i in range(4):
-                    extra[e // 2, b, EAST + i] = fields[i, :, cols[b]]
+            extra[e // 2, b] = edge
     for d in distances:
-        copy = pltpu.make_async_copy(
-            extra.at[d % tc // 2, lax.div(rank ^ d, tc), pl.ds(0, n_extra(d))],
-            out[d].at[pl.ds(tpc, n_extra(d))],
-            store_sem.at[1, d // 2],
-        )
-        copy.start()
-        stores.append(copy)
+        block = lax.div(rank ^ d, tc)
+        cut = pl.ds(pl.multiple_of(block * LANES, LANES), LANES)
+        out[d][tpc + EDGE] = extra[d % tc // 2, block]
+        if not odd:
+            for i in range(4):
+                out[d][tpc + EAST + i] = fields[i, :, cut]
     for copy in stores:
         copy.wait()
-
-
-def keep_kernel(prepared, piece, own, sem):
-    del prepared
-    copy = pltpu.make_async_copy(piece, own, sem.at[0])
-    copy.start()
-    copy.wait()
 
 
 def relay_kernel(nb, tc, tpc, east, north, up, diff, *refs):
@@ -374,24 +361,28 @@
 
     there, home = pairing(half, THERE), pairing(half, HOME)
     packed = {}
+    held = [
+        pltpu.with_memory_space_constraint(value, pltpu.HBM)
+        for value in (tracer, east_flow, north_flow, up_flow, diffusivity, kmt)
+    ]
     for odd in range(2):
         distances = [d for d in devices(half) if d % 2 == odd]
         pieces = pl.pallas_call(
             functools.partial(pack_kernel, nb, tc, tpc, odd),
-            out_shape=tuple(struct(tpc + n_extra(d)) for d in distances),
+            out_shape=tuple(pltpu.VMEM((tpc + n_extra(d),) + tile, f32) for d in distances),
             in_specs=[hbm] * 6,
-            out_specs=(hbm,) * len(distances),
+            out_specs=(vm,) * len(distances),
             scratch_shapes=[
                 pltpu.VMEM((ntr // 2, ny, nx), f32),
                 pltpu.VMEM((4, ny, nx), f32),
                 pltpu.VMEM((ny, nx), jnp.int32),
-                pltpu.VMEM((tc // 2, nb, EXTRA) + tile, f32),
+                pltpu.VMEM((tc // 2, nb) + tile, f32),
                 pltpu.SemaphoreType.DMA((5 + tc // 2,)),
-                pltpu.SemaphoreType.DMA((2, half // 2)),
+                pltpu.SemaphoreType.DMA((half // 2,)),
             ],
-            compiler_params=pltpu.CompilerParams(vmem_limit_bytes=PACK_LIMIT),
+            compiler_params=params,
             name="pack",
-        )(tracer, east_flow, north_flow, up_flow, diffusivity, kmt)
+        )(*held)
         packed.update(zip(distances, pieces))
     pieces = tuple(packed[d] for d in devices(half))
     wet, depth, decay = pl.pallas_call(
@@ -407,16 +398,7 @@
         compiler_params=params,
         name="prep",
     )(thickness, group, group_rate, kmt)
-    kept = pl.pallas_call(
-        keep_kernel,
-        out_shape=struct(tpc + EXTRA),
-        in_specs=[anywhere] * 2,
-        out_specs=vm,
-        scratch_shapes=[pltpu.SemaphoreType.DMA((1,))],
-        compiler_params=params,
-        name="keep",
-    )(wet, pieces[-1])
-    arrived = exchange(pieces[:-1] + (kept,), there)
+    arrived = exchange(pieces, there)
     evens = half // 2 - 1
     relayed, seam = pl.pallas_call(
         functools.partial(relay_kernel, nb, tc, tpc),

time: 46.5 us -> 45.1 us (0.970)
  Pallas kernels: 8.1 us -> 6.73 us
    pallas_call x2, Pallas kernels: 4.32 us -> 3.15 us  [shards(): pl.pallas_call(functools.partial(pack_kernel, nb, tc, tpc, odd), out_shap...]
  transfers between devices with their start and end apart: 17 -> 17, of which waited for: 10 -> 9; matrix products, arithmetic and copies ran while one was open for 0% -> 0% of each run, Pallas kernels for 10% -> 9%
where the time goes in v6:
time: 45.1 us; the launch traced here: 45 us
  starting transfers between devices  20.1 us (45%)
  waiting for transfers between devices  18 us (40%)
  Pallas kernels  6.73 us (15%)
    ppermute x17, starting transfers between devices, flip(): return lax.ppermute(value, 'lev', [(i, i ^ bits) for i in range(count)])  20.1 us
    ppermute x17, waiting for transfers between devices, flip(): return lax.ppermute(value, 'lev', [(i, i ^ bits) for i in range(count)])  18 us
    pallas_call x2, Pallas kernels, shards(): pl.pallas_call(functools.partial(pack_kernel, nb, tc, tpc, odd), out_shap...  3.15 us
    pallas_call x1, Pallas kernels, shards(): pl.pallas_call(functools.partial(solve_kernel, nb, tc, tpc, there), out_s...  1.53 us
    pallas_call x1, Pallas kernels, shards(): pl.pallas_call(functools.partial(join_kernel, nb, tc, tpc, home), out_sha...  1.02 us
  transfers between devices with their start and end apart: 17, of which 9 were waited for; matrix products, arithmetic and copies ran while one was open for 0% of the time, Pallas kernels for 9%

profile of v6, /device:TPU:0, one launch (start us, length us, event | category | flops | bytes accessed | tf_op | source)
XLA Modules:
  0.0 45.0 jit_solution(1937480185000872223)
XLA Ops:
  0.0 1.5 %pack.2 = (f32[37,8,128]{2,1,0:T(8,128)S(1)}, f32[37,8,128]{2,1,0:T(8,128)S(1)}, f32[37,8,128]{2,1,0:T(8,128)S(1)}, f32[37,8,128]{2,1,0:T(8,128)S(1)}) custom-call(f32[64,1,8,512]{3,2,1,0:T(8,128)} %tracer.3, f32[1,8,512]{2,1,0:T(8,128)} %east.5, f32[1,8,512]{2,1,0:T(8,128)} %north.5, f32[1,8,512]{2,1,0:T(8,128)} %up.5, f32[1,8,512]{2,1,0:T(8,128)} %diff.5, ...), custom_call_target="tpu_custom_call" | custom-call | tf_op jit(solution)/shard_map/pack/pallas_call | solution.py:370
  1.5 4.1 %collective-permute-start = (f32[37,8,128]{2,1,0:T(8,128)S(1)}, f32[37,8,128]{2,1,0:T(8,128)S(1)}, u32[]{:S(2)}, u32[]{:S(2)}) collective-permute-start(f32[37,8,128]{2,1,0:T(8,128)S(1)} %get-tuple-element.36), channel_id=1, source_target_pairs={{0,6},{1,7},{2,4},{3,5},{4,2},{5,3},{6,0},{7,1},{8,14},{9,15},{10,... | collective-permute-start | bytes 454664 | tf_op jit(solution)/shard_map/ppermute | solution.py:337
  5.7 0.3 collective-permute-start.1
  6.0 0.3 collective-permute-start.2
  6.3 0.0 copy-start
  6.3 0.0 copy-start.1
  6.3 0.0 copy-start.2
  6.3 0.0 copy-start.3
  6.4 1.6 %pack.3 = (f32[33,8,128]{2,1,0:T(8,128)S(1)}, f32[33,8,128]{2,1,0:T(8,128)S(1)}, f32[33,8,128]{2,1,0:T(8,128)S(1)}, f32[33,8,128]{2,1,0:T(8,128)S(1)}) custom-call(f32[64,1,8,512]{3,2,1,0:T(8,128)} %tracer.3, f32[1,8,512]{2,1,0:T(8,128)} %east.5, f32[1,8,512]{2,1,0:T(8,128)} %north.5, f32[1,8,512]{2,1,0:T(8,128)} %up.5, f32[1,8,512]{2,1,0:T(8,128)} %diff.5, ...), custom_call_target="tpu_custom_call" | custom-call | tf_op jit(solution)/shard_map/pack/pallas_call | solution.py:370
  8.0 1.4 %collective-permute-start.4 = (f32[33,8,128]{2,1,0:T(8,128)S(1)}, f32[33,8,128]{2,1,0:T(8,128)S(1)}, u32[]{:S(2)}, u32[]{:S(2)}) collective-permute-start(f32[33,8,128]{2,1,0:T(8,128)S(1)} %get-tuple-element.40), channel_id=1, source_target_pairs={{0,7},{1,6},{2,5},{3,4},{4,3},{5,2},{6,1},{7,0},{8,15},{9,14},{10,... | collective-permute-start | bytes 405512 | tf_op jit(solution)/shard_map/ppermute | solution.py:337
  9.4 1.6 %collective-permute-start.5 = (f32[33,8,128]{2,1,0:T(8,128)S(1)}, f32[33,8,128]{2,1,0:T(8,128)S(1)}, u32[]{:S(2)}, u32[]{:S(2)}) collective-permute-start(f32[33,8,128]{2,1,0:T(8,128)S(1)} %get-tuple-element.41), channel_id=1, source_target_pairs={{0,5},{1,4},{2,7},{3,6},{4,1},{5,0},{6,3},{7,2},{8,13},{9,12},{10,... | collective-permute-start | bytes 405512 | tf_op jit(solution)/shard_map/ppermute | solution.py:337
  10.9 0.0 collective-permute-done.refs_0_
  10.9 0.3 collective-permute-start.6
  11.2 2.4 %collective-permute-done.1.refs_1_ = f32[37,8,128]{2,1,0:T(8,128)S(1)} collective-permute-done((f32[37,8,128]{2,1,0:T(8,128)S(1)}, f32[37,8,128]{2,1,0:T(8,128)S(1)}, u32[]{:S(2)}, u32[]{:S(2)}) %collective-permute-start.1) | collective-permute-done | bytes 151584 | tf_op jit(solution)/shard_map/ppermute | solution.py:337
  13.6 0.0 collective-permute-start.7
  13.6 0.0 collective-permute-done.2.refs_2_
  13.6 0.0 copy-done
  13.6 0.0 copy-done.1
  13.6 0.0 copy-done.2
  13.6 0.0 copy-done.3
  13.7 0.6 %collective-permute-start.3 = (f32[18,8,128]{2,1,0:T(8,128)S(1)}, f32[18,8,128]{2,1,0:T(8,128)S(1)}, u32[]{:S(2)}, u32[]{:S(2)}) collective-permute-start(f32[18,8,128]{2,1,0:T(8,128)S(1)} %get-tuple-element.39), channel_id=1, source_target_pairs={{0,1},{1,0},{2,3},{3,2},{4,5},{5,4},{6,7},{7,6},{8,9},{9,8},{10,11... | collective-permute-start | bytes 221192 | tf_op jit(solution)/shard_map/ppermute | solution.py:337
  14.2 0.9 %collective-permute-done.3.swapped = f32[18,8,128]{2,1,0:T(8,128)S(1)} collective-permute-done((f32[18,8,128]{2,1,0:T(8,128)S(1)}, f32[18,8,128]{2,1,0:T(8,128)S(1)}, u32[]{:S(2)}, u32[]{:S(2)}) %collective-permute-start.3) | collective-permute-done | bytes 73760 | tf_op jit(solution)/shard_map/ppermute | solution.py:337
  15.2 0.0 copy-start.4
  15.2 0.0 copy-start.5
  15.2 0.0 copy-start.6
  15.2 0.0 copy-start.7
  15.2 2.7 %collective-permute-start.8 = (f32[2,8,128]{2,1,0:T(8,128)S(1)}, f32[2,8,128]{2,1,0:T(8,128)S(1)}, u32[]{:S(2)}, u32[]{:S(2)}) collective-permute-start(f32[2,8,128]{2,1,0:T(8,128)S(1)} %pick.1.own), channel_id=1, source_target_pairs={{0,8},{1,9},{2,10},{3,11},{4,12},{5,13},{6,14},{7,15},{8,0},{9,1},... | collective-permute-start | bytes 24584 | tf_op jit(solution)/shard_map/ppermute | solution.py:337
  17.8 0.0 copy-done.4
  17.8 0.0 copy-done.5
  17.8 0.0 copy-done.6
  17.8 0.0 copy-done.7
  17.9 0.7 %prep.1 = (f32[9,8,128]{2,1,0:T(8,128)S(1)}, f32[9,8,128]{2,1,0:T(8,128)S(1)}, f32[32,8,128]{2,1,0:T(8,128)S(1)}) custom-call(f32[16]{0:T(128)S(1)} %copy-done.6, s32[64]{0:T(128)S(1)} %copy-done.7, f32[8,16]{1,0:T(8,128)S(1)} %copy-done.5, s32[8,512]{1,0:T(8,128)S(1)} %copy-done.4), custom_call_target="tpu_custom_call" | custom-call | tf_op jit(solution)/shard_map/prep/pallas_call | solution.py:388
  18.6 0.0 collective-permute-done.4.refs_3_
  18.6 0.0 collective-permute-done.5.refs_4_
  18.6 0.0 collective-permute-done.6.refs_5_
  18.6 0.0 collective-permute-done.7.refs_6_
  18.6 1.5 %solve.1 = (f32[8,32,8,128]{3,2,1,0:T(8,128)S(1)}, f32[32,8,128]{2,1,0:T(8,128)S(1)}, f32[7,8,128]{2,1,0:T(8,128)S(1)}, f32[5,8,128]{2,1,0:T(8,128)S(1)}) custom-call(f32[9,8,128]{2,1,0:T(8,128)S(1)} %get-tuple-element.33.wets, f32[9,8,128]{2,1,0:T(8,128)S(1)} %get-tuple-element.34.depths, f32[32,8,128]{2,1,0:T(8,128)S(1)} %get-tuple-element.35.decay, ...), custom_call_target="tpu_custom_call" | custom-call | tf_op jit(solution)/shard_map/solve/pallas_call | solution.py:421
  20.2 0.0 collective-permute-done.8.other
  20.2 0.1 seam.1
  20.2 2.7 %collective-permute-start.9 = (f32[33,8,128]{2,1,0:T(8,128)S(1)}, f32[33,8,128]{2,1,0:T(8,128)S(1)}, u32[]{:S(2)}, u32[]{:S(2)}) collective-permute-start(f32[33,8,128]{2,1,0:T(8,128)S(1)} %get-tuple-element.52.sent), channel_id=1, source_target_pairs={{0,8},{1,9},{2,10},{3,11},{4,12},{5,13},{6,14},{7,15},{8,0},{9,1},... | collective-permute-start | bytes 405512 | tf_op jit(solution)/shard_map/ppermute | solution.py:337
  22.9 6.8 %collective-permute-done.9.got = f32[33,8,128]{2,1,0:T(8,128)S(1)} collective-permute-done((f32[33,8,128]{2,1,0:T(8,128)S(1)}, f32[33,8,128]{2,1,0:T(8,128)S(1)}, u32[]{:S(2)}, u32[]{:S(2)}) %collective-permute-start.9) | collective-permute-done | bytes 135200 | tf_op jit(solution)/shard_map/ppermute | solution.py:337
  29.7 0.2 back.1
  29.9 1.6 %collective-permute-start.10 = (f32[32,8,128]{2,1,0:T(8,128)S(1)}, f32[32,8,128]{2,1,0:T(8,128)S(1)}, u32[]{:S(2)}, u32[]{:S(2)}) collective-permute-start(f32[32,8,128]{2,1,0:T(8,128)S(1)} %get-tuple-element.53), channel_id=1, source_target_pairs={{0,6},{1,7},{2,4},{3,5},{4,2},{5,3},{6,0},{7,1},{8,14},{9,15},{10,... | collective-permute-start | bytes 393224 | tf_op jit(solution)/shard_map/ppermute | solution.py:337
  31.5 1.3 %collective-permute-start.11 = (f32[32,8,128]{2,1,0:T(8,128)S(1)}, f32[32,8,128]{2,1,0:T(8,128)S(1)}, u32[]{:S(2)}, u32[]{:S(2)}) collective-permute-start(f32[32,8,128]{2,1,0:T(8,128)S(1)} %get-tuple-element.54), channel_id=1, source_target_pairs={{0,4},{1,5},{2,6},{3,7},{4,0},{5,1},{6,2},{7,3},{8,12},{9,13},{10,... | collective-permute-start | bytes 393224 | tf_op jit(solution)/shard_map/ppermute | solution.py:337
  32.8 0.6 %collective-permute-start.12 = (f32[32,8,128]{2,1,0:T(8,128)S(1)}, f32[32,8,128]{2,1,0:T(8,128)S(1)}, u32[]{:S(2)}, u32[]{:S(2)}) collective-permute-start(f32[32,8,128]{2,1,0:T(8,128)S(1)} %get-tuple-element.55), channel_id=1, source_target_pairs={{0,2},{1,3},{2,0},{3,1},{4,6},{5,7},{6,4},{7,5},{8,10},{9,11},{10,... | collective-permute-start | bytes 393224 | tf_op jit(solution)/shard_map/ppermute | solution.py:337
  33.5 0.3 collective-permute-start.13
  33.7 2.3 %collective-permute-start.14 = (f32[32,8,128]{2,1,0:T(8,128)S(1)}, f32[32,8,128]{2,1,0:T(8,128)S(1)}, u32[]{:S(2)}, u32[]{:S(2)}) collective-permute-start(f32[32,8,128]{2,1,0:T(8,128)S(1)} %get-tuple-element.57), channel_id=1, source_target_pairs={{0,5},{1,4},{2,7},{3,6},{4,1},{5,0},{6,3},{7,2},{8,13},{9,12},{10,... | collective-permute-start | bytes 393224 | tf_op jit(solution)/shard_map/ppermute | solution.py:337
  36.0 0.9 %collective-permute-done.10.refs_0_ = f32[32,8,128]{2,1,0:T(8,128)S(1)} collective-permute-done((f32[32,8,128]{2,1,0:T(8,128)S(1)}, f32[32,8,128]{2,1,0:T(8,128)S(1)}, u32[]{:S(2)}, u32[]{:S(2)}) %collective-permute-start.10) | collective-permute-done | bytes 131104 | tf_op jit(solution)/shard_map/ppermute | solution.py:337
  37.0 0.0 collective-permute-start.15
  37.0 1.9 %collective-permute-done.11.refs_1_ = f32[32,8,128]{2,1,0:T(8,128)S(1)} collective-permute-done((f32[32,8,128]{2,1,0:T(8,128)S(1)}, f32[32,8,128]{2,1,0:T(8,128)S(1)}, u32[]{:S(2)}, u32[]{:S(2)}) %collective-permute-start.11) | collective-permute-done | bytes 131104 | tf_op jit(solution)/shard_map/ppermute | solution.py:337
  38.8 0.0 collective-permute-start.16
  38.8 0.4 collective-permute-done.12.refs_2_
  39.3 1.7 %collective-permute-done.13.refs_3_ = f32[32,8,128]{2,1,0:T(8,128)S(1)} collective-permute-done((f32[32,8,128]{2,1,0:T(8,128)S(1)}, f32[32,8,128]{2,1,0:T(8,128)S(1)}, u32[]{:S(2)}, u32[]{:S(2)}) %collective-permute-start.13) | collective-permute-done | bytes 131104 | tf_op jit(solution)/shard_map/ppermute | solution.py:337
  41.0 2.0 %collective-permute-done.14.refs_4_ = f32[32,8,128]{2,1,0:T(8,128)S(1)} collective-permute-done((f32[32,8,128]{2,1,0:T(8,128)S(1)}, f32[32,8,128]{2,1,0:T(8,128)S(1)}, u32[]{:S(2)}, u32[]{:S(2)}) %collective-permute-start.14) | collective-permute-done | bytes 131104 | tf_op jit(solution)/shard_map/ppermute | solution.py:337
  42.9 1.0 %collective-permute-done.15.refs_5_ = f32[32,8,128]{2,1,0:T(8,128)S(1)} collective-permute-done((f32[32,8,128]{2,1,0:T(8,128)S(1)}, f32[32,8,128]{2,1,0:T(8,128)S(1)}, u32[]{:S(2)}, u32[]{:S(2)}) %collective-permute-start.15) | collective-permute-done | bytes 131104 | tf_op jit(solution)/shard_map/ppermute | solution.py:337
  43.9 0.0 collective-permute-done.16.refs_6_
  44.0 1.0 %join.1 = f32[64,1,8,512]{3,2,1,0:T(8,128)} custom-call(f32[32,8,128]{2,1,0:T(8,128)S(1)} %collective-permute-done.10.refs_0_, f32[32,8,128]{2,1,0:T(8,128)S(1)} %collective-permute-done.11.refs_1_, f32[32,8,128]{2,1,0:T(8,128)S(1)} %collective-permute-done.12.refs_2_, f32[32,8,128]{2,1,0:T(8,128)S(1)} %collective-permute-done.13.refs_3_, ...), custom_call_target="tpu_custom_call" | custom-call | tf_op jit(solution)/shard_map/join/pallas_call | solution.py:448
  (2 shorter events, 0.0 us)
Async XLA Ops:
  1.5 9.4 %collective-permute-start = (f32[37,8,128]{2,1,0:T(8,128)S(1)}, f32[37,8,128]{2,1,0:T(8,128)S(1)}, u32[]{:S(2)}, u32[]{:S(2)}) collective-permute-start(f32[37,8,128]{2,1,0:T(8,128)S(1)} %get-tuple-element.36), channel_id=1, source_target_pairs={{0,6},{1,7},{2,4},{3,5},{4,2},{5,3},{6,0},{7,1},{8,14},{9,15},{10,... | collective-permute-start | bytes 454664 | tf_op jit(solution)/shard_map/ppermute | solution.py:337
  5.7 7.9 %collective-permute-start.1 = (f32[37,8,128]{2,1,0:T(8,128)S(1)}, f32[37,8,128]{2,1,0:T(8,128)S(1)}, u32[]{:S(2)}, u32[]{:S(2)}) collective-permute-start(f32[37,8,128]{2,1,0:T(8,128)S(1)} %get-tuple-element.37), channel_id=1, source_target_pairs={{0,4},{1,5},{2,6},{3,7},{4,0},{5,1},{6,2},{7,3},{8,12},{9,13},{10,... | collective-permute-start | bytes 454664 | tf_op jit(solution)/shard_map/ppermute | solution.py:337
  6.0 7.6 %collective-permute-start.2 = (f32[37,8,128]{2,1,0:T(8,128)S(1)}, f32[37,8,128]{2,1,0:T(8,128)S(1)}, u32[]{:S(2)}, u32[]{:S(2)}) collective-permute-start(f32[37,8,128]{2,1,0:T(8,128)S(1)} %get-tuple-element.38), channel_id=1, source_target_pairs={{0,2},{1,3},{2,0},{3,1},{4,6},{5,7},{6,4},{7,5},{8,10},{9,11},{10,... | collective-permute-start | bytes 454664 | tf_op jit(solution)/shard_map/ppermute | solution.py:337
  6.3 7.3 %copy-start = (f32[1,8,512]{2,1,0:T(8,128)S(1)}, f32[1,8,512]{2,1,0:T(8,128)}, u32[]{:S(2)}) copy-start(f32[1,8,512]{2,1,0:T(8,128)} %east.5) | copy-start | bytes 49156
  6.3 7.3 %copy-start.1 = (f32[1,8,512]{2,1,0:T(8,128)S(1)}, f32[1,8,512]{2,1,0:T(8,128)}, u32[]{:S(2)}) copy-start(f32[1,8,512]{2,1,0:T(8,128)} %north.5) | copy-start | bytes 49156
  6.3 7.3 %copy-start.2 = (f32[1,8,512]{2,1,0:T(8,128)S(1)}, f32[1,8,512]{2,1,0:T(8,128)}, u32[]{:S(2)}) copy-start(f32[1,8,512]{2,1,0:T(8,128)} %up.5) | copy-start | bytes 49156
  6.3 7.3 %copy-start.3 = (f32[1,8,512]{2,1,0:T(8,128)S(1)}, f32[1,8,512]{2,1,0:T(8,128)}, u32[]{:S(2)}) copy-start(f32[1,8,512]{2,1,0:T(8,128)} %diff.5) | copy-start | bytes 49156
  8.0 10.6 %collective-permute-start.4 = (f32[33,8,128]{2,1,0:T(8,128)S(1)}, f32[33,8,128]{2,1,0:T(8,128)S(1)}, u32[]{:S(2)}, u32[]{:S(2)}) collective-permute-start(f32[33,8,128]{2,1,0:T(8,128)S(1)} %get-tuple-element.40), channel_id=1, source_target_pairs={{0,7},{1,6},{2,5},{3,4},{4,3},{5,2},{6,1},{7,0},{8,15},{9,14},{10,... | collective-permute-start | bytes 405512 | tf_op jit(solution)/shard_map/ppermute | solution.py:337
  9.4 9.2 %collective-permute-start.5 = (f32[33,8,128]{2,1,0:T(8,128)S(1)}, f32[33,8,128]{2,1,0:T(8,128)S(1)}, u32[]{:S(2)}, u32[]{:S(2)}) collective-permute-start(f32[33,8,128]{2,1,0:T(8,128)S(1)} %get-tuple-element.41), channel_id=1, source_target_pairs={{0,5},{1,4},{2,7},{3,6},{4,1},{5,0},{6,3},{7,2},{8,13},{9,12},{10,... | collective-permute-start | bytes 405512 | tf_op jit(solution)/shard_map/ppermute | solution.py:337
  10.9 7.7 %collective-permute-start.6 = (f32[33,8,128]{2,1,0:T(8,128)S(1)}, f32[33,8,128]{2,1,0:T(8,128)S(1)}, u32[]{:S(2)}, u32[]{:S(2)}) collective-permute-start(f32[33,8,128]{2,1,0:T(8,128)S(1)} %get-tuple-element.42), channel_id=1, source_target_pairs={{0,3},{1,2},{2,1},{3,0},{4,7},{5,6},{6,5},{7,4},{8,11},{9,10},{10,... | collective-permute-start | bytes 405512 | tf_op jit(solution)/shard_map/ppermute | solution.py:337
  13.6 5.0 %collective-permute-start.7 = (f32[33,8,128]{2,1,0:T(8,128)S(1)}, f32[33,8,128]{2,1,0:T(8,128)S(1)}, u32[]{:S(2)}, u32[]{:S(2)}) collective-permute-start(f32[33,8,128]{2,1,0:T(8,128)S(1)} %get-tuple-element.43), channel_id=1, source_target_pairs={{0,1},{1,0},{2,3},{3,2},{4,5},{5,4},{6,7},{7,6},{8,9},{9,8},{10,11... | collective-permute-start | bytes 405512 | tf_op jit(solution)/shard_map/ppermute | solution.py:337
  13.7 1.5 %collective-permute-start.3 = (f32[18,8,128]{2,1,0:T(8,128)S(1)}, f32[18,8,128]{2,1,0:T(8,128)S(1)}, u32[]{:S(2)}, u32[]{:S(2)}) collective-permute-start(f32[18,8,128]{2,1,0:T(8,128)S(1)} %get-tuple-element.39), channel_id=1, source_target_pairs={{0,1},{1,0},{2,3},{3,2},{4,5},{5,4},{6,7},{7,6},{8,9},{9,8},{10,11... | collective-permute-start | bytes 221192 | tf_op jit(solution)/shard_map/ppermute | solution.py:337
  15.2 2.7 %copy-start.4 = (s32[8,512]{1,0:T(8,128)S(1)}, s32[8,512]{1,0:T(8,128)}, u32[]{:S(2)}) copy-start(s32[8,512]{1,0:T(8,128)} %kmt.3) | copy-start | bytes 49156
  15.2 2.7 %copy-start.5 = (f32[8,16]{1,0:T(8,128)S(1)}, f32[8,16]{1,0:T(8,128)}, u32[]{:S(2)}) copy-start(f32[8,16]{1,0:T(8,128)} %rates.1) | copy-start | bytes 1540
  15.2 2.7 %copy-start.6 = (f32[16]{0:T(128)S(1)}, f32[16]{0:T(128)}, u32[]{:S(2)}) copy-start(f32[16]{0:T(128)} %thickness.1) | copy-start | bytes 196
  15.2 2.7 %copy-start.7 = (s32[64]{0:T(128)S(1)}, s32[64]{0:T(128)}, u32[]{:S(2)}) copy-start(s32[64]{0:T(128)} %group.1) | copy-start | bytes 772
  15.2 5.0 %collective-permute-start.8 = (f32[2,8,128]{2,1,0:T(8,128)S(1)}, f32[2,8,128]{2,1,0:T(8,128)S(1)}, u32[]{:S(2)}, u32[]{:S(2)}) collective-permute-start(f32[2,8,128]{2,1,0:T(8,128)S(1)} %pick.1.own), channel_id=1, source_target_pairs={{0,8},{1,9},{2,10},{3,11},{4,12},{5,13},{6,14},{7,15},{8,0},{9,1},... | collective-permute-start | bytes 24584 | tf_op jit(solution)/shard_map/ppermute | solution.py:337
  20.2 9.4 %collective-permute-start.9 = (f32[33,8,128]{2,1,0:T(8,128)S(1)}, f32[33,8,128]{2,1,0:T(8,128)S(1)}, u32[]{:S(2)}, u32[]{:S(2)}) collective-permute-start(f32[33,8,128]{2,1,0:T(8,128)S(1)} %get-tuple-element.52.sent), channel_id=1, source_target_pairs={{0,8},{1,9},{2,10},{3,11},{4,12},{5,13},{6,14},{7,15},{8,0},{9,1},... | collective-permute-start | bytes 405512 | tf_op jit(solution)/shard_map/ppermute | solution.py:337
  29.9 7.1 %collective-permute-start.10 = (f32[32,8,128]{2,1,0:T(8,128)S(1)}, f32[32,8,128]{2,1,0:T(8,128)S(1)}, u32[]{:S(2)}, u32[]{:S(2)}) collective-permute-start(f32[32,8,128]{2,1,0:T(8,128)S(1)} %get-tuple-element.53), channel_id=1, source_target_pairs={{0,6},{1,7},{2,4},{3,5},{4,2},{5,3},{6,0},{7,1},{8,14},{9,15},{10,... | collective-permute-start | bytes 393224 | tf_op jit(solution)/shard_map/ppermute | solution.py:337
  31.5 7.4 %collective-permute-start.11 = (f32[32,8,128]{2,1,0:T(8,128)S(1)}, f32[32,8,128]{2,1,0:T(8,128)S(1)}, u32[]{:S(2)}, u32[]{:S(2)}) collective-permute-start(f32[32,8,128]{2,1,0:T(8,128)S(1)} %get-tuple-element.54), channel_id=1, source_target_pairs={{0,4},{1,5},{2,6},{3,7},{4,0},{5,1},{6,2},{7,3},{8,12},{9,13},{10,... | collective-permute-start | bytes 393224 | tf_op jit(solution)/shard_map/ppermute | solution.py:337
  32.8 6.4 %collective-permute-start.12 = (f32[32,8,128]{2,1,0:T(8,128)S(1)}, f32[32,8,128]{2,1,0:T(8,128)S(1)}, u32[]{:S(2)}, u32[]{:S(2)}) collective-permute-start(f32[32,8,128]{2,1,0:T(8,128)S(1)} %get-tuple-element.55), channel_id=1, source_target_pairs={{0,2},{1,3},{2,0},{3,1},{4,6},{5,7},{6,4},{7,5},{8,10},{9,11},{10,... | collective-permute-start | bytes 393224 | tf_op jit(solution)/shard_map/ppermute | solution.py:337
  33.5 7.5 %collective-permute-start.13 = (f32[32,8,128]{2,1,0:T(8,128)S(1)}, f32[32,8,128]{2,1,0:T(8,128)S(1)}, u32[]{:S(2)}, u32[]{:S(2)}) collective-permute-start(f32[32,8,128]{2,1,0:T(8,128)S(1)} %get-tuple-element.56), channel_id=1, source_target_pairs={{0,7},{1,6},{2,5},{3,4},{4,3},{5,2},{6,1},{7,0},{8,15},{9,14},{10,... | collective-permute-start | bytes 393224 | tf_op jit(solution)/shard_map/ppermute | solution.py:337
  33.7 9.2 %collective-permute-start.14 = (f32[32,8,128]{2,1,0:T(8,128)S(1)}, f32[32,8,128]{2,1,0:T(8,128)S(1)}, u32[]{:S(2)}, u32[]{:S(2)}) collective-permute-start(f32[32,8,128]{2,1,0:T(8,128)S(1)} %get-tuple-element.57), channel_id=1, source_target_pairs={{0,5},{1,4},{2,7},{3,6},{4,1},{5,0},{6,3},{7,2},{8,13},{9,12},{10,... | collective-permute-start | bytes 393224 | tf_op jit(solution)/shard_map/ppermute | solution.py:337
  37.0 7.0 %collective-permute-start.15 = (f32[32,8,128]{2,1,0:T(8,128)S(1)}, f32[32,8,128]{2,1,0:T(8,128)S(1)}, u32[]{:S(2)}, u32[]{:S(2)}) collective-permute-start(f32[32,8,128]{2,1,0:T(8,128)S(1)} %get-tuple-element.58), channel_id=1, source_target_pairs={{0,3},{1,2},{2,1},{3,0},{4,7},{5,6},{6,5},{7,4},{8,11},{9,10},{10,... | collective-permute-start | bytes 393224 | tf_op jit(solution)/shard_map/ppermute | solution.py:337
  38.8 5.1 %collective-permute-start.16 = (f32[32,8,128]{2,1,0:T(8,128)S(1)}, f32[32,8,128]{2,1,0:T(8,128)S(1)}, u32[]{:S(2)}, u32[]{:S(2)}) collective-permute-start(f32[32,8,128]{2,1,0:T(8,128)S(1)} %get-tuple-element.59), channel_id=1, source_target_pairs={{0,1},{1,0},{2,3},{3,2},{4,5},{5,4},{6,7},{7,6},{8,9},{9,8},{10,11... | collective-permute-start | bytes 393224 | tf_op jit(solution)/shard_map/ppermute | solution.py:337

commit v7 on v6

v7 whole, which is shorter than its diff:
```python
import functools

import jax
import jax.numpy as jnp
from jax import lax
from jax.experimental import pallas as pl
from jax.experimental.pallas import tpu as pltpu
from jax.sharding import PartitionSpec as P

LANES = 128
ROWS = 8
MID, TOUT, TIN, OUTER, ALPHA = range(5)
EDGE, EAST, NORTH, UP, DIFF, EXTRA = 0, 1, 2, 3, 4, 5
f32 = jnp.float32
VMEM_LIMIT = 16 * 1024 * 1024


def lanes_iota():
    return lax.broadcasted_iota(jnp.int32, (ROWS, LANES), 1)


def rows_iota():
    return lax.broadcasted_iota(jnp.int32, (ROWS, LANES), 0)


def crossed(half, d):
    return (d & half // 2 > 0) + (d & half // 4 > 0)


def devices(half):
    return sorted(range(1, half), key=lambda d: (d < 2, d & 1, -crossed(half, d), -d)) + [0]


def homeward(half):
    return sorted(range(1, half), key=lambda d: (d < 2, d & 1, crossed(half, d) * (2 * (d & 1) - 1), -d)) + [0]


def early(half):
    return [d for d in devices(half) if d < 2 or d % 2 == 0]


def n_extra(d):
    return 1 if d % 2 else EXTRA


def place(nb, tc):
    half = nb * tc
    index = lax.axis_index("lev")
    rank = lax.rem(index, half)
    return lax.div(index, half), rank, lax.div(rank, tc), lax.rem(rank, tc)


def pack_kernel(nb, tc, tpc, odd, tracer, east, north, up, diff, kmt, *refs):
    half = nb * tc
    _, rank, _, chunk = place(nb, tc)
    distances = [d for d in devices(half) if d % 2 == odd]
    turns = range(odd, tc, 2)
    scalars, refs = refs[: 3 * odd], refs[3 * odd :]
    out, ready = dict(zip(distances, refs)), refs[len(distances) : -7]
    cells, fields, depth, extra, table, sem, store_sem = refs[-7:]
    loads = [pltpu.make_async_copy(kmt, depth, sem.at[0])]
    for i, field in enumerate((east,) if odd else (east, north, up, diff)):
        loads.append(pltpu.make_async_copy(field, fields.at[pl.ds(i, 1)], sem.at[1 + i]))
    chunks = [
        pltpu.make_async_copy(
            tracer.at[pl.ds((chunk ^ e) * tpc, tpc), 0], cells.at[pl.ds(e // 2 * tpc, tpc)], sem.at[5 + e // 2]
        )
        for e in turns
    ]
    for copy in chunks + loads:
        copy.start()
    stores = []
    for d in distances:
        cut = pl.ds(pl.multiple_of(lax.div(rank ^ d, tc) * LANES, LANES), LANES)
        copy = pltpu.make_async_copy(
            tracer.at[pl.ds((chunk ^ d % tc) * tpc, tpc), 0, :, cut], out[d].at[pl.ds(0, tpc)], store_sem.at[d // 2]
        )
        copy.start()
        stores.append(copy)
    for copy in loads:
        copy.wait()
    if odd:
        prepare(nb, tc, tpc, *scalars, depth, *ready, table)
    for copy in chunks:
        copy.wait()
    lane = lanes_iota()
    cols = [slice(b * LANES, (b + 1) * LANES) for b in range(nb)]
    wet = [(lax.axis_index("lev") < depth[:, cols[b]]).astype(f32) for b in range(nb)]
    flow = [None]
    for b in range(1, nb):
        ends = fields[0, :, cols[b - 1]][:, LANES - 1 :]
        ends = ends * wet[b - 1][:, LANES - 1 :] * wet[b][:, :1]
        flow.append(jnp.broadcast_to(ends, (ROWS, LANES)))
    for e in turns:
        faces = [jnp.zeros((ROWS, LANES), f32) for _ in range(nb)]
        for t in range(tpc):
            at = e // 2 * tpc + t
            for b in range(1, nb):
                west = pltpu.roll(cells[at, :, cols[b - 1]], (2 * t + 1) % LANES, 1)
                here = cells[at, :, cols[b]]
                here = pltpu.roll(here, 2 * t, 1) if t else here
                face = jnp.maximum(flow[b], 0.0) * west + jnp.minimum(flow[b], 0.0) * here
                faces[b] = jnp.where(lane == 2 * t, face, faces[b])
        for b in range(nb):
            edge = faces[b]
            if b + 1 < nb:
                edge = edge - pltpu.roll(faces[b + 1], LANES - 1, 1)
            extra[e // 2, b] = edge
    for d in distances:
        block = lax.div(rank ^ d, tc)
        cut = pl.ds(pl.multiple_of(block * LANES, LANES), LANES)
        out[d][tpc + EDGE] = extra[d % tc // 2, block]
        if not odd:
            for i in range(4):
                out[d][tpc + EAST + i] = fields[i, :, cut]
    for copy in stores:
        copy.wait()


def relay_kernel(nb, tc, tpc, east, north, up, diff, *refs):
    half = nb * tc
    arrived, (out, seam) = refs[:-2], refs[-2:]
    _, rank, block, _ = place(nb, tc)
    cols = pl.ds(pl.multiple_of(block * LANES, LANES), LANES)
    for j, even in enumerate(arrived):
        for i in range(4):
            out[4 * j + i] = even[tpc + EAST + i]
    own = [level[0, :, cols] for level in (east, north, up, diff)]
    for i in range(4):
        out[4 * len(arrived) + i] = own[i]
    for i in range(2):
        field = own[UP - EAST + i]
        for d, even in zip(devices(half), arrived):
            field = jnp.where(rank == d, even[tpc + UP + i], field)
        out[4 * len(arrived) + 4 + i] = field
        seam[i] = field


def pick_kernel(nb, tc, seam, swapped, own):
    _, rank, _, _ = place(nb, tc)
    for i in range(2):
        own[i] = jnp.where(lax.rem(rank, 2) == 1, swapped[swapped.shape[0] - 2 + i], seam[i])


def prepare(nb, tc, tpc, thickness, group, rates, kmt_all, wet, depth, decay, table):
    half = nb * tc
    upper, _, block, chunk = place(nb, tc)
    kmt = kmt_all[:, pl.ds(pl.multiple_of(block * LANES, LANES), LANES)]
    levels = [jnp.where(upper == 1, 2 * half - 1 - o, o) for o in range(half + 1)]
    for o, k in enumerate(levels):
        wet[o] = (k < kmt).astype(f32)
        depth[o] = jnp.full((ROWS, LANES), thickness[k], f32)
    row = rows_iota()
    for g in range(rates.shape[0]):
        for at in range(0, half, ROWS):
            tile = jnp.zeros((ROWS, LANES), f32)
            for i in range(min(ROWS, half - at)):
                tile = jnp.where(row == i, rates[g, levels[at + i]], tile)
            table[g, at : at + ROWS] = tile[: min(ROWS, half - at)]
    for t in range(tpc):
        decay[t] = table[group[chunk * tpc + t]]


def horizontal(half, tpc, d, piece, fields, rank, upper, wets, decay, cells, sums):
    lane, row = lanes_iota(), rows_iota()
    ends = jnp.logical_or(lane == 0, lane == LANES - 1)
    slot = rank ^ d
    o = jnp.where(upper == 1, half - 1 - slot, slot)
    wet = wets[o]
    east = fields[0] * wet * pltpu.roll(wet, LANES - 1, 1)
    east = jnp.where(lane == LANES - 1, 0.0, east)
    north = fields[1] * wet * pltpu.roll(wet, ROWS - 1, 0)
    north = jnp.where(row == ROWS - 1, 0.0, north)
    e_pos, e_neg = jnp.maximum(east, 0.0), jnp.minimum(east, 0.0)
    n_pos, n_neg = jnp.maximum(north, 0.0), jnp.minimum(north, 0.0)
    mid = wet - e_pos - n_pos + pltpu.roll(e_neg, 1, 1) + pltpu.roll(n_neg, 1, 0)
    e_pos, n_pos = pltpu.roll(e_pos, 1, 1), pltpu.roll(n_pos, 1, 0)
    edges = piece[tpc + EDGE]
    for t in range(tpc):
        c = piece[t]
        star = c * (mid - decay[t, pl.ds(o, 1)] * wet)
        star += e_pos * pltpu.roll(c, 1, 1) - e_neg * pltpu.roll(c, LANES - 1, 1)
        star += n_pos * pltpu.roll(c, 1, 0) - n_neg * pltpu.roll(c, ROWS - 1, 0)
        edge = pltpu.roll(edges, LANES - 2 * t, 1) if t else edges
        cells[slot, t] = c
        sums[slot, t] = star + jnp.where(ends, edge, 0.0)


def field_of(half, tpc, d, pieces, swapped):
    evens = [e for e in devices(half) if e % 2 == 0]
    if d % 2 == 0:
        return [pieces[d][tpc + EAST + i] for i in range(4)]
    return [swapped[4 * evens.index(d ^ 1) + i] for i in range(4)]


def first_kernel(nb, tc, tpc, wets, depths, decay, swapped, *refs):
    half = nb * tc
    pieces = dict(zip(early(half), refs))
    cells, sums, coef, cin_out, base, vertical = refs[len(pieces) :]
    upper, rank, _, _ = place(nb, tc)
    sign = 1.0 - 2.0 * upper.astype(f32)
    for d in range(half):
        fields = field_of(half, tpc, d, pieces, swapped)
        vertical[rank ^ d, 0], vertical[rank ^ d, 1] = fields[2], fields[3]
        if d in pieces:
            horizontal(half, tpc, d, pieces[d], fields, rank, upper, wets, decay, cells, sums)

    def slot_of(o):
        return jnp.where(upper == 1, half - 1 - o, o)

    zero = jnp.zeros((ROWS, LANES), f32)
    cin = tout = outer = mid = zero
    for o in range(half):
        dz, dz_next = depths[o], depths[o + 1]
        open_face = wets[o] * wets[o + 1]
        denom = 1.0 - outer - outer * cin
        coef[o, TOUT], coef[o, OUTER] = tout, outer
        if o + 1 == half:
            coef[o, MID] = mid
            base[0], base[1], base[3], base[4] = denom, open_face, dz, dz_next
            base[2] = jnp.full((ROWS, LANES), sign, f32)
        else:
            face = jnp.where(upper == 1, slot_of(o), slot_of(o + 1))
            pos, neg, g = interface(vertical[face, 0], vertical[face, 1], sign, open_face, dz, dz_next)
            inner = -g / dz
            alpha = 1.0 / (denom - inner)
            cin = inner * alpha
            coef[o, MID], coef[o, TIN], coef[o, ALPHA] = mid + neg / dz, pos / dz, alpha
            cin_out[o] = cin
            tout, outer, mid = -neg / dz_next, -g / dz_next, -pos / dz_next


def solve_kernel(nb, tc, tpc, wets, decay, swapped, coef, *refs):
    half = nb * tc
    late = [d for d in devices(half) if d not in early(half)]
    pieces = dict(zip(late, refs))
    cells, sums, f_out = refs[-3:]
    upper, rank, _, _ = place(nb, tc)
    for d in late:
        fields = field_of(half, tpc, d, pieces, swapped)
        horizontal(half, tpc, d, pieces[d], fields, rank, upper, wets, decay, cells, sums)
    for o in range(half):
        slot, before, after = [jnp.where(upper == 1, half - 1 - k, k) for k in (o, o - 1, o + 1)]
        for t in range(tpc):
            star = sums[slot, t] + coef[o, MID] * cells[slot, t]
            if o:
                star += coef[o, TOUT] * cells[before, t] - coef[o, OUTER] * f_out[o - 1, t]
            if o + 1 < half:
                star = coef[o, ALPHA] * (star + coef[o, TIN] * cells[after, t])
            f_out[o, t] = star


def interface(w, g, sign, open_face, dz, dz_next):
    w = sign * w * open_face
    dz_min = jnp.minimum(dz, dz_next)
    g = g * open_face / (0.5 * (dz + dz_next))
    return dz_min * jnp.maximum(w, 0.0), dz_min * jnp.minimum(w, 0.0), g


def seam_kernel(nb, tc, count, star, cells, base, own, other, f_out, coef_out, message):
    half = nb * tc
    upper, _, _, _ = place(nb, tc)
    slot = jnp.where(upper == 1, 0, half - 1)
    sign, dz, dz_next = base[2], base[3], base[4]
    w = jnp.where(sign < 0.0, own[0], other[0])
    g = jnp.where(sign < 0.0, own[1], other[1])
    pos, neg, g = interface(w, g, sign, base[1], dz, dz_next)
    inner, outer_next = -g / dz, -g / dz_next
    mid, tout_next = neg / dz, -neg / dz_next
    alpha = 1.0 / (base[0] - inner)
    for t in range(count):
        c = cells[slot, t]
        f = alpha * (star[half - 1, t] + mid * c)
        f_out[t] = f
        message[t] = tout_next * c - outer_next * f
    coef_out[0] = inner * alpha
    coef_out[1] = alpha
    coef_out[2] = outer_next
    message[count] = alpha


def back_kernel(nb, tc, tpc, f_in, cin, f_last, coef, sent, got, *refs):
    half = nb * tc
    out, solved = refs[:-1], refs[-1]
    upper, rank, _, _ = place(nb, tc)
    slots = [jnp.where(upper == 1, half - 1 - o, o) for o in range(half)]
    other = coef[0] * got[tpc]
    scale = 1.0 / (1.0 - other * coef[2])
    mine, theirs = scale * coef[1], scale * other
    for t in range(tpc):
        x = f_last[t] + (mine * got[t] - theirs * sent[t])
        solved[slots[half - 1], t] = x
        for o in range(half - 2, -1, -1):
            x = f_in[o, t] - cin[o] * x
            solved[slots[o], t] = x
    for d, piece in zip(homeward(half), out):
        for t in range(tpc):
            piece[t] = solved[rank ^ d, t]


def join_kernel(nb, tc, tpc, *refs):
    half = nb * tc
    arrived, out, sem = refs[:half], refs[half], refs[half + 1]
    _, rank, _, _ = place(nb, tc)
    copies = []
    for d, piece in zip(homeward(half), arrived):
        r = rank ^ d
        cols = pl.ds(pl.multiple_of(lax.div(r, tc) * LANES, LANES), LANES)
        copies.append(
            pltpu.make_async_copy(
                piece, out.at[pl.ds(lax.rem(r, tc) * tpc, tpc), 0, :, cols], sem.at[d]
            )
        )
    for copy in copies:
        copy.start()
    for copy in copies:
        copy.wait()


def shards(tracer, east_flow, north_flow, up_flow, diffusivity, thickness, kmt, group, group_rate):
    ntr, ldev, ny, nx = tracer.shape
    count = lax.axis_size("lev")
    half = count // 2
    nb = nx // LANES
    tc = half // nb
    tpc = ntr // tc
    assert tc % 2 == 0 and 2 * tpc <= LANES
    assert ldev == 1 and ny == ROWS and nb * LANES == nx and tc * nb == half and tpc * tc == ntr
    tile = (ROWS, LANES)
    vm = pl.BlockSpec(memory_space=pltpu.VMEM)
    sm = pl.BlockSpec(memory_space=pltpu.SMEM)
    hbm = pl.BlockSpec(memory_space=pltpu.HBM)
    anywhere = pl.BlockSpec(memory_space=pl.ANY)
    params = pltpu.CompilerParams(vmem_limit_bytes=VMEM_LIMIT)

    def flip(value, bits):
        return lax.ppermute(value, "lev", [(i, i ^ bits) for i in range(count)])

    def struct(*shape):
        return jax.ShapeDtypeStruct(shape + tile, f32)

    def exchange(values, order):
        return [flip(piece, d) if d else piece for d, piece in zip(order, values)]

    packed = {}
    held = [
        pltpu.with_memory_space_constraint(value, pltpu.HBM)
        for value in (tracer, east_flow, north_flow, up_flow, diffusivity, kmt)
    ]
    ready = (
        pltpu.VMEM((half + 1,) + tile, f32),
        pltpu.VMEM((half + 1,) + tile, f32),
        pltpu.VMEM((tpc, half, LANES), f32),
    )
    for odd in range(2):
        distances = [d for d in devices(half) if d % 2 == odd]
        made = pl.pallas_call(
            functools.partial(pack_kernel, nb, tc, tpc, odd),
            out_shape=tuple(pltpu.VMEM((tpc + n_extra(d),) + tile, f32) for d in distances) + ready * odd,
            in_specs=[hbm] * 6 + [sm] * (3 * odd),
            out_specs=(vm,) * (len(distances) + 3 * odd),
            scratch_shapes=[
                pltpu.VMEM((ntr // 2, ny, nx), f32),
                pltpu.VMEM((4, ny, nx), f32),
                pltpu.VMEM((ny, nx), jnp.int32),
                pltpu.VMEM((tc // 2, nb) + tile, f32),
                pltpu.VMEM((group_rate.shape[0], half, LANES), f32),
                pltpu.SemaphoreType.DMA((5 + tc // 2,)),
                pltpu.SemaphoreType.DMA((half // 2,)),
            ],
            compiler_params=params,
            name="pack",
        )(*held, *(thickness, group, group_rate)[: 3 * odd])
        packed.update(zip(distances, made))
    wet, depth, decay = made[-3:]
    pieces = [packed[d] for d in devices(half)]
    arrived = exchange(pieces, devices(half))
    evens = half // 2 - 1
    relayed, seam = pl.pallas_call(
        functools.partial(relay_kernel, nb, tc, tpc),
        out_shape=(struct(4 * (evens + 1) + 2), struct(2)),
        in_specs=[vm] * (4 + evens),
        out_specs=(vm, vm),
        compiler_params=params,
        name="relay",
    )(east_flow, north_flow, up_flow, diffusivity, *arrived[:evens])
    swapped = flip(relayed, 1)
    own = pl.pallas_call(
        functools.partial(pick_kernel, nb, tc),
        out_shape=struct(2),
        in_specs=[vm, vm],
        out_specs=vm,
        compiler_params=params,
        name="pick",
    )(seam, swapped)
    other = flip(own, half)
    order = devices(half)
    cells, sums, coef, cin, base = pl.pallas_call(
        functools.partial(first_kernel, nb, tc, tpc),
        out_shape=(struct(half, tpc), struct(half, tpc), struct(half, 5), struct(half - 1), struct(5)),
        in_specs=[vm] * (4 + len(early(half))),
        out_specs=(vm,) * 5,
        scratch_shapes=[pltpu.VMEM((half, 2) + tile, f32)],
        compiler_params=params,
        name="first",
    )(wet, depth, decay, swapped, *[arrived[order.index(d)] for d in early(half)])
    late = [arrived[order.index(d)] for d in order if d not in early(half)]
    cells, _, f = pl.pallas_call(
        functools.partial(solve_kernel, nb, tc, tpc),
        out_shape=(struct(half, tpc), struct(half, tpc), struct(half, tpc)),
        in_specs=[vm] * (6 + len(late)),
        out_specs=(vm,) * 3,
        input_output_aliases={4 + len(late): 0, 5 + len(late): 1},
        compiler_params=params,
        name="solve",
    )(wet, decay, swapped, coef, *late, cells, sums)
    f_last, coef, message = pl.pallas_call(
        functools.partial(seam_kernel, nb, tc, tpc),
        out_shape=(struct(tpc), struct(3), struct(tpc + 1)),
        in_specs=[vm] * 5,
        out_specs=(vm,) * 3,
        compiler_params=params,
        name="seam",
    )(f, cells, base, own, other)
    solved = pl.pallas_call(
        functools.partial(back_kernel, nb, tc, tpc),
        out_shape=(struct(tpc),) * half,
        in_specs=[vm] * 6,
        out_specs=(vm,) * half,
        scratch_shapes=[pltpu.VMEM((half, tpc) + tile, f32)],
        compiler_params=params,
        name="back",
    )(f, cin, f_last, coef, message, flip(message, half))
    back = exchange(solved, homeward(half))
    return pl.pallas_call(
        functools.partial(join_kernel, nb, tc, tpc),
        out_shape=jax.ShapeDtypeStruct(tracer.shape, f32),
        in_specs=[anywhere] * len(back),
        out_specs=hbm,
        scratch_shapes=[pltpu.SemaphoreType.DMA((half,))],
        compiler_params=params,
        name="join",
    )(*back)


def solution(mesh):
    placed = (
        P(None, "lev", "band", None),
        P("lev", "band", None),
        P("lev", "band", None),
        P("lev", "band", None),
        P("lev", "band", None),
        P(),
        P("band", None),
        P(),
        P(),
    )
    return jax.shard_map(
        shards, mesh=mesh, in_specs=placed, out_specs=P(None, "lev", "band", None), check_vma=False
    )
```

time: 45.1 us -> 44.4 us (0.984)
  starting transfers between devices: 20.1 us -> 19.1 us
    ppermute x17, starting transfers between devices: 20.1 us -> 19.1 us  [flip(): return lax.ppermute(value, 'lev', [(i, i ^ bits) for i in range(count)])]
    pallas_call x2, Pallas kernels: 3.15 us -> 3.75 us  [shards(): pl.pallas_call(functools.partial(pack_kernel, nb, tc, tpc, odd), out_shap...]
    pallas_call x5, Pallas kernels: 3.54 us -> 3.07 us  [the longest x1 1.02 us: shards(): pl.pallas_call(functools.partial(join_kernel, nb, tc, tpc), out_shape=jax...]
where the time goes in v7:
time: 44.4 us; the launch traced here: 44.3 us
  starting transfers between devices  19.1 us (43%)
  waiting for transfers between devices  18.1 us (41%)
  Pallas kernels  6.84 us (15%)
    ppermute x17, starting transfers between devices, flip(): return lax.ppermute(value, 'lev', [(i, i ^ bits) for i in range(count)])  19.1 us
    ppermute x17, waiting for transfers between devices, flip(): return lax.ppermute(value, 'lev', [(i, i ^ bits) for i in range(count)])  18.1 us
    pallas_call x2, Pallas kernels, shards(): pl.pallas_call(functools.partial(pack_kernel, nb, tc, tpc, odd), out_shap...  3.75 us
    pallas_call x1, Pallas kernels, shards(): pl.pallas_call(functools.partial(join_kernel, nb, tc, tpc), out_shape=jax...  1.02 us
    pallas_call x1, Pallas kernels, shards(): pl.pallas_call(functools.partial(first_kernel, nb, tc, tpc), out_shape=(s...  0.91 us
  transfers between devices with their start and end apart: 17, of which 9 were waited for; matrix products, arithmetic and copies ran while one was open for 0% of the time, Pallas kernels for 9%

profile of v7, /device:TPU:0, one launch (start us, length us, event | category | flops | bytes accessed | tf_op | source)
XLA Modules:
  0.0 44.3 jit_solution(15955388553806495457)
XLA Ops:
  0.0 1.5 %pack.3 = (f32[37,8,128]{2,1,0:T(8,128)S(1)}, f32[37,8,128]{2,1,0:T(8,128)S(1)}, f32[37,8,128]{2,1,0:T(8,128)S(1)}, f32[37,8,128]{2,1,0:T(8,128)S(1)}) custom-call(f32[64,1,8,512]{3,2,1,0:T(8,128)} %tracer.3, f32[1,8,512]{2,1,0:T(8,128)} %east.5, f32[1,8,512]{2,1,0:T(8,128)} %north.5, f32[1,8,512]{2,1,0:T(8,128)} %up.5, f32[1,8,512]{2,1,0:T(8,128)} %diff.5, ...), custom_call_target="tpu_custom_call" | custom-call | tf_op jit(solution)/shard_map/pack/pallas_call | solution.py:357
  1.6 0.0 copy-start.4
  1.6 4.1 %collective-permute-start = (f32[37,8,128]{2,1,0:T(8,128)S(1)}, f32[37,8,128]{2,1,0:T(8,128)S(1)}, u32[]{:S(2)}, u32[]{:S(2)}) collective-permute-start(f32[37,8,128]{2,1,0:T(8,128)S(1)} %get-tuple-element.38), channel_id=1, source_target_pairs={{0,6},{1,7},{2,4},{3,5},{4,2},{5,3},{6,0},{7,1},{8,14},{9,15},{10,... | collective-permute-start | bytes 454664 | tf_op jit(solution)/shard_map/ppermute | solution.py:337
  5.7 0.0 copy-start.5
  5.7 0.0 copy-start.6
  5.7 0.3 collective-permute-start.1
  6.1 0.3 collective-permute-start.2
  6.4 0.0 copy-done.4
  6.4 0.0 copy-done.5
  6.4 0.0 copy-done.6
  6.4 0.0 copy-start
  6.4 0.0 copy-start.1
  6.4 0.0 copy-start.2
  6.4 0.0 copy-start.3
  6.4 2.2 %pack.2 = (f32[33,8,128]{2,1,0:T(8,128)S(1)}, f32[33,8,128]{2,1,0:T(8,128)S(1)}, f32[33,8,128]{2,1,0:T(8,128)S(1)}, f32[33,8,128]{2,1,0:T(8,128)S(1)}, f32[9,8,1...) custom-call(f32[64,1,8,512]{3,2,1,0:T(8,128)} %tracer.3, f32[1,8,512]{2,1,0:T(8,128)} %east.5, ...), custom_call_target="tpu_custom_call" | custom-call | tf_op jit(solution)/shard_map/pack/pallas_call | solution.py:357
  8.6 0.1 collective-permute-start.4
  8.7 3.0 %collective-permute-start.5 = (f32[33,8,128]{2,1,0:T(8,128)S(1)}, f32[33,8,128]{2,1,0:T(8,128)S(1)}, u32[]{:S(2)}, u32[]{:S(2)}) collective-permute-start(f32[33,8,128]{2,1,0:T(8,128)S(1)} %get-tuple-element.46), channel_id=1, source_target_pairs={{0,7},{1,6},{2,5},{3,4},{4,3},{5,2},{6,1},{7,0},{8,15},{9,14},{10,... | collective-permute-start | bytes 405512 | tf_op jit(solution)/shard_map/ppermute | solution.py:337
  11.7 0.0 collective-permute-done.refs_0_
  11.7 0.0 collective-permute-start.6
  11.7 1.2 %collective-permute-done.1.refs_1_ = f32[37,8,128]{2,1,0:T(8,128)S(1)} collective-permute-done((f32[37,8,128]{2,1,0:T(8,128)S(1)}, f32[37,8,128]{2,1,0:T(8,128)S(1)}, u32[]{:S(2)}, u32[]{:S(2)}) %collective-permute-start.1) | collective-permute-done | bytes 151584 | tf_op jit(solution)/shard_map/ppermute | solution.py:337
  12.9 0.8 %collective-permute-start.7 = (f32[33,8,128]{2,1,0:T(8,128)S(1)}, f32[33,8,128]{2,1,0:T(8,128)S(1)}, u32[]{:S(2)}, u32[]{:S(2)}) collective-permute-start(f32[33,8,128]{2,1,0:T(8,128)S(1)} %get-tuple-element.48), channel_id=1, source_target_pairs={{0,3},{1,2},{2,1},{3,0},{4,7},{5,6},{6,5},{7,4},{8,11},{9,10},{10,... | collective-permute-start | bytes 405512 | tf_op jit(solution)/shard_map/ppermute | solution.py:337
  13.7 0.0 collective-permute-done.2.refs_2_
  13.7 0.0 copy-done
  13.7 0.0 copy-done.1
  13.8 0.0 copy-done.2
  13.8 0.0 copy-done.3
  13.8 0.1 collective-permute-start.3
  13.9 1.3 %collective-permute-done.3.swapped = f32[18,8,128]{2,1,0:T(8,128)S(1)} collective-permute-done((f32[18,8,128]{2,1,0:T(8,128)S(1)}, f32[18,8,128]{2,1,0:T(8,128)S(1)}, u32[]{:S(2)}, u32[]{:S(2)}) %collective-permute-start.3) | collective-permute-done | bytes 73760 | tf_op jit(solution)/shard_map/ppermute | solution.py:337
  15.1 2.6 %collective-permute-start.8 = (f32[2,8,128]{2,1,0:T(8,128)S(1)}, f32[2,8,128]{2,1,0:T(8,128)S(1)}, u32[]{:S(2)}, u32[]{:S(2)}) collective-permute-start(f32[2,8,128]{2,1,0:T(8,128)S(1)} %pick.1.own), channel_id=1, source_target_pairs={{0,8},{1,9},{2,10},{3,11},{4,12},{5,13},{6,14},{7,15},{8,0},{9,1},... | collective-permute-start | bytes 24584 | tf_op jit(solution)/shard_map/ppermute | solution.py:337
  17.7 0.0 collective-permute-done.4.refs_3_
  17.7 0.9 %first.1 = (f32[8,32,8,128]{3,2,1,0:T(8,128)S(1)}, f32[8,32,8,128]{3,2,1,0:T(8,128)S(1)}, f32[8,5,8,128]{3,2,1,0:T(8,128)S(1)}, f32[7,8,128]{2,1,0:T(8,128)S(1)}, f32[5,8,128]{2,1,0:T(8,128)S(1)}) custom-call(f32[9,8,128]{2,1,0:T(8,128)S(1)} %get-tuple-element.36.wets, f32[9,8,128]{2,1,0:T(8,128)S(1)} %get-tuple-element.42.depths, ...), custom_call_target="tpu_custom_call" | custom-call | tf_op jit(solution)/shard_map/first/pallas_call | solution.py:398
  18.6 0.0 collective-permute-done.5.refs_0_
  18.7 0.0 collective-permute-done.6.refs_1_
  18.7 0.2 collective-permute-done.7.refs_2_
  18.8 0.9 %solve.1 = (f32[8,32,8,128]{3,2,1,0:T(8,128)S(1)}, f32[8,32,8,128]{3,2,1,0:T(8,128)S(1)}, f32[8,32,8,128]{3,2,1,0:T(8,128)S(1)}) custom-call(f32[9,8,128]{2,1,0:T(8,128)S(1)} %get-tuple-element.36.wets, f32[32,8,128]{2,1,0:T(8,128)S(1)} %get-tuple-element.37.decay, ...), custom_call_target="tpu_custom_call", output_to_operand_aliasing={{0}: (7, {}), {1}: (8, {})} | custom-call | tf_op jit(solution)/shard_map/solve/pallas_call | solution.py:408
  19.7 0.0 collective-permute-done.8.other
  19.8 2.8 %collective-permute-start.9 = (f32[33,8,128]{2,1,0:T(8,128)S(1)}, f32[33,8,128]{2,1,0:T(8,128)S(1)}, u32[]{:S(2)}, u32[]{:S(2)}) collective-permute-start(f32[33,8,128]{2,1,0:T(8,128)S(1)} %get-tuple-element.58.sent), channel_id=1, source_target_pairs={{0,8},{1,9},{2,10},{3,11},{4,12},{5,13},{6,14},{7,15},{8,0},{9,1},... | collective-permute-start | bytes 405512 | tf_op jit(solution)/shard_map/ppermute | solution.py:337
  22.5 6.7 %collective-permute-done.9.got = f32[33,8,128]{2,1,0:T(8,128)S(1)} collective-permute-done((f32[33,8,128]{2,1,0:T(8,128)S(1)}, f32[33,8,128]{2,1,0:T(8,128)S(1)}, u32[]{:S(2)}, u32[]{:S(2)}) %collective-permute-start.9) | collective-permute-done | bytes 135200 | tf_op jit(solution)/shard_map/ppermute | solution.py:337
  29.2 0.2 back.1
  29.4 1.3 %collective-permute-start.10 = (f32[32,8,128]{2,1,0:T(8,128)S(1)}, f32[32,8,128]{2,1,0:T(8,128)S(1)}, u32[]{:S(2)}, u32[]{:S(2)}) collective-permute-start(f32[32,8,128]{2,1,0:T(8,128)S(1)} %get-tuple-element.59), channel_id=1, source_target_pairs={{0,6},{1,7},{2,4},{3,5},{4,2},{5,3},{6,0},{7,1},{8,14},{9,15},{10,... | collective-permute-start | bytes 393224 | tf_op jit(solution)/shard_map/ppermute | solution.py:337
  30.7 1.4 %collective-permute-start.11 = (f32[32,8,128]{2,1,0:T(8,128)S(1)}, f32[32,8,128]{2,1,0:T(8,128)S(1)}, u32[]{:S(2)}, u32[]{:S(2)}) collective-permute-start(f32[32,8,128]{2,1,0:T(8,128)S(1)} %get-tuple-element.60), channel_id=1, source_target_pairs={{0,4},{1,5},{2,6},{3,7},{4,0},{5,1},{6,2},{7,3},{8,12},{9,13},{10,... | collective-permute-start | bytes 393224 | tf_op jit(solution)/shard_map/ppermute | solution.py:337
  32.1 0.9 %collective-permute-start.12 = (f32[32,8,128]{2,1,0:T(8,128)S(1)}, f32[32,8,128]{2,1,0:T(8,128)S(1)}, u32[]{:S(2)}, u32[]{:S(2)}) collective-permute-start(f32[32,8,128]{2,1,0:T(8,128)S(1)} %get-tuple-element.61), channel_id=1, source_target_pairs={{0,2},{1,3},{2,0},{3,1},{4,6},{5,7},{6,4},{7,5},{8,10},{9,11},{10,... | collective-permute-start | bytes 393224 | tf_op jit(solution)/shard_map/ppermute | solution.py:337
  33.0 0.0 collective-permute-start.13
  33.0 1.5 %collective-permute-start.14 = (f32[32,8,128]{2,1,0:T(8,128)S(1)}, f32[32,8,128]{2,1,0:T(8,128)S(1)}, u32[]{:S(2)}, u32[]{:S(2)}) collective-permute-start(f32[32,8,128]{2,1,0:T(8,128)S(1)} %get-tuple-element.63), channel_id=1, source_target_pairs={{0,3},{1,2},{2,1},{3,0},{4,7},{5,6},{6,5},{7,4},{8,11},{9,10},{10,... | collective-permute-start | bytes 393224 | tf_op jit(solution)/shard_map/ppermute | solution.py:337
  34.5 2.0 %collective-permute-done.10.refs_0_ = f32[32,8,128]{2,1,0:T(8,128)S(1)} collective-permute-done((f32[32,8,128]{2,1,0:T(8,128)S(1)}, f32[32,8,128]{2,1,0:T(8,128)S(1)}, u32[]{:S(2)}, u32[]{:S(2)}) %collective-permute-start.10) | collective-permute-done | bytes 131104 | tf_op jit(solution)/shard_map/ppermute | solution.py:337
  36.5 0.0 collective-permute-start.15
  36.5 2.4 %collective-permute-done.11.refs_1_ = f32[32,8,128]{2,1,0:T(8,128)S(1)} collective-permute-done((f32[32,8,128]{2,1,0:T(8,128)S(1)}, f32[32,8,128]{2,1,0:T(8,128)S(1)}, u32[]{:S(2)}, u32[]{:S(2)}) %collective-permute-start.11) | collective-permute-done | bytes 131104 | tf_op jit(solution)/shard_map/ppermute | solution.py:337
  38.9 0.0 collective-permute-start.16
  38.9 0.2 collective-permute-done.12.refs_2_
  39.1 0.9 %collective-permute-done.13.refs_3_ = f32[32,8,128]{2,1,0:T(8,128)S(1)} collective-permute-done((f32[32,8,128]{2,1,0:T(8,128)S(1)}, f32[32,8,128]{2,1,0:T(8,128)S(1)}, u32[]{:S(2)}, u32[]{:S(2)}) %collective-permute-start.13) | collective-permute-done | bytes 131104 | tf_op jit(solution)/shard_map/ppermute | solution.py:337
  40.0 0.0 collective-permute-done.14.refs_4_
  40.0 3.2 %collective-permute-done.15.refs_5_ = f32[32,8,128]{2,1,0:T(8,128)S(1)} collective-permute-done((f32[32,8,128]{2,1,0:T(8,128)S(1)}, f32[32,8,128]{2,1,0:T(8,128)S(1)}, u32[]{:S(2)}, u32[]{:S(2)}) %collective-permute-start.15) | collective-permute-done | bytes 131104 | tf_op jit(solution)/shard_map/ppermute | solution.py:337
  43.3 0.0 collective-permute-done.16.refs_6_
  43.3 1.0 %join.1 = f32[64,1,8,512]{3,2,1,0:T(8,128)} custom-call(f32[32,8,128]{2,1,0:T(8,128)S(1)} %collective-permute-done.10.refs_0_, f32[32,8,128]{2,1,0:T(8,128)S(1)} %collective-permute-done.11.refs_1_, f32[32,8,128]{2,1,0:T(8,128)S(1)} %collective-permute-done.12.refs_2_, f32[32,8,128]{2,1,0:T(8,128)S(1)} %collective-permute-done.13.refs_3_, ...), custom_call_target="tpu_custom_call" | custom-call | tf_op jit(solution)/shard_map/join/pallas_call | solution.py:435
  (3 shorter events, 0.1 us)
Async XLA Ops:
  1.6 4.8 %copy-start.4 = (f32[8,16]{1,0:T(8,128)S(1)}, f32[8,16]{1,0:T(8,128)}, u32[]{:S(2)}) copy-start(f32[8,16]{1,0:T(8,128)} %refs_2_.1) | copy-start | bytes 1540
  1.6 10.1 %collective-permute-start = (f32[37,8,128]{2,1,0:T(8,128)S(1)}, f32[37,8,128]{2,1,0:T(8,128)S(1)}, u32[]{:S(2)}, u32[]{:S(2)}) collective-permute-start(f32[37,8,128]{2,1,0:T(8,128)S(1)} %get-tuple-element.38), channel_id=1, source_target_pairs={{0,6},{1,7},{2,4},{3,5},{4,2},{5,3},{6,0},{7,1},{8,14},{9,15},{10,... | collective-permute-start | bytes 454664 | tf_op jit(solution)/shard_map/ppermute | solution.py:337
  5.7 0.7 %copy-start.5 = (f32[16]{0:T(128)S(1)}, f32[16]{0:T(128)}, u32[]{:S(2)}) copy-start(f32[16]{0:T(128)} %refs_0_.1) | copy-start | bytes 196
  5.7 0.7 %copy-start.6 = (s32[64]{0:T(128)S(1)}, s32[64]{0:T(128)}, u32[]{:S(2)}) copy-start(s32[64]{0:T(128)} %refs_1_.1) | copy-start | bytes 772
  5.7 7.2 %collective-permute-start.1 = (f32[37,8,128]{2,1,0:T(8,128)S(1)}, f32[37,8,128]{2,1,0:T(8,128)S(1)}, u32[]{:S(2)}, u32[]{:S(2)}) collective-permute-start(f32[37,8,128]{2,1,0:T(8,128)S(1)} %get-tuple-element.39), channel_id=1, source_target_pairs={{0,4},{1,5},{2,6},{3,7},{4,0},{5,1},{6,2},{7,3},{8,12},{9,13},{10,... | collective-permute-start | bytes 454664 | tf_op jit(solution)/shard_map/ppermute | solution.py:337
  6.1 7.7 %collective-permute-start.2 = (f32[37,8,128]{2,1,0:T(8,128)S(1)}, f32[37,8,128]{2,1,0:T(8,128)S(1)}, u32[]{:S(2)}, u32[]{:S(2)}) collective-permute-start(f32[37,8,128]{2,1,0:T(8,128)S(1)} %get-tuple-element.40), channel_id=1, source_target_pairs={{0,2},{1,3},{2,0},{3,1},{4,6},{5,7},{6,4},{7,5},{8,10},{9,11},{10,... | collective-permute-start | bytes 454664 | tf_op jit(solution)/shard_map/ppermute | solution.py:337
  6.4 7.4 %copy-start = (f32[1,8,512]{2,1,0:T(8,128)S(1)}, f32[1,8,512]{2,1,0:T(8,128)}, u32[]{:S(2)}) copy-start(f32[1,8,512]{2,1,0:T(8,128)} %east.5) | copy-start | bytes 49156
  6.4 7.4 %copy-start.1 = (f32[1,8,512]{2,1,0:T(8,128)S(1)}, f32[1,8,512]{2,1,0:T(8,128)}, u32[]{:S(2)}) copy-start(f32[1,8,512]{2,1,0:T(8,128)} %north.5) | copy-start | bytes 49156
  6.4 7.3 %copy-start.2 = (f32[1,8,512]{2,1,0:T(8,128)S(1)}, f32[1,8,512]{2,1,0:T(8,128)}, u32[]{:S(2)}) copy-start(f32[1,8,512]{2,1,0:T(8,128)} %up.5) | copy-start | bytes 49156
  6.4 7.3 %copy-start.3 = (f32[1,8,512]{2,1,0:T(8,128)S(1)}, f32[1,8,512]{2,1,0:T(8,128)}, u32[]{:S(2)}) copy-start(f32[1,8,512]{2,1,0:T(8,128)} %diff.5) | copy-start | bytes 49156
  8.6 9.1 %collective-permute-start.4 = (f32[33,8,128]{2,1,0:T(8,128)S(1)}, f32[33,8,128]{2,1,0:T(8,128)S(1)}, u32[]{:S(2)}, u32[]{:S(2)}) collective-permute-start(f32[33,8,128]{2,1,0:T(8,128)S(1)} %get-tuple-element.43), channel_id=1, source_target_pairs={{0,1},{1,0},{2,3},{3,2},{4,5},{5,4},{6,7},{7,6},{8,9},{9,8},{10,11... | collective-permute-start | bytes 405512 | tf_op jit(solution)/shard_map/ppermute | solution.py:337
  8.7 9.9 %collective-permute-start.5 = (f32[33,8,128]{2,1,0:T(8,128)S(1)}, f32[33,8,128]{2,1,0:T(8,128)S(1)}, u32[]{:S(2)}, u32[]{:S(2)}) collective-permute-start(f32[33,8,128]{2,1,0:T(8,128)S(1)} %get-tuple-element.46), channel_id=1, source_target_pairs={{0,7},{1,6},{2,5},{3,4},{4,3},{5,2},{6,1},{7,0},{8,15},{9,14},{10,... | collective-permute-start | bytes 405512 | tf_op jit(solution)/shard_map/ppermute | solution.py:337
  11.7 7.0 %collective-permute-start.6 = (f32[33,8,128]{2,1,0:T(8,128)S(1)}, f32[33,8,128]{2,1,0:T(8,128)S(1)}, u32[]{:S(2)}, u32[]{:S(2)}) collective-permute-start(f32[33,8,128]{2,1,0:T(8,128)S(1)} %get-tuple-element.47), channel_id=1, source_target_pairs={{0,5},{1,4},{2,7},{3,6},{4,1},{5,0},{6,3},{7,2},{8,13},{9,12},{10,... | collective-permute-start | bytes 405512 | tf_op jit(solution)/shard_map/ppermute | solution.py:337
  12.9 5.9 %collective-permute-start.7 = (f32[33,8,128]{2,1,0:T(8,128)S(1)}, f32[33,8,128]{2,1,0:T(8,128)S(1)}, u32[]{:S(2)}, u32[]{:S(2)}) collective-permute-start(f32[33,8,128]{2,1,0:T(8,128)S(1)} %get-tuple-element.48), channel_id=1, source_target_pairs={{0,3},{1,2},{2,1},{3,0},{4,7},{5,6},{6,5},{7,4},{8,11},{9,10},{10,... | collective-permute-start | bytes 405512 | tf_op jit(solution)/shard_map/ppermute | solution.py:337
  13.8 1.3 %collective-permute-start.3 = (f32[18,8,128]{2,1,0:T(8,128)S(1)}, f32[18,8,128]{2,1,0:T(8,128)S(1)}, u32[]{:S(2)}, u32[]{:S(2)}) collective-permute-start(f32[18,8,128]{2,1,0:T(8,128)S(1)} %get-tuple-element.41), channel_id=1, source_target_pairs={{0,1},{1,0},{2,3},{3,2},{4,5},{5,4},{6,7},{7,6},{8,9},{9,8},{10,11... | collective-permute-start | bytes 221192 | tf_op jit(solution)/shard_map/ppermute | solution.py:337
  15.1 4.6 %collective-permute-start.8 = (f32[2,8,128]{2,1,0:T(8,128)S(1)}, f32[2,8,128]{2,1,0:T(8,128)S(1)}, u32[]{:S(2)}, u32[]{:S(2)}) collective-permute-start(f32[2,8,128]{2,1,0:T(8,128)S(1)} %pick.1.own), channel_id=1, source_target_pairs={{0,8},{1,9},{2,10},{3,11},{4,12},{5,13},{6,14},{7,15},{8,0},{9,1},... | collective-permute-start | bytes 24584 | tf_op jit(solution)/shard_map/ppermute | solution.py:337
  19.8 9.4 %collective-permute-start.9 = (f32[33,8,128]{2,1,0:T(8,128)S(1)}, f32[33,8,128]{2,1,0:T(8,128)S(1)}, u32[]{:S(2)}, u32[]{:S(2)}) collective-permute-start(f32[33,8,128]{2,1,0:T(8,128)S(1)} %get-tuple-element.58.sent), channel_id=1, source_target_pairs={{0,8},{1,9},{2,10},{3,11},{4,12},{5,13},{6,14},{7,15},{8,0},{9,1},... | collective-permute-start | bytes 405512 | tf_op jit(solution)/shard_map/ppermute | solution.py:337
  29.4 7.1 %collective-permute-start.10 = (f32[32,8,128]{2,1,0:T(8,128)S(1)}, f32[32,8,128]{2,1,0:T(8,128)S(1)}, u32[]{:S(2)}, u32[]{:S(2)}) collective-permute-start(f32[32,8,128]{2,1,0:T(8,128)S(1)} %get-tuple-element.59), channel_id=1, source_target_pairs={{0,6},{1,7},{2,4},{3,5},{4,2},{5,3},{6,0},{7,1},{8,14},{9,15},{10,... | collective-permute-start | bytes 393224 | tf_op jit(solution)/shard_map/ppermute | solution.py:337
  30.7 8.2 %collective-permute-start.11 = (f32[32,8,128]{2,1,0:T(8,128)S(1)}, f32[32,8,128]{2,1,0:T(8,128)S(1)}, u32[]{:S(2)}, u32[]{:S(2)}) collective-permute-start(f32[32,8,128]{2,1,0:T(8,128)S(1)} %get-tuple-element.60), channel_id=1, source_target_pairs={{0,4},{1,5},{2,6},{3,7},{4,0},{5,1},{6,2},{7,3},{8,12},{9,13},{10,... | collective-permute-start | bytes 393224 | tf_op jit(solution)/shard_map/ppermute | solution.py:337
  32.1 7.0 %collective-permute-start.12 = (f32[32,8,128]{2,1,0:T(8,128)S(1)}, f32[32,8,128]{2,1,0:T(8,128)S(1)}, u32[]{:S(2)}, u32[]{:S(2)}) collective-permute-start(f32[32,8,128]{2,1,0:T(8,128)S(1)} %get-tuple-element.61), channel_id=1, source_target_pairs={{0,2},{1,3},{2,0},{3,1},{4,6},{5,7},{6,4},{7,5},{8,10},{9,11},{10,... | collective-permute-start | bytes 393224 | tf_op jit(solution)/shard_map/ppermute | solution.py:337
  33.0 7.0 %collective-permute-start.13 = (f32[32,8,128]{2,1,0:T(8,128)S(1)}, f32[32,8,128]{2,1,0:T(8,128)S(1)}, u32[]{:S(2)}, u32[]{:S(2)}) collective-permute-start(f32[32,8,128]{2,1,0:T(8,128)S(1)} %get-tuple-element.62), channel_id=1, source_target_pairs={{0,5},{1,4},{2,7},{3,6},{4,1},{5,0},{6,3},{7,2},{8,13},{9,12},{10,... | collective-permute-start | bytes 393224 | tf_op jit(solution)/shard_map/ppermute | solution.py:337
  33.0 7.0 %collective-permute-start.14 = (f32[32,8,128]{2,1,0:T(8,128)S(1)}, f32[32,8,128]{2,1,0:T(8,128)S(1)}, u32[]{:S(2)}, u32[]{:S(2)}) collective-permute-start(f32[32,8,128]{2,1,0:T(8,128)S(1)} %get-tuple-element.63), channel_id=1, source_target_pairs={{0,3},{1,2},{2,1},{3,0},{4,7},{5,6},{6,5},{7,4},{8,11},{9,10},{10,... | collective-permute-start | bytes 393224 | tf_op jit(solution)/shard_map/ppermute | solution.py:337
  36.5 6.8 %collective-permute-start.15 = (f32[32,8,128]{2,1,0:T(8,128)S(1)}, f32[32,8,128]{2,1,0:T(8,128)S(1)}, u32[]{:S(2)}, u32[]{:S(2)}) collective-permute-start(f32[32,8,128]{2,1,0:T(8,128)S(1)} %get-tuple-element.64), channel_id=1, source_target_pairs={{0,7},{1,6},{2,5},{3,4},{4,3},{5,2},{6,1},{7,0},{8,15},{9,14},{10,... | collective-permute-start | bytes 393224 | tf_op jit(solution)/shard_map/ppermute | solution.py:337
  38.9 4.3 %collective-permute-start.16 = (f32[32,8,128]{2,1,0:T(8,128)S(1)}, f32[32,8,128]{2,1,0:T(8,128)S(1)}, u32[]{:S(2)}, u32[]{:S(2)}) collective-permute-start(f32[32,8,128]{2,1,0:T(8,128)S(1)} %get-tuple-element.65), channel_id=1, source_target_pairs={{0,1},{1,0},{2,3},{3,2},{4,5},{5,4},{6,7},{7,6},{8,9},{9,8},{10,11... | collective-permute-start | bytes 393224 | tf_op jit(solution)/shard_map/ppermute | solution.py:337

commit v8 on v7

--- a/solution.py
+++ b/solution.py
@@ -32,11 +32,11 @@
 
 
 def homeward(half):
-    return sorted(range(1, half), key=lambda d: (d < 2, d & 1, crossed(half, d) * (2 * (d & 1) - 1), -d)) + [0]
+    return sorted(range(1, half), key=lambda d: (d < 2, d & 1, -crossed(half, d), d)) + [0]
 
 
 def early(half):
-    return [d for d in devices(half) if d < 2 or d % 2 == 0]
+    return [d for d in devices(half) if d < 2 or d % 2 == 0 or crossed(half, d) == 2]
 
 
 def n_extra(d):

time: 44.4 us -> 43.9 us (0.989)
  waiting for transfers between devices: 18.1 us -> 17 us
    ppermute x17, waiting for transfers between devices: 18.1 us -> 17 us  [flip(): return lax.ppermute(value, 'lev', [(i, i ^ bits) for i in range(count)])]
  transfers between devices with their start and end apart: 17 -> 17, of which waited for: 9 -> 7; matrix products, arithmetic and copies ran while one was open for 0% -> 0% of each run, Pallas kernels for 9% -> 9%
where the time goes in v8:
time: 43.9 us; the launch traced here: 43.5 us
  starting transfers between devices  19.4 us (44%)
  waiting for transfers between devices  17 us (39%)
  Pallas kernels  6.87 us (16%)
    ppermute x17, starting transfers between devices, flip(): return lax.ppermute(value, 'lev', [(i, i ^ bits) for i in range(count)])  19.4 us
    ppermute x17, waiting for transfers between devices, flip(): return lax.ppermute(value, 'lev', [(i, i ^ bits) for i in range(count)])  17 us
    pallas_call x2, Pallas kernels, shards(): pl.pallas_call(functools.partial(pack_kernel, nb, tc, tpc, odd), out_shap...  3.75 us
    pallas_call x1, Pallas kernels, shards(): pl.pallas_call(functools.partial(first_kernel, nb, tc, tpc), out_shape=(s...  1.08 us
    pallas_call x1, Pallas kernels, shards(): pl.pallas_call(functools.partial(join_kernel, nb, tc, tpc), out_shape=jax...  1.03 us
  transfers between devices with their start and end apart: 17, of which 7 were waited for; matrix products, arithmetic and copies ran while one was open for 0% of the time, Pallas kernels for 9%

profile of v8, /device:TPU:0, one launch (start us, length us, event | category | flops | bytes accessed | tf_op | source)
XLA Modules:
  0.0 43.5 jit_solution(4976407266147982411)
XLA Ops:
  0.0 1.5 %pack.3 = (f32[37,8,128]{2,1,0:T(8,128)S(1)}, f32[37,8,128]{2,1,0:T(8,128)S(1)}, f32[37,8,128]{2,1,0:T(8,128)S(1)}, f32[37,8,128]{2,1,0:T(8,128)S(1)}) custom-call(f32[64,1,8,512]{3,2,1,0:T(8,128)} %tracer.3, f32[1,8,512]{2,1,0:T(8,128)} %east.5, f32[1,8,512]{2,1,0:T(8,128)} %north.5, f32[1,8,512]{2,1,0:T(8,128)} %up.5, f32[1,8,512]{2,1,0:T(8,128)} %diff.5, ...), custom_call_target="tpu_custom_call" | custom-call | tf_op jit(solution)/shard_map/pack/pallas_call | solution.py:357
  1.6 0.0 copy-start.4
  1.6 4.1 %collective-permute-start = (f32[37,8,128]{2,1,0:T(8,128)S(1)}, f32[37,8,128]{2,1,0:T(8,128)S(1)}, u32[]{:S(2)}, u32[]{:S(2)}) collective-permute-start(f32[37,8,128]{2,1,0:T(8,128)S(1)} %get-tuple-element.38), channel_id=1, source_target_pairs={{0,6},{1,7},{2,4},{3,5},{4,2},{5,3},{6,0},{7,1},{8,14},{9,15},{10,... | collective-permute-start | bytes 454664 | tf_op jit(solution)/shard_map/ppermute | solution.py:337
  5.7 0.0 copy-start.5
  5.7 0.0 copy-start.6
  5.7 0.3 collective-permute-start.1
  6.1 0.3 collective-permute-start.2
  6.4 0.0 copy-done.4
  6.4 0.0 copy-done.5
  6.4 0.0 copy-done.6
  6.4 0.0 copy-start
  6.4 0.0 copy-start.1
  6.4 0.0 copy-start.2
  6.4 0.0 copy-start.3
  6.4 2.2 %pack.2 = (f32[33,8,128]{2,1,0:T(8,128)S(1)}, f32[33,8,128]{2,1,0:T(8,128)S(1)}, f32[33,8,128]{2,1,0:T(8,128)S(1)}, f32[33,8,128]{2,1,0:T(8,128)S(1)}, f32[9,8,1...) custom-call(f32[64,1,8,512]{3,2,1,0:T(8,128)} %tracer.3, f32[1,8,512]{2,1,0:T(8,128)} %east.5, ...), custom_call_target="tpu_custom_call" | custom-call | tf_op jit(solution)/shard_map/pack/pallas_call | solution.py:357
  8.6 1.4 %collective-permute-start.4 = (f32[33,8,128]{2,1,0:T(8,128)S(1)}, f32[33,8,128]{2,1,0:T(8,128)S(1)}, u32[]{:S(2)}, u32[]{:S(2)}) collective-permute-start(f32[33,8,128]{2,1,0:T(8,128)S(1)} %get-tuple-element.43), channel_id=1, source_target_pairs={{0,7},{1,6},{2,5},{3,4},{4,3},{5,2},{6,1},{7,0},{8,15},{9,14},{10,... | collective-permute-start | bytes 405512 | tf_op jit(solution)/shard_map/ppermute | solution.py:337
  10.0 1.6 %collective-permute-start.5 = (f32[33,8,128]{2,1,0:T(8,128)S(1)}, f32[33,8,128]{2,1,0:T(8,128)S(1)}, u32[]{:S(2)}, u32[]{:S(2)}) collective-permute-start(f32[33,8,128]{2,1,0:T(8,128)S(1)} %get-tuple-element.44), channel_id=1, source_target_pairs={{0,1},{1,0},{2,3},{3,2},{4,5},{5,4},{6,7},{7,6},{8,9},{9,8},{10,11... | collective-permute-start | bytes 405512 | tf_op jit(solution)/shard_map/ppermute | solution.py:337
  11.7 0.0 collective-permute-done.refs_0_
  11.7 0.0 collective-permute-start.6
  11.7 1.3 %collective-permute-done.1.refs_1_ = f32[37,8,128]{2,1,0:T(8,128)S(1)} collective-permute-done((f32[37,8,128]{2,1,0:T(8,128)S(1)}, f32[37,8,128]{2,1,0:T(8,128)S(1)}, u32[]{:S(2)}, u32[]{:S(2)}) %collective-permute-start.1) | collective-permute-done | bytes 151584 | tf_op jit(solution)/shard_map/ppermute | solution.py:337
  13.0 0.8 %collective-permute-start.7 = (f32[33,8,128]{2,1,0:T(8,128)S(1)}, f32[33,8,128]{2,1,0:T(8,128)S(1)}, u32[]{:S(2)}, u32[]{:S(2)}) collective-permute-start(f32[33,8,128]{2,1,0:T(8,128)S(1)} %get-tuple-element.48), channel_id=1, source_target_pairs={{0,3},{1,2},{2,1},{3,0},{4,7},{5,6},{6,5},{7,4},{8,11},{9,10},{10,... | collective-permute-start | bytes 405512 | tf_op jit(solution)/shard_map/ppermute | solution.py:337
  13.7 0.0 collective-permute-done.2.refs_2_
  13.7 0.0 copy-done
  13.7 0.0 copy-done.1
  13.8 0.0 copy-done.2
  13.8 0.0 copy-done.3
  13.8 0.1 collective-permute-start.3
  13.9 1.3 %collective-permute-done.3.swapped = f32[18,8,128]{2,1,0:T(8,128)S(1)} collective-permute-done((f32[18,8,128]{2,1,0:T(8,128)S(1)}, f32[18,8,128]{2,1,0:T(8,128)S(1)}, u32[]{:S(2)}, u32[]{:S(2)}) %collective-permute-start.3) | collective-permute-done | bytes 73760 | tf_op jit(solution)/shard_map/ppermute | solution.py:337
  15.1 2.6 %collective-permute-start.8 = (f32[2,8,128]{2,1,0:T(8,128)S(1)}, f32[2,8,128]{2,1,0:T(8,128)S(1)}, u32[]{:S(2)}, u32[]{:S(2)}) collective-permute-start(f32[2,8,128]{2,1,0:T(8,128)S(1)} %pick.1.own), channel_id=1, source_target_pairs={{0,8},{1,9},{2,10},{3,11},{4,12},{5,13},{6,14},{7,15},{8,0},{9,1},... | collective-permute-start | bytes 24584 | tf_op jit(solution)/shard_map/ppermute | solution.py:337
  17.7 0.0 collective-permute-done.4.refs_3_
  17.7 0.0 collective-permute-done.5.refs_4_
  17.7 1.1 %first.1 = (f32[8,32,8,128]{3,2,1,0:T(8,128)S(1)}, f32[8,32,8,128]{3,2,1,0:T(8,128)S(1)}, f32[8,5,8,128]{3,2,1,0:T(8,128)S(1)}, f32[7,8,128]{2,1,0:T(8,128)S(1)}, f32[5,8,128]{2,1,0:T(8,128)S(1)}) custom-call(f32[9,8,128]{2,1,0:T(8,128)S(1)} %get-tuple-element.36.wets, f32[9,8,128]{2,1,0:T(8,128)S(1)} %get-tuple-element.42.depths, ...), custom_call_target="tpu_custom_call" | custom-call | tf_op jit(solution)/shard_map/first/pallas_call | solution.py:398
  18.8 0.0 collective-permute-done.6.refs_0_
  18.8 0.0 collective-permute-done.7.refs_1_
  18.8 0.7 %solve.1 = (f32[8,32,8,128]{3,2,1,0:T(8,128)S(1)}, f32[8,32,8,128]{3,2,1,0:T(8,128)S(1)}, f32[8,32,8,128]{3,2,1,0:T(8,128)S(1)}) custom-call(f32[9,8,128]{2,1,0:T(8,128)S(1)} %get-tuple-element.36.wets, f32[32,8,128]{2,1,0:T(8,128)S(1)} %get-tuple-element.37.decay, ...), custom_call_target="tpu_custom_call", output_to_operand_aliasing={{0}: (6, {}), {1}: (7, {})} | custom-call | tf_op jit(solution)/shard_map/solve/pallas_call | solution.py:408
  19.6 0.1 collective-permute-done.8.other
  19.7 2.7 %collective-permute-start.9 = (f32[33,8,128]{2,1,0:T(8,128)S(1)}, f32[33,8,128]{2,1,0:T(8,128)S(1)}, u32[]{:S(2)}, u32[]{:S(2)}) collective-permute-start(f32[33,8,128]{2,1,0:T(8,128)S(1)} %get-tuple-element.58.sent), channel_id=1, source_target_pairs={{0,8},{1,9},{2,10},{3,11},{4,12},{5,13},{6,14},{7,15},{8,0},{9,1},... | collective-permute-start | bytes 405512 | tf_op jit(solution)/shard_map/ppermute | solution.py:337
  22.4 6.6 %collective-permute-done.9.got = f32[33,8,128]{2,1,0:T(8,128)S(1)} collective-permute-done((f32[33,8,128]{2,1,0:T(8,128)S(1)}, f32[33,8,128]{2,1,0:T(8,128)S(1)}, u32[]{:S(2)}, u32[]{:S(2)}) %collective-permute-start.9) | collective-permute-done | bytes 135200 | tf_op jit(solution)/shard_map/ppermute | solution.py:337
  29.0 0.2 back.1
  29.2 1.5 %collective-permute-start.10 = (f32[32,8,128]{2,1,0:T(8,128)S(1)}, f32[32,8,128]{2,1,0:T(8,128)S(1)}, u32[]{:S(2)}, u32[]{:S(2)}) collective-permute-start(f32[32,8,128]{2,1,0:T(8,128)S(1)} %get-tuple-element.59), channel_id=1, source_target_pairs={{0,6},{1,7},{2,4},{3,5},{4,2},{5,3},{6,0},{7,1},{8,14},{9,15},{10,... | collective-permute-start | bytes 393224 | tf_op jit(solution)/shard_map/ppermute | solution.py:337
  30.8 0.7 %collective-permute-start.11 = (f32[32,8,128]{2,1,0:T(8,128)S(1)}, f32[32,8,128]{2,1,0:T(8,128)S(1)}, u32[]{:S(2)}, u32[]{:S(2)}) collective-permute-start(f32[32,8,128]{2,1,0:T(8,128)S(1)} %get-tuple-element.60), channel_id=1, source_target_pairs={{0,2},{1,3},{2,0},{3,1},{4,6},{5,7},{6,4},{7,5},{8,10},{9,11},{10,... | collective-permute-start | bytes 393224 | tf_op jit(solution)/shard_map/ppermute | solution.py:337
  31.4 1.3 %collective-permute-start.12 = (f32[32,8,128]{2,1,0:T(8,128)S(1)}, f32[32,8,128]{2,1,0:T(8,128)S(1)}, u32[]{:S(2)}, u32[]{:S(2)}) collective-permute-start(f32[32,8,128]{2,1,0:T(8,128)S(1)} %get-tuple-element.61), channel_id=1, source_target_pairs={{0,4},{1,5},{2,6},{3,7},{4,0},{5,1},{6,2},{7,3},{8,12},{9,13},{10,... | collective-permute-start | bytes 393224 | tf_op jit(solution)/shard_map/ppermute | solution.py:337
  32.8 0.3 collective-permute-start.13
  33.1 1.6 %collective-permute-start.14 = (f32[32,8,128]{2,1,0:T(8,128)S(1)}, f32[32,8,128]{2,1,0:T(8,128)S(1)}, u32[]{:S(2)}, u32[]{:S(2)}) collective-permute-start(f32[32,8,128]{2,1,0:T(8,128)S(1)} %get-tuple-element.63), channel_id=1, source_target_pairs={{0,3},{1,2},{2,1},{3,0},{4,7},{5,6},{6,5},{7,4},{8,11},{9,10},{10,... | collective-permute-start | bytes 393224 | tf_op jit(solution)/shard_map/ppermute | solution.py:337
  34.7 1.4 %collective-permute-done.10.refs_0_ = f32[32,8,128]{2,1,0:T(8,128)S(1)} collective-permute-done((f32[32,8,128]{2,1,0:T(8,128)S(1)}, f32[32,8,128]{2,1,0:T(8,128)S(1)}, u32[]{:S(2)}, u32[]{:S(2)}) %collective-permute-start.10) | collective-permute-done | bytes 131104 | tf_op jit(solution)/shard_map/ppermute | solution.py:337
  36.1 0.0 collective-permute-start.15
  36.1 4.4 %collective-permute-done.11.refs_1_ = f32[32,8,128]{2,1,0:T(8,128)S(1)} collective-permute-done((f32[32,8,128]{2,1,0:T(8,128)S(1)}, f32[32,8,128]{2,1,0:T(8,128)S(1)}, u32[]{:S(2)}, u32[]{:S(2)}) %collective-permute-start.11) | collective-permute-done | bytes 131104 | tf_op jit(solution)/shard_map/ppermute | solution.py:337
  40.4 0.0 collective-permute-start.16
  40.4 0.0 collective-permute-done.12.refs_2_
  40.4 0.0 collective-permute-done.13.refs_3_
  40.4 2.0 %collective-permute-done.14.refs_4_ = f32[32,8,128]{2,1,0:T(8,128)S(1)} collective-permute-done((f32[32,8,128]{2,1,0:T(8,128)S(1)}, f32[32,8,128]{2,1,0:T(8,128)S(1)}, u32[]{:S(2)}, u32[]{:S(2)}) %collective-permute-start.14) | collective-permute-done | bytes 131104 | tf_op jit(solution)/shard_map/ppermute | solution.py:337
  42.4 0.0 collective-permute-done.15.refs_5_
  42.4 0.0 collective-permute-done.16.refs_6_
  42.4 1.0 %join.1 = f32[64,1,8,512]{3,2,1,0:T(8,128)} custom-call(f32[32,8,128]{2,1,0:T(8,128)S(1)} %collective-permute-done.10.refs_0_, f32[32,8,128]{2,1,0:T(8,128)S(1)} %collective-permute-done.11.refs_1_, f32[32,8,128]{2,1,0:T(8,128)S(1)} %collective-permute-done.12.refs_2_, f32[32,8,128]{2,1,0:T(8,128)S(1)} %collective-permute-done.13.refs_3_, ...), custom_call_target="tpu_custom_call" | custom-call | tf_op jit(solution)/shard_map/join/pallas_call | solution.py:435
  (3 shorter events, 0.1 us)
Async XLA Ops:
  1.6 4.8 %copy-start.4 = (f32[8,16]{1,0:T(8,128)S(1)}, f32[8,16]{1,0:T(8,128)}, u32[]{:S(2)}) copy-start(f32[8,16]{1,0:T(8,128)} %refs_2_.1) | copy-start | bytes 1540
  1.6 10.1 %collective-permute-start = (f32[37,8,128]{2,1,0:T(8,128)S(1)}, f32[37,8,128]{2,1,0:T(8,128)S(1)}, u32[]{:S(2)}, u32[]{:S(2)}) collective-permute-start(f32[37,8,128]{2,1,0:T(8,128)S(1)} %get-tuple-element.38), channel_id=1, source_target_pairs={{0,6},{1,7},{2,4},{3,5},{4,2},{5,3},{6,0},{7,1},{8,14},{9,15},{10,... | collective-permute-start | bytes 454664 | tf_op jit(solution)/shard_map/ppermute | solution.py:337
  5.7 0.7 %copy-start.5 = (f32[16]{0:T(128)S(1)}, f32[16]{0:T(128)}, u32[]{:S(2)}) copy-start(f32[16]{0:T(128)} %refs_0_.1) | copy-start | bytes 196
  5.7 0.7 %copy-start.6 = (s32[64]{0:T(128)S(1)}, s32[64]{0:T(128)}, u32[]{:S(2)}) copy-start(s32[64]{0:T(128)} %refs_1_.1) | copy-start | bytes 772
  5.7 7.3 %collective-permute-start.1 = (f32[37,8,128]{2,1,0:T(8,128)S(1)}, f32[37,8,128]{2,1,0:T(8,128)S(1)}, u32[]{:S(2)}, u32[]{:S(2)}) collective-permute-start(f32[37,8,128]{2,1,0:T(8,128)S(1)} %get-tuple-element.39), channel_id=1, source_target_pairs={{0,4},{1,5},{2,6},{3,7},{4,0},{5,1},{6,2},{7,3},{8,12},{9,13},{10,... | collective-permute-start | bytes 454664 | tf_op jit(solution)/shard_map/ppermute | solution.py:337
  6.1 7.7 %collective-permute-start.2 = (f32[37,8,128]{2,1,0:T(8,128)S(1)}, f32[37,8,128]{2,1,0:T(8,128)S(1)}, u32[]{:S(2)}, u32[]{:S(2)}) collective-permute-start(f32[37,8,128]{2,1,0:T(8,128)S(1)} %get-tuple-element.40), channel_id=1, source_target_pairs={{0,2},{1,3},{2,0},{3,1},{4,6},{5,7},{6,4},{7,5},{8,10},{9,11},{10,... | collective-permute-start | bytes 454664 | tf_op jit(solution)/shard_map/ppermute | solution.py:337
  6.4 7.4 %copy-start = (f32[1,8,512]{2,1,0:T(8,128)S(1)}, f32[1,8,512]{2,1,0:T(8,128)}, u32[]{:S(2)}) copy-start(f32[1,8,512]{2,1,0:T(8,128)} %east.5) | copy-start | bytes 49156
  6.4 7.4 %copy-start.1 = (f32[1,8,512]{2,1,0:T(8,128)S(1)}, f32[1,8,512]{2,1,0:T(8,128)}, u32[]{:S(2)}) copy-start(f32[1,8,512]{2,1,0:T(8,128)} %north.5) | copy-start | bytes 49156
  6.4 7.3 %copy-start.2 = (f32[1,8,512]{2,1,0:T(8,128)S(1)}, f32[1,8,512]{2,1,0:T(8,128)}, u32[]{:S(2)}) copy-start(f32[1,8,512]{2,1,0:T(8,128)} %up.5) | copy-start | bytes 49156
  6.4 7.3 %copy-start.3 = (f32[1,8,512]{2,1,0:T(8,128)S(1)}, f32[1,8,512]{2,1,0:T(8,128)}, u32[]{:S(2)}) copy-start(f32[1,8,512]{2,1,0:T(8,128)} %diff.5) | copy-start | bytes 49156
  8.6 9.1 %collective-permute-start.4 = (f32[33,8,128]{2,1,0:T(8,128)S(1)}, f32[33,8,128]{2,1,0:T(8,128)S(1)}, u32[]{:S(2)}, u32[]{:S(2)}) collective-permute-start(f32[33,8,128]{2,1,0:T(8,128)S(1)} %get-tuple-element.43), channel_id=1, source_target_pairs={{0,7},{1,6},{2,5},{3,4},{4,3},{5,2},{6,1},{7,0},{8,15},{9,14},{10,... | collective-permute-start | bytes 405512 | tf_op jit(solution)/shard_map/ppermute | solution.py:337
  10.0 7.7 %collective-permute-start.5 = (f32[33,8,128]{2,1,0:T(8,128)S(1)}, f32[33,8,128]{2,1,0:T(8,128)S(1)}, u32[]{:S(2)}, u32[]{:S(2)}) collective-permute-start(f32[33,8,128]{2,1,0:T(8,128)S(1)} %get-tuple-element.44), channel_id=1, source_target_pairs={{0,1},{1,0},{2,3},{3,2},{4,5},{5,4},{6,7},{7,6},{8,9},{9,8},{10,11... | collective-permute-start | bytes 405512 | tf_op jit(solution)/shard_map/ppermute | solution.py:337
  11.7 7.1 %collective-permute-start.6 = (f32[33,8,128]{2,1,0:T(8,128)S(1)}, f32[33,8,128]{2,1,0:T(8,128)S(1)}, u32[]{:S(2)}, u32[]{:S(2)}) collective-permute-start(f32[33,8,128]{2,1,0:T(8,128)S(1)} %get-tuple-element.47), channel_id=1, source_target_pairs={{0,5},{1,4},{2,7},{3,6},{4,1},{5,0},{6,3},{7,2},{8,13},{9,12},{10,... | collective-permute-start | bytes 405512 | tf_op jit(solution)/shard_map/ppermute | solution.py:337
  13.0 5.9 %collective-permute-start.7 = (f32[33,8,128]{2,1,0:T(8,128)S(1)}, f32[33,8,128]{2,1,0:T(8,128)S(1)}, u32[]{:S(2)}, u32[]{:S(2)}) collective-permute-start(f32[33,8,128]{2,1,0:T(8,128)S(1)} %get-tuple-element.48), channel_id=1, source_target_pairs={{0,3},{1,2},{2,1},{3,0},{4,7},{5,6},{6,5},{7,4},{8,11},{9,10},{10,... | collective-permute-start | bytes 405512 | tf_op jit(solution)/shard_map/ppermute | solution.py:337
  13.8 1.3 %collective-permute-start.3 = (f32[18,8,128]{2,1,0:T(8,128)S(1)}, f32[18,8,128]{2,1,0:T(8,128)S(1)}, u32[]{:S(2)}, u32[]{:S(2)}) collective-permute-start(f32[18,8,128]{2,1,0:T(8,128)S(1)} %get-tuple-element.41), channel_id=1, source_target_pairs={{0,1},{1,0},{2,3},{3,2},{4,5},{5,4},{6,7},{7,6},{8,9},{9,8},{10,11... | collective-permute-start | bytes 221192 | tf_op jit(solution)/shard_map/ppermute | solution.py:337
  15.1 4.5 %collective-permute-start.8 = (f32[2,8,128]{2,1,0:T(8,128)S(1)}, f32[2,8,128]{2,1,0:T(8,128)S(1)}, u32[]{:S(2)}, u32[]{:S(2)}) collective-permute-start(f32[2,8,128]{2,1,0:T(8,128)S(1)} %pick.1.own), channel_id=1, source_target_pairs={{0,8},{1,9},{2,10},{3,11},{4,12},{5,13},{6,14},{7,15},{8,0},{9,1},... | collective-permute-start | bytes 24584 | tf_op jit(solution)/shard_map/ppermute | solution.py:337
  19.7 9.3 %collective-permute-start.9 = (f32[33,8,128]{2,1,0:T(8,128)S(1)}, f32[33,8,128]{2,1,0:T(8,128)S(1)}, u32[]{:S(2)}, u32[]{:S(2)}) collective-permute-start(f32[33,8,128]{2,1,0:T(8,128)S(1)} %get-tuple-element.58.sent), channel_id=1, source_target_pairs={{0,8},{1,9},{2,10},{3,11},{4,12},{5,13},{6,14},{7,15},{8,0},{9,1},... | collective-permute-start | bytes 405512 | tf_op jit(solution)/shard_map/ppermute | solution.py:337
  29.2 6.8 %collective-permute-start.10 = (f32[32,8,128]{2,1,0:T(8,128)S(1)}, f32[32,8,128]{2,1,0:T(8,128)S(1)}, u32[]{:S(2)}, u32[]{:S(2)}) collective-permute-start(f32[32,8,128]{2,1,0:T(8,128)S(1)} %get-tuple-element.59), channel_id=1, source_target_pairs={{0,6},{1,7},{2,4},{3,5},{4,2},{5,3},{6,0},{7,1},{8,14},{9,15},{10,... | collective-permute-start | bytes 393224 | tf_op jit(solution)/shard_map/ppermute | solution.py:337
  30.8 9.7 %collective-permute-start.11 = (f32[32,8,128]{2,1,0:T(8,128)S(1)}, f32[32,8,128]{2,1,0:T(8,128)S(1)}, u32[]{:S(2)}, u32[]{:S(2)}) collective-permute-start(f32[32,8,128]{2,1,0:T(8,128)S(1)} %get-tuple-element.60), channel_id=1, source_target_pairs={{0,2},{1,3},{2,0},{3,1},{4,6},{5,7},{6,4},{7,5},{8,10},{9,11},{10,... | collective-permute-start | bytes 393224 | tf_op jit(solution)/shard_map/ppermute | solution.py:337
  31.4 9.0 %collective-permute-start.12 = (f32[32,8,128]{2,1,0:T(8,128)S(1)}, f32[32,8,128]{2,1,0:T(8,128)S(1)}, u32[]{:S(2)}, u32[]{:S(2)}) collective-permute-start(f32[32,8,128]{2,1,0:T(8,128)S(1)} %get-tuple-element.61), channel_id=1, source_target_pairs={{0,4},{1,5},{2,6},{3,7},{4,0},{5,1},{6,2},{7,3},{8,12},{9,13},{10,... | collective-permute-start | bytes 393224 | tf_op jit(solution)/shard_map/ppermute | solution.py:337
  32.8 7.7 %collective-permute-start.13 = (f32[32,8,128]{2,1,0:T(8,128)S(1)}, f32[32,8,128]{2,1,0:T(8,128)S(1)}, u32[]{:S(2)}, u32[]{:S(2)}) collective-permute-start(f32[32,8,128]{2,1,0:T(8,128)S(1)} %get-tuple-element.62), channel_id=1, source_target_pairs={{0,7},{1,6},{2,5},{3,4},{4,3},{5,2},{6,1},{7,0},{8,15},{9,14},{10,... | collective-permute-start | bytes 393224 | tf_op jit(solution)/shard_map/ppermute | solution.py:337
  33.1 9.4 %collective-permute-start.14 = (f32[32,8,128]{2,1,0:T(8,128)S(1)}, f32[32,8,128]{2,1,0:T(8,128)S(1)}, u32[]{:S(2)}, u32[]{:S(2)}) collective-permute-start(f32[32,8,128]{2,1,0:T(8,128)S(1)} %get-tuple-element.63), channel_id=1, source_target_pairs={{0,3},{1,2},{2,1},{3,0},{4,7},{5,6},{6,5},{7,4},{8,11},{9,10},{10,... | collective-permute-start | bytes 393224 | tf_op jit(solution)/shard_map/ppermute | solution.py:337
  36.1 6.4 %collective-permute-start.15 = (f32[32,8,128]{2,1,0:T(8,128)S(1)}, f32[32,8,128]{2,1,0:T(8,128)S(1)}, u32[]{:S(2)}, u32[]{:S(2)}) collective-permute-start(f32[32,8,128]{2,1,0:T(8,128)S(1)} %get-tuple-element.64), channel_id=1, source_target_pairs={{0,5},{1,4},{2,7},{3,6},{4,1},{5,0},{6,3},{7,2},{8,13},{9,12},{10,... | collective-permute-start | bytes 393224 | tf_op jit(solution)/shard_map/ppermute | solution.py:337
  40.4 2.0 %collective-permute-start.16 = (f32[32,8,128]{2,1,0:T(8,128)S(1)}, f32[32,8,128]{2,1,0:T(8,128)S(1)}, u32[]{:S(2)}, u32[]{:S(2)}) collective-permute-start(f32[32,8,128]{2,1,0:T(8,128)S(1)} %get-tuple-element.65), channel_id=1, source_target_pairs={{0,1},{1,0},{2,3},{3,2},{4,5},{5,4},{6,7},{7,6},{8,9},{9,8},{10,11... | collective-permute-start | bytes 393224 | tf_op jit(solution)/shard_map/ppermute | solution.py:337
